TPU v7x, 256 devices: a whole 4x4x8 slice. The times are simulated.
256 devices in a mesh: adapter: 32 (over z, x), feature: 8 (over y, core).
Axes of the slice: x: 4, y: 4, z: 8, core: 2. Of those that a mesh axis runs over, the one named last changes fastest.
Arguments:
- adapter_down: bfloat16 [512, 16, 8192], P('adapter', None, 'feature'), may hold values from -6 to 6
- adapter_up: bfloat16 [512, 16, 8192], P('adapter', None, 'feature'), may hold values from -6 to 6
- fisher: float32 [512], P('adapter'), may hold values from 0.1 to 10
- init_v: float32 [8192, 64], P('feature'), may hold values from -0.0625 to 0.0625
- init_u: float32 [8192, 64], P('feature'), may hold values from -0.0625 to 0.0625
- prompt_rows: bfloat16 [16384, 8192], P('adapter', 'feature'), may hold values from -6 to 6
- request_ids: int32 [128], P('adapter'), may hold values from 0 to 511
Outputs:
- served: bfloat16 [16384, 8192], P('adapter', 'feature')
All inputs are finite; a program needn't handle non-finite values.
Results may differ from a plain program's by a relative error of at most 0.025.
Values may be sent and summed in bfloat16 or wider, within the bound.
No kernel may reach another device: no remote copies, remote signals or barrier semaphores. Data moves between devices by JAX's collectives and lax.ppermute only.
A program may use at most 64 MiB of HBM per device.

v0:
```python
import jax
import jax.numpy as jnp
from jax import lax
from jax.experimental import pallas as pl
from jax.experimental.pallas import tpu as pltpu
from jax.sharding import PartitionSpec as P

SWEEPS = 3
RANK = 16
CORES = 2
BF = jnp.bfloat16
F32 = jnp.float32
highest = lax.Precision.HIGHEST


def call(body, outs, *args):
    whole = pl.BlockSpec(memory_space=pltpu.VMEM)
    single = not isinstance(outs, (list, tuple))
    return pl.pallas_call(
        body,
        out_shape=outs,
        in_specs=[whole] * len(args),
        out_specs=whole if single else [whole] * len(outs),
        compiler_params=pltpu.CompilerParams(vmem_limit_bytes=40 * 1024 * 1024),
    )(*args)


def shape(dims, dtype):
    return jax.ShapeDtypeStruct(dims, dtype)


def dot_nt(a, b, precision=None):
    return lax.dot_general(
        a, b, (((1,), (1,)), ((), ())), preferred_element_type=F32, precision=precision
    )


def dot_tn(a, b, precision=None):
    return lax.dot_general(
        a, b, (((0,), (0,)), ((), ())), preferred_element_type=F32, precision=precision
    )


def dot_nn(a, b, precision=None):
    return jnp.dot(a, b, preferred_element_type=F32, precision=precision)


def inverse_factor(gram):
    size = gram.shape[0]
    rows = lax.broadcasted_iota(jnp.int32, (size, size), 0)
    lanes = lax.broadcasted_iota(jnp.int32, (size, size), 1)
    eye = rows == lanes
    diagonal = jnp.where(eye, gram, 0.0)
    by_row = lax.rsqrt(jnp.sum(diagonal, axis=1, keepdims=True))
    by_lane = lax.rsqrt(jnp.sum(diagonal, axis=0, keepdims=True))
    work = jnp.concatenate([gram * by_row * by_lane, eye.astype(F32)], axis=1)
    group = 8
    whole = (group, 2 * size)
    blocks = [work[group * i : group * (i + 1)] for i in range(size // group)]
    within = lax.broadcasted_iota(jnp.int32, whole, 0)
    for b in range(len(blocks)):
        first = group * b
        columns = [
            {
                j: jnp.broadcast_to(blocks[j][:, first + m : first + m + 1], whole)
                for j in range(b, len(blocks))
            }
            for m in range(group)
        ]
        pivot_rows = [blocks[b][i : i + 1] for i in range(group)]
        pivots = {
            (i, m): columns[m][b][i : i + 1] for i in range(group) for m in range(i, group)
        }
        solved = []
        for p in range(0, group, 2):
            top, mix, low = pivots[p, p], pivots[p, p + 1], pivots[p + 1, p + 1]
            over = 1.0 / (top * low - mix * mix)
            a, b01, c = low * over, -mix * over, top * over
            factors = []
            for i in range(p + 2, group):
                x, y = pivots[p, i], pivots[p + 1, i]
                factors.append((i, a * x + b01 * y, b01 * x + c * y))
            for i, u, v in factors:
                for m in range(i, group):
                    pivots[i, m] = pivots[i, m] - (u * pivots[p, m] + v * pivots[p + 1, m])
                pivot_rows[i] = pivot_rows[i] - (u * pivot_rows[p] + v * pivot_rows[p + 1])
            solved.append((a, b01, c, factors))
        terms = [None] * group
        for p in range(group - 2, -1, -2):
            a, b01, c, factors = solved[p // 2]
            t0 = a * pivot_rows[p] + b01 * pivot_rows[p + 1]
            t1 = b01 * pivot_rows[p] + c * pivot_rows[p + 1]
            for i, u, v in factors:
                t0 = t0 - u * terms[i]
                t1 = t1 - v * terms[i]
            terms[p], terms[p + 1] = t0, t1
        for j in range(b + 1, len(blocks)):
            for m in range(group):
                blocks[j] = blocks[j] - columns[m][j] * terms[m]
        done = blocks[b]
        for p in range(0, group, 2):
            second = pivot_rows[p + 1] - (pivots[p, p + 1] / pivots[p, p]) * pivot_rows[p]
            done = jnp.where(within == p, pivot_rows[p], done)
            done = jnp.where(within == p + 1, second, done)
        blocks[b] = done
    work = jnp.concatenate(blocks, axis=0)
    diagonal = jnp.sum(jnp.where(eye, work[:, :size], 0.0), axis=1, keepdims=True)
    return work[:, size:] * lax.rsqrt(diagonal) * by_lane


def write_copies(ref, value):
    for i in range(ref.shape[0]):
        ref[i] = value


def halves(gram):
    high = gram.astype(BF)
    low = (gram - high.astype(F32)).astype(BF)
    return jnp.concatenate([high, low], axis=1)


def weighted_terms(fresh, other, fisher_row):
    count = fresh.shape[1]
    inner = dot_tn(fresh, fresh, highest)
    a = lax.broadcasted_iota(jnp.int32, (count, count), 0) // RANK
    b = lax.broadcasted_iota(jnp.int32, (count, count), 1) // RANK
    inner = jnp.where(a == b, inner, 0.0)
    return (dot_nn(other, inner, highest) * fisher_row).astype(BF)


def added(refs):
    total = refs[0][...].astype(F32)
    for ref in refs[1:]:
        total = total + ref[...].astype(F32)
    return total


def write_tiles(ref, value):
    across = value.shape[1] // 128
    for i in range(ref.shape[0]):
        r, c = divmod(i, across)
        ref[i] = value[16 * r : 16 * r + 16, 128 * c : 128 * c + 128].astype(BF)


def read_tiles(ref, width):
    across = width // 128
    down = ref.shape[0] // across
    return jnp.concatenate(
        [
            jnp.concatenate([ref[r * across + c, :16] for c in range(across)], axis=1)
            for r in range(down)
        ],
        axis=0,
    )


def start_body(down, up, vt, ut, out):
    q = dot_nt(ut[...], up[...])
    p = dot_nt(vt[...], down[...])
    out[...] = jnp.concatenate([q, p], axis=1)


def pair_body(own, got, out):
    total = own[...] + got[...]
    plain = 2 * total.shape[1] - out.shape[1]
    if plain == total.shape[1]:
        out[...] = total.astype(BF)
    else:
        out[...] = jnp.concatenate([total[:, :plain].astype(BF), halves(total[:, plain:])], axis=1)


def first_body(a, b, c, d, stack, fisher_row, tiles, q_out, p_out):
    total = added((a, b, c, d))
    count = total.shape[1] // 2
    q, p = total[:, :count], total[:, count:]
    q_out[...] = q
    p_out[...] = p
    terms = weighted_terms(p, q, fisher_row[...])
    write_tiles(tiles, dot_nn(terms, stack[...]))


def summed(ref):
    total = ref[0].astype(F32)
    for i in range(1, ref.shape[0]):
        total = total + ref[i].astype(F32)
    return total


def sum_body(parts, out):
    write_copies(out, summed(parts).astype(BF))


def sum_ids_body(parts, ids, out):
    write_copies(out, jnp.concatenate([summed(parts).astype(BF), ids[...]], axis=0))


def project_body(tiles, stack, out):
    numer = read_tiles(tiles, stack.shape[1])
    out[...] = jnp.concatenate([dot_nt(numer, stack[...]), dot_nt(numer, numer)], axis=1)


def project_ids_body(tiles, stack, out, ids_out):
    project_body(tiles, stack, out)
    ids = summed(tiles.at[:, 16:])
    ids_out[...] = (ids[0:1] * RANK + ids[1:2]).astype(jnp.int32)


def split_gram(total, at, size):
    return total[:, at : at + size] + total[:, at + size : at + 2 * size]


def renew(parts, other, stack, fisher_row, tiles, fresh_out):
    total = added(parts)
    size, count = other.shape
    inverse = inverse_factor(split_gram(total, count, size))
    fresh = dot_nn(inverse, total[:, :count], highest)
    fresh_out[...] = fresh
    terms = weighted_terms(fresh, other[...], fisher_row[...])
    write_tiles(tiles, dot_nn(terms, stack[...]))
    return inverse


def renew_body(a, b, c, d, other, stack, fisher_row, tiles, fresh_out):
    renew((a, b, c, d), other, stack, fisher_row, tiles, fresh_out)


def last_renew_body(
    a, b, c, d, other, stack, fisher_row, numer_tiles, tiles, fresh_out, basis_out
):
    inverse = renew((a, b, c, d), other, stack, fisher_row, tiles, fresh_out)
    numer = read_tiles(numer_tiles, stack.shape[1]).astype(F32)
    basis_out[...] = dot_nn(inverse, numer, highest).astype(BF)


def pick_body(tiles, stack, prompts, q_ref, ids, picked, hidden_out, gram_out):
    numer = read_tiles(tiles, stack.shape[1])
    z = dot_nt(stack[...], numer).astype(BF)
    q = q_ref[...].T.astype(BF)
    both = jnp.concatenate([z, q], axis=1)
    count = both.shape[0]
    wanted = picked.shape[0] * picked.shape[1]
    r = lax.broadcasted_iota(jnp.int32, (wanted, count), 0)
    c = lax.broadcasted_iota(jnp.int32, (wanted, count), 1)
    hot = ids[...] * RANK + (r & (RANK - 1)) == c
    chosen = dot_nn(hot.astype(F32).astype(BF), both).astype(BF)
    each = picked.shape[1]
    for i in range(picked.shape[0]):
        picked[i] = chosen[i * each : (i + 1) * each]
    hidden_out[...] = dot_nt(numer, prompts[...])
    gram_out[...] = dot_nt(numer, numer)


def join_body(parts, hidden, gram, out, own):
    total = summed(parts)
    own[...] = total
    size = gram.shape[1]
    out[...] = jnp.concatenate([hidden[...], total[:, :size], gram[...]], axis=1)


def serve_body(a, b, c, d, own, basis, out):
    total = added((a, b, c, d))
    size = total.shape[0]
    rows = out.shape[0]
    inverse = inverse_factor(split_gram(total, rows + size, size))
    hidden = dot_nn(inverse, total[:, :rows], highest).astype(BF)
    z = total[:, rows : rows + size]
    p = dot_nt(z, inverse, highest)
    q = own[...][:, size:]
    blocks = own.shape[0] // RANK
    each = rows // blocks
    for j in range(blocks):
        take = slice(j * RANK, (j + 1) * RANK)
        core = dot_tn(q[take], p[take], highest).astype(BF)
        mixed = dot_nn(core, hidden[:, j * each : (j + 1) * each]).astype(BF)
        out[j * each : (j + 1) * each, :] = dot_tn(mixed, basis[...]).astype(BF)


def around_y(value, d):
    size = lax.axis_size("feature")
    return lax.ppermute(value, "feature", [(i, (i + d * CORES) % size) for i in range(size)])


def other_core(value):
    size = lax.axis_size("feature")
    return lax.ppermute(value, "feature", [(i, i ^ 1) for i in range(size)])


def over_feature(value, gram_size):
    rows, lanes = value.shape
    pair = call(pair_body, shape((rows, lanes + gram_size), BF), value, other_core(value))
    return [pair] + [around_y(pair, d) for d in (1, 3, 2)]


def on_device(adapter_down, adapter_up, fisher, init_v, init_u, prompt_rows, request_ids):
    ways = lax.axis_size("adapter")
    width = adapter_down.shape[-1]
    size = init_v.shape[1]
    down = adapter_down.reshape(-1, width)
    up = adapter_up.reshape(-1, width)
    count = down.shape[0]
    rows = prompt_rows.shape[0]
    blocks = request_ids.shape[0]
    position = lax.axis_index("adapter")
    fisher_row = jnp.repeat(fisher, RANK)[None, :]
    tile = (size * width // ways // 128, 128)
    tile_shape = shape((ways, *tile), BF)
    flat = shape((size, count), F32)
    digits = jnp.stack([request_ids // RANK, request_ids % RANK]).astype(BF)
    id_tile = lax.dynamic_update_slice(jnp.zeros(tile, BF), digits, (0, position * blocks))

    def swap(parts):
        return lax.all_to_all(parts, "adapter", 0, 0, tiled=True)

    def reduced(tiles):
        return swap(call(sum_body, tile_shape, swap(tiles)))

    def projected(numer, stack):
        value = call(project_body, shape((size, count + size), F32), numer, stack)
        return over_feature(value, size)

    value = call(
        start_body,
        shape((size, 2 * count), F32),
        down,
        up,
        init_v.T.astype(BF),
        init_u.T.astype(BF),
    )
    tiles, q, p = call(
        first_body, [tile_shape, flat, flat], *over_feature(value, 0), up, fisher_row
    )
    for sweep in range(SWEEPS):
        if sweep == 0:
            copies = call(
                sum_ids_body, shape((ways, 2 * tile[0], 128), BF), swap(tiles), id_tile
            )
            value, every_id = call(
                project_ids_body,
                [shape((size, count + size), F32), shape((1, 128), jnp.int32)],
                swap(copies),
                up,
            )
            parts = over_feature(value, size)
        else:
            numer = reduced(tiles)
            parts = projected(numer, up)
        if sweep < SWEEPS - 1:
            tiles, q = call(renew_body, [tile_shape, flat], *parts, p, down, fisher_row)
            parts = projected(reduced(tiles), down)
            tiles, p = call(renew_body, [tile_shape, flat], *parts, q, up, fisher_row)
        else:
            tiles, q, basis = call(
                last_renew_body,
                [tile_shape, flat, shape((size, width), BF)],
                *parts,
                p,
                down,
                fisher_row,
                numer,
            )
    pick_rows = jnp.repeat(every_id[0, : ways * blocks] - position * fisher.shape[0], RANK)[:, None]
    asked = blocks * RANK
    picked, hidden, gram = call(
        pick_body,
        [shape((ways, asked, 2 * size), BF), shape((size, rows), F32), shape((size, size), F32)],
        reduced(tiles),
        down,
        prompt_rows,
        q,
        pick_rows,
    )
    value, own = call(
        join_body,
        [shape((size, rows + 2 * size), F32), shape((asked, 2 * size), F32)],
        swap(picked),
        hidden,
        gram,
    )
    return call(serve_body, shape((rows, width), BF), *over_feature(value, size), own, basis)


def solution(mesh):
    placed = (
        P("adapter", None, "feature"),
        P("adapter", None, "feature"),
        P("adapter"),
        P("feature", None),
        P("feature", None),
        P("adapter", "feature"),
        P("adapter"),
    )
    return jax.shard_map(
        on_device, mesh=mesh, in_specs=placed, out_specs=P("adapter", "feature"), check_vma=False
    )
```

profile of v0, /device:TPU:1, one launch (start us, length us, event | category | flops | bytes accessed | tf_op | source)
XLA Modules:
  0.0 300.5 jit_solution(11989905070864091792)
XLA Ops:
  2.7 3.3 %collective-permute-start = (f32[64,512]{1,0:T(8,128)S(1)}, f32[64,512]{1,0:T(8,128)S(1)}, u32[]{:S(2)}, u32[]{:S(2)}) collective-permute-start(f32[64,512]{1,0:T(8,128)S(1)} %shard_map.73.own), channel_id=1, source_target_pairs={{0,1},{1,0},{2,3},{3,2},{4,5},{5,4},{6,7},{7,6},{8,9},{9,8},{10,11... | collective-permute-start | bytes 393224 | tf_op jit(solution)/shard_map/ppermute | solution.py:285
  7.0 1.3 collective-permute-start.3
  10.6 1.2 collective-permute-done.3.d
  12.2 1.2 collective-permute-done.1.b
  13.4 1.8 shard_map.75
  15.1 11.2 %all-to-all-start = ((bf16[32,16,128]{2,1,0:T(8,128)(2,1)}), bf16[32,16,128]{2,1,0:T(8,128)(2,1)S(1)}, u32[]{:S(2)}, u32[]{:S(2)}) async-start(bf16[32,16,128]{2,1,0:T(8,128)(2,1)} %get-tuple-element.25), calls=%async_computation | async-start | bytes 262144 | tf_op jit(solution)/shard_map/all_to_all | solution.py:312
  26.7 9.0 %all-to-all-done.parts = bf16[32,16,128]{2,1,0:T(8,128)(2,1)S(1)} async-done(((bf16[32,16,128]{2,1,0:T(8,128)(2,1)}), bf16[32,16,128]{2,1,0:T(8,128)(2,1)S(1)}, u32[]{:S(2)}, u32[]{:S(2)}) %all-to-all-start) | async-done | bytes 131104 | tf_op jit(solution)/shard_map/all_to_all | solution.py:312
  35.7 13.7 %all_to_all.65.tiles = bf16[32,32,128]{2,1,0:T(8,128)(2,1)S(1)} all-to-all(bf16[32,32,128]{2,1,0:T(8,128)(2,1)S(1)} %shard_map.76), channel_id=1, replica_groups=mesh['adapter'=32,'feature'=8] {'adapter'}, dimensions={0} | all-to-all | bytes 524288 | tf_op jit(solution)/shard_map/all_to_all | solution.py:312
  49.8 4.6 %collective-permute-start.4 = (f32[64,320]{1,0:T(8,128)S(1)}, f32[64,320]{1,0:T(8,128)S(1)}, u32[]{:S(2)}, u32[]{:S(2)}) collective-permute-start(f32[64,320]{1,0:T(8,128)S(1)} %get-tuple-element.26.own), channel_id=1, source_target_pairs={{0,1},{1,0},{2,3},{3,2},{4,5},{5,4},{6,7},{7,6},{8,9},{9,8},{10,11... | collective-permute-start | bytes 245768 | tf_op jit(solution)/shard_map/ppermute | solution.py:285
  55.9 1.5 collective-permute-start.6
  57.4 2.5 collective-permute-done.7.d
  59.9 1.6 collective-permute-done.5.b
  61.5 3.5 %shard_map.79 = (bf16[32,16,128]{2,1,0:T(8,128)(2,1)S(1)}, f32[64,256]{1,0:T(8,128)S(1)}) custom-call(bf16[64,384]{1,0:T(8,128)(2,1)S(1)} %shard_map.78.a, bf16[64,384]{1,0:T(8,128)(2,1)S(1)} %collective-permute-done.5.b, bf16[64,384]{1,0:T(8,128)(2,1)S(1)} %collective-permute-done.6.c, bf16[64,384]{1,0:T(8,128)(2,1)S(1)} %collective-permute-done.7.d, ...), custom_call_target="tpu_custom_call" | custom-call | tf_op jit(solution)/shard_map/pallas_call | solution.py:19
  65.0 12.7 %all_to_all.66.parts = bf16[32,16,128]{2,1,0:T(8,128)(2,1)S(1)} all-to-all(bf16[32,16,128]{2,1,0:T(8,128)(2,1)S(1)} %get-tuple-element.28), channel_id=1, replica_groups=mesh['adapter'=32,'feature'=8] {'adapter'}, dimensions={0} | all-to-all | bytes 262144 | tf_op jit(solution)/shard_map/all_to_all | solution.py:312
  77.8 12.6 %all_to_all.67.tiles = bf16[32,16,128]{2,1,0:T(8,128)(2,1)S(1)} all-to-all(bf16[32,16,128]{2,1,0:T(8,128)(2,1)S(1)} %shard_map.80), channel_id=1, replica_groups=mesh['adapter'=32,'feature'=8] {'adapter'}, dimensions={0} | all-to-all | bytes 262144 | tf_op jit(solution)/shard_map/all_to_all | solution.py:312
  90.8 4.7 %collective-permute-start.8 = (f32[64,320]{1,0:T(8,128)S(1)}, f32[64,320]{1,0:T(8,128)S(1)}, u32[]{:S(2)}, u32[]{:S(2)}) collective-permute-start(f32[64,320]{1,0:T(8,128)S(1)} %shard_map.81.own), channel_id=1, source_target_pairs={{0,1},{1,0},{2,3},{3,2},{4,5},{5,4},{6,7},{7,6},{8,9},{9,8},{10,11... | collective-permute-start | bytes 245768 | tf_op jit(solution)/shard_map/ppermute | solution.py:285
  96.6 1.3 collective-permute-start.10
  98.4 2.6 collective-permute-done.11.d
  101.0 1.3 collective-permute-done.9.b
  102.4 3.5 %shard_map.83 = (bf16[32,16,128]{2,1,0:T(8,128)(2,1)S(1)}, f32[64,256]{1,0:T(8,128)S(1)}) custom-call(bf16[64,384]{1,0:T(8,128)(2,1)S(1)} %shard_map.82.a, bf16[64,384]{1,0:T(8,128)(2,1)S(1)} %collective-permute-done.9.b, bf16[64,384]{1,0:T(8,128)(2,1)S(1)} %collective-permute-done.10.c, bf16[64,384]{1,0:T(8,128)(2,1)S(1)} %collective-permute-done.11.d, ...), custom_call_target="tpu_custom_call" | custom-call | tf_op jit(solution)/shard_map/pallas_call | solution.py:19
  105.9 12.4 %all_to_all.68.parts = bf16[32,16,128]{2,1,0:T(8,128)(2,1)S(1)} all-to-all(bf16[32,16,128]{2,1,0:T(8,128)(2,1)S(1)} %get-tuple-element.30), channel_id=1, replica_groups=mesh['adapter'=32,'feature'=8] {'adapter'}, dimensions={0} | all-to-all | bytes 262144 | tf_op jit(solution)/shard_map/all_to_all | solution.py:312
  118.3 12.6 %all_to_all.69.tiles = bf16[32,16,128]{2,1,0:T(8,128)(2,1)S(1)} all-to-all(bf16[32,16,128]{2,1,0:T(8,128)(2,1)S(1)} %shard_map.84), channel_id=1, replica_groups=mesh['adapter'=32,'feature'=8] {'adapter'}, dimensions={0} | all-to-all | bytes 262144 | tf_op jit(solution)/shard_map/all_to_all | solution.py:312
  131.3 4.4 %collective-permute-start.12 = (f32[64,320]{1,0:T(8,128)S(1)}, f32[64,320]{1,0:T(8,128)S(1)}, u32[]{:S(2)}, u32[]{:S(2)}) collective-permute-start(f32[64,320]{1,0:T(8,128)S(1)} %shard_map.85.own), channel_id=1, source_target_pairs={{0,1},{1,0},{2,3},{3,2},{4,5},{5,4},{6,7},{7,6},{8,9},{9,8},{10,11... | collective-permute-start | bytes 245768 | tf_op jit(solution)/shard_map/ppermute | solution.py:285
  138.7 2.5 collective-permute-done.15.d
  141.1 1.3 collective-permute-done.13.b
  142.5 3.5 %shard_map.87 = (bf16[32,16,128]{2,1,0:T(8,128)(2,1)S(1)}, f32[64,256]{1,0:T(8,128)S(1)}) custom-call(bf16[64,384]{1,0:T(8,128)(2,1)S(1)} %shard_map.86.a, bf16[64,384]{1,0:T(8,128)(2,1)S(1)} %collective-permute-done.13.b, bf16[64,384]{1,0:T(8,128)(2,1)S(1)} %collective-permute-done.14.c, bf16[64,384]{1,0:T(8,128)(2,1)S(1)} %collective-permute-done.15.d, ...), custom_call_target="tpu_custom_call" | custom-call | tf_op jit(solution)/shard_map/pallas_call | solution.py:19
  146.0 12.4 %all_to_all.70.parts = bf16[32,16,128]{2,1,0:T(8,128)(2,1)S(1)} all-to-all(bf16[32,16,128]{2,1,0:T(8,128)(2,1)S(1)} %get-tuple-element.32), channel_id=1, replica_groups=mesh['adapter'=32,'feature'=8] {'adapter'}, dimensions={0} | all-to-all | bytes 262144 | tf_op jit(solution)/shard_map/all_to_all | solution.py:312
  158.4 12.7 %all_to_all.71.tiles = bf16[32,16,128]{2,1,0:T(8,128)(2,1)S(1)} all-to-all(bf16[32,16,128]{2,1,0:T(8,128)(2,1)S(1)} %shard_map.88), channel_id=1, replica_groups=mesh['adapter'=32,'feature'=8] {'adapter'}, dimensions={0} | all-to-all | bytes 262144 | tf_op jit(solution)/shard_map/all_to_all | solution.py:312
  171.5 4.2 %collective-permute-start.16 = (f32[64,320]{1,0:T(8,128)S(1)}, f32[64,320]{1,0:T(8,128)S(1)}, u32[]{:S(2)}, u32[]{:S(2)}) collective-permute-start(f32[64,320]{1,0:T(8,128)S(1)} %shard_map.89.own), channel_id=1, source_target_pairs={{0,1},{1,0},{2,3},{3,2},{4,5},{5,4},{6,7},{7,6},{8,9},{9,8},{10,11... | collective-permute-start | bytes 245768 | tf_op jit(solution)/shard_map/ppermute | solution.py:285
  178.7 9.1 %collective-permute-start.17 = (bf16[64,384]{1,0:T(8,128)(2,1)S(1)}, bf16[64,384]{1,0:T(8,128)(2,1)S(1)}, u32[]{:S(2)}, u32[]{:S(2)}) collective-permute-start(bf16[64,384]{1,0:T(8,128)(2,1)S(1)} %shard_map.90.a), channel_id=1, source_target_pairs={{0,2},{1,3},{2,4},{3,5},{4,6},{5,7},{6,0},{7,1},{8,10},{9,11},{10,... | collective-permute-start | bytes 147464 | tf_op jit(solution)/shard_map/ppermute | solution.py:280
  187.8 3.7 %collective-permute-done.17.b = bf16[64,384]{1,0:T(8,128)(2,1)S(1)} collective-permute-done((bf16[64,384]{1,0:T(8,128)(2,1)S(1)}, bf16[64,384]{1,0:T(8,128)(2,1)S(1)}, u32[]{:S(2)}, u32[]{:S(2)}) %collective-permute-start.17) | collective-permute-done | bytes 49184 | tf_op jit(solution)/shard_map/ppermute | solution.py:280
  191.5 3.5 %shard_map.91 = (bf16[32,16,128]{2,1,0:T(8,128)(2,1)S(1)}, f32[64,256]{1,0:T(8,128)S(1)}) custom-call(bf16[64,384]{1,0:T(8,128)(2,1)S(1)} %shard_map.90.a, bf16[64,384]{1,0:T(8,128)(2,1)S(1)} %collective-permute-done.17.b, bf16[64,384]{1,0:T(8,128)(2,1)S(1)} %collective-permute-done.18.c, bf16[64,384]{1,0:T(8,128)(2,1)S(1)} %collective-permute-done.19.d, ...), custom_call_target="tpu_custom_call" | custom-call | tf_op jit(solution)/shard_map/pallas_call | solution.py:19
  195.0 12.4 %all_to_all.72.parts = bf16[32,16,128]{2,1,0:T(8,128)(2,1)S(1)} all-to-all(bf16[32,16,128]{2,1,0:T(8,128)(2,1)S(1)} %get-tuple-element.34), channel_id=1, replica_groups=mesh['adapter'=32,'feature'=8] {'adapter'}, dimensions={0} | all-to-all | bytes 262144 | tf_op jit(solution)/shard_map/all_to_all | solution.py:312
  207.4 12.6 %all_to_all.73.tiles.numer_tiles = bf16[32,16,128]{2,1,0:T(8,128)(2,1)S(1)} all-to-all(bf16[32,16,128]{2,1,0:T(8,128)(2,1)S(1)} %shard_map.92), channel_id=1, replica_groups=mesh['adapter'=32,'feature'=8] {'adapter'}, dimensions={0} | all-to-all | bytes 262144 | tf_op jit(solution)/shard_map/all_to_all | solution.py:312
  220.4 4.7 %collective-permute-start.20 = (f32[64,320]{1,0:T(8,128)S(1)}, f32[64,320]{1,0:T(8,128)S(1)}, u32[]{:S(2)}, u32[]{:S(2)}) collective-permute-start(f32[64,320]{1,0:T(8,128)S(1)} %shard_map.93.own), channel_id=1, source_target_pairs={{0,1},{1,0},{2,3},{3,2},{4,5},{5,4},{6,7},{7,6},{8,9},{9,8},{10,11... | collective-permute-start | bytes 245768 | tf_op jit(solution)/shard_map/ppermute | solution.py:285
  226.2 1.6 collective-permute-start.22
  227.8 2.8 collective-permute-done.23.d
  230.7 1.3 collective-permute-done.21.b
  232.0 3.7 %shard_map.95 = (bf16[32,16,128]{2,1,0:T(8,128)(2,1)S(1)}, f32[64,256]{1,0:T(8,128)S(1)}, bf16[64,1024]{1,0:T(8,128)(2,1)S(1)}) custom-call(bf16[64,384]{1,0:T(8,128)(2,1)S(1)} %shard_map.94.a, bf16[64,384]{1,0:T(8,128)(2,1)S(1)} %collective-permute-done.21.b, bf16[64,384]{1,0:T(8,128)(2,1)S(1)} %collective-permute-done.22.c, ...), custom_call_target="tpu_custom_call" | custom-call | tf_op jit(solution)/shard_map/pallas_call | solution.py:19
  235.7 12.5 %all_to_all.74.parts = bf16[32,16,128]{2,1,0:T(8,128)(2,1)S(1)} all-to-all(bf16[32,16,128]{2,1,0:T(8,128)(2,1)S(1)} %get-tuple-element.36), channel_id=1, replica_groups=mesh['adapter'=32,'feature'=8] {'adapter'}, dimensions={0} | all-to-all | bytes 262144 | tf_op jit(solution)/shard_map/all_to_all | solution.py:312
  248.9 3.9 %all-to-all-start.11 = ((bf16[32,16,128]{2,1,0:T(8,128)(2,1)}), bf16[32,16,128]{2,1,0:T(8,128)(2,1)S(1)}, u32[]{:S(2)}, u32[]{:S(2)}) async-start(bf16[32,16,128]{2,1,0:T(8,128)(2,1)} %shard_map.96), calls=%async_computation.11 | async-start | bytes 262144 | tf_op jit(solution)/shard_map/all_to_all | solution.py:312
  253.5 8.7 %all-to-all-done.11.tiles = bf16[32,16,128]{2,1,0:T(8,128)(2,1)S(1)} async-done(((bf16[32,16,128]{2,1,0:T(8,128)(2,1)}), bf16[32,16,128]{2,1,0:T(8,128)(2,1)S(1)}, u32[]{:S(2)}, u32[]{:S(2)}) %all-to-all-start.11) | async-done | bytes 131104 | tf_op jit(solution)/shard_map/all_to_all | solution.py:312
  263.3 16.0 %all_to_all.75.parts = bf16[32,64,128]{2,1,0:T(8,128)(2,1)S(1)} all-to-all(bf16[32,64,128]{2,1,0:T(8,128)(2,1)S(1)} %get-tuple-element.39), channel_id=1, replica_groups=mesh['adapter'=32,'feature'=8] {'adapter'}, dimensions={0} | all-to-all | bytes 1048576 | tf_op jit(solution)/shard_map/all_to_all | solution.py:312
  279.4 6.4 %collective-permute-start.24 = (f32[64,640]{1,0:T(8,128)S(1)}, f32[64,640]{1,0:T(8,128)S(1)}, u32[]{:S(2)}, u32[]{:S(2)}) collective-permute-start(f32[64,640]{1,0:T(8,128)S(1)} %get-tuple-element.42.own), channel_id=1, source_target_pairs={{0,1},{1,0},{2,3},{3,2},{4,5},{5,4},{6,7},{7,6},{8,9},{9,8},{10,11... | collective-permute-start | bytes 491528 | tf_op jit(solution)/shard_map/ppermute | solution.py:285
  287.3 1.6 collective-permute-start.26
  289.0 3.6 %collective-permute-done.27.d = bf16[64,704]{1,0:T(8,128)(2,1)S(1)} collective-permute-done((bf16[64,704]{1,0:T(8,128)(2,1)S(1)}, bf16[64,704]{1,0:T(8,128)(2,1)S(1)}, u32[]{:S(2)}, u32[]{:S(2)}) %collective-permute-start.27) | collective-permute-done | bytes 90144 | tf_op jit(solution)/shard_map/ppermute | solution.py:280
  292.6 1.9 collective-permute-done.25.b
  294.5 5.7 %shard_map.100 = bf16[512,1024]{1,0:T(8,128)(2,1)} custom-call(bf16[64,704]{1,0:T(8,128)(2,1)S(1)} %shard_map.99.a, bf16[64,704]{1,0:T(8,128)(2,1)S(1)} %collective-permute-done.25.b, bf16[64,704]{1,0:T(8,128)(2,1)S(1)} %collective-permute-done.26.c, bf16[64,704]{1,0:T(8,128)(2,1)S(1)} %collective-permute-done.27.d, f32[64,128]{1,0:T(8,128)S(1)} %get-tuple-element.43.own, ...), custom_call_target="tpu_custom_call" | custom-call | tf_op jit(solution)/shard_map/pallas_call | solution.py:19
  (73 shorter events, 23.1 us)
Async XLA Ops:
  0.0 1.2 copy-start
  1.2 1.0 copy-start.1
  2.7 4.3 %collective-permute-start = (f32[64,512]{1,0:T(8,128)S(1)}, f32[64,512]{1,0:T(8,128)S(1)}, u32[]{:S(2)}, u32[]{:S(2)}) collective-permute-start(f32[64,512]{1,0:T(8,128)S(1)} %shard_map.73.own), channel_id=1, source_target_pairs={{0,1},{1,0},{2,3},{3,2},{4,5},{5,4},{6,7},{7,6},{8,9},{9,8},{10,11... | collective-permute-start | bytes 393224 | tf_op jit(solution)/shard_map/ppermute | solution.py:285
  7.0 4.7 %collective-permute-start.3 = (bf16[64,512]{1,0:T(8,128)(2,1)S(1)}, bf16[64,512]{1,0:T(8,128)(2,1)S(1)}, u32[]{:S(2)}, u32[]{:S(2)}) collective-permute-start(bf16[64,512]{1,0:T(8,128)(2,1)S(1)} %shard_map.74.a), channel_id=1, source_target_pairs={{0,4},{1,5},{2,6},{3,7},{4,0},{5,1},{6,2},{7,3},{8,12},{9,13},{10,... | collective-permute-start | bytes 196616 | tf_op jit(solution)/shard_map/ppermute | solution.py:280
  8.3 3.9 %collective-permute-start.2 = (bf16[64,512]{1,0:T(8,128)(2,1)S(1)}, bf16[64,512]{1,0:T(8,128)(2,1)S(1)}, u32[]{:S(2)}, u32[]{:S(2)}) collective-permute-start(bf16[64,512]{1,0:T(8,128)(2,1)S(1)} %shard_map.74.a), channel_id=1, source_target_pairs={{0,6},{1,7},{2,0},{3,1},{4,2},{5,3},{6,4},{7,5},{8,14},{9,15},{10,... | collective-permute-start | bytes 196616 | tf_op jit(solution)/shard_map/ppermute | solution.py:280
  9.1 4.3 %collective-permute-start.1 = (bf16[64,512]{1,0:T(8,128)(2,1)S(1)}, bf16[64,512]{1,0:T(8,128)(2,1)S(1)}, u32[]{:S(2)}, u32[]{:S(2)}) collective-permute-start(bf16[64,512]{1,0:T(8,128)(2,1)S(1)} %shard_map.74.a), channel_id=1, source_target_pairs={{0,2},{1,3},{2,4},{3,5},{4,6},{5,7},{6,0},{7,1},{8,10},{9,11},{10,... | collective-permute-start | bytes 196616 | tf_op jit(solution)/shard_map/ppermute | solution.py:280
  9.7 0.7 copy-start.4
  15.1 11.2 %copy-start.5 = (s32[4]{0:T(128)S(1)}, s32[4]{0:T(128)}, u32[]{:S(2)}) copy-start(s32[4]{0:T(128)} %param.13) | copy-start | bytes 52
  15.1 20.5 %all-to-all-start = ((bf16[32,16,128]{2,1,0:T(8,128)(2,1)}), bf16[32,16,128]{2,1,0:T(8,128)(2,1)S(1)}, u32[]{:S(2)}, u32[]{:S(2)}) async-start(bf16[32,16,128]{2,1,0:T(8,128)(2,1)} %get-tuple-element.25), calls=%async_computation | async-start | bytes 262144 | tf_op jit(solution)/shard_map/all_to_all | solution.py:312
  49.4 12.1 %copy-start.2 = (bf16[16,16,1024]{2,1,0:T(8,128)(2,1)S(1)}, bf16[16,16,1024]{2,1,0:T(8,128)(2,1)}, u32[]{:S(2)}) copy-start(bf16[16,16,1024]{2,1,0:T(8,128)(2,1)} %param.7) | copy-start | bytes 1572868
  49.8 5.6 %collective-permute-start.4 = (f32[64,320]{1,0:T(8,128)S(1)}, f32[64,320]{1,0:T(8,128)S(1)}, u32[]{:S(2)}, u32[]{:S(2)}) collective-permute-start(f32[64,320]{1,0:T(8,128)S(1)} %get-tuple-element.26.own), channel_id=1, source_target_pairs={{0,1},{1,0},{2,3},{3,2},{4,5},{5,4},{6,7},{7,6},{8,9},{9,8},{10,11... | collective-permute-start | bytes 245768 | tf_op jit(solution)/shard_map/ppermute | solution.py:285
  55.4 4.5 %collective-permute-start.7 = (bf16[64,384]{1,0:T(8,128)(2,1)S(1)}, bf16[64,384]{1,0:T(8,128)(2,1)S(1)}, u32[]{:S(2)}, u32[]{:S(2)}) collective-permute-start(bf16[64,384]{1,0:T(8,128)(2,1)S(1)} %shard_map.78.a), channel_id=1, source_target_pairs={{0,4},{1,5},{2,6},{3,7},{4,0},{5,1},{6,2},{7,3},{8,12},{9,13},{10,... | collective-permute-start | bytes 147464 | tf_op jit(solution)/shard_map/ppermute | solution.py:280
  55.9 4.0 %collective-permute-start.6 = (bf16[64,384]{1,0:T(8,128)(2,1)S(1)}, bf16[64,384]{1,0:T(8,128)(2,1)S(1)}, u32[]{:S(2)}, u32[]{:S(2)}) collective-permute-start(bf16[64,384]{1,0:T(8,128)(2,1)S(1)} %shard_map.78.a), channel_id=1, source_target_pairs={{0,6},{1,7},{2,0},{3,1},{4,2},{5,3},{6,4},{7,5},{8,14},{9,15},{10,... | collective-permute-start | bytes 147464 | tf_op jit(solution)/shard_map/ppermute | solution.py:280
  57.4 4.2 %collective-permute-start.5 = (bf16[64,384]{1,0:T(8,128)(2,1)S(1)}, bf16[64,384]{1,0:T(8,128)(2,1)S(1)}, u32[]{:S(2)}, u32[]{:S(2)}) collective-permute-start(bf16[64,384]{1,0:T(8,128)(2,1)S(1)} %shard_map.78.a), channel_id=1, source_target_pairs={{0,2},{1,3},{2,4},{3,5},{4,6},{5,7},{6,0},{7,1},{8,10},{9,11},{10,... | collective-permute-start | bytes 147464 | tf_op jit(solution)/shard_map/ppermute | solution.py:280
  90.8 5.7 %collective-permute-start.8 = (f32[64,320]{1,0:T(8,128)S(1)}, f32[64,320]{1,0:T(8,128)S(1)}, u32[]{:S(2)}, u32[]{:S(2)}) collective-permute-start(f32[64,320]{1,0:T(8,128)S(1)} %shard_map.81.own), channel_id=1, source_target_pairs={{0,1},{1,0},{2,3},{3,2},{4,5},{5,4},{6,7},{7,6},{8,9},{9,8},{10,11... | collective-permute-start | bytes 245768 | tf_op jit(solution)/shard_map/ppermute | solution.py:285
  96.5 4.5 %collective-permute-start.11 = (bf16[64,384]{1,0:T(8,128)(2,1)S(1)}, bf16[64,384]{1,0:T(8,128)(2,1)S(1)}, u32[]{:S(2)}, u32[]{:S(2)}) collective-permute-start(bf16[64,384]{1,0:T(8,128)(2,1)S(1)} %shard_map.82.a), channel_id=1, source_target_pairs={{0,4},{1,5},{2,6},{3,7},{4,0},{5,1},{6,2},{7,3},{8,12},{9,13},{10,... | collective-permute-start | bytes 147464 | tf_op jit(solution)/shard_map/ppermute | solution.py:280
  96.6 4.4 %collective-permute-start.10 = (bf16[64,384]{1,0:T(8,128)(2,1)S(1)}, bf16[64,384]{1,0:T(8,128)(2,1)S(1)}, u32[]{:S(2)}, u32[]{:S(2)}) collective-permute-start(bf16[64,384]{1,0:T(8,128)(2,1)S(1)} %shard_map.82.a), channel_id=1, source_target_pairs={{0,6},{1,7},{2,0},{3,1},{4,2},{5,3},{6,4},{7,5},{8,14},{9,15},{10,... | collective-permute-start | bytes 147464 | tf_op jit(solution)/shard_map/ppermute | solution.py:280
  97.9 4.5 %collective-permute-start.9 = (bf16[64,384]{1,0:T(8,128)(2,1)S(1)}, bf16[64,384]{1,0:T(8,128)(2,1)S(1)}, u32[]{:S(2)}, u32[]{:S(2)}) collective-permute-start(bf16[64,384]{1,0:T(8,128)(2,1)S(1)} %shard_map.82.a), channel_id=1, source_target_pairs={{0,2},{1,3},{2,4},{3,5},{4,6},{5,7},{6,0},{7,1},{8,10},{9,11},{10,... | collective-permute-start | bytes 147464 | tf_op jit(solution)/shard_map/ppermute | solution.py:280
  131.3 5.3 %collective-permute-start.12 = (f32[64,320]{1,0:T(8,128)S(1)}, f32[64,320]{1,0:T(8,128)S(1)}, u32[]{:S(2)}, u32[]{:S(2)}) collective-permute-start(f32[64,320]{1,0:T(8,128)S(1)} %shard_map.85.own), channel_id=1, source_target_pairs={{0,1},{1,0},{2,3},{3,2},{4,5},{5,4},{6,7},{7,6},{8,9},{9,8},{10,11... | collective-permute-start | bytes 245768 | tf_op jit(solution)/shard_map/ppermute | solution.py:285
  136.6 4.5 %collective-permute-start.15 = (bf16[64,384]{1,0:T(8,128)(2,1)S(1)}, bf16[64,384]{1,0:T(8,128)(2,1)S(1)}, u32[]{:S(2)}, u32[]{:S(2)}) collective-permute-start(bf16[64,384]{1,0:T(8,128)(2,1)S(1)} %shard_map.86.a), channel_id=1, source_target_pairs={{0,4},{1,5},{2,6},{3,7},{4,0},{5,1},{6,2},{7,3},{8,12},{9,13},{10,... | collective-permute-start | bytes 147464 | tf_op jit(solution)/shard_map/ppermute | solution.py:280
  137.2 3.9 %collective-permute-start.14 = (bf16[64,384]{1,0:T(8,128)(2,1)S(1)}, bf16[64,384]{1,0:T(8,128)(2,1)S(1)}, u32[]{:S(2)}, u32[]{:S(2)}) collective-permute-start(bf16[64,384]{1,0:T(8,128)(2,1)S(1)} %shard_map.86.a), channel_id=1, source_target_pairs={{0,6},{1,7},{2,0},{3,1},{4,2},{5,3},{6,4},{7,5},{8,14},{9,15},{10,... | collective-permute-start | bytes 147464 | tf_op jit(solution)/shard_map/ppermute | solution.py:280
  138.2 4.2 %collective-permute-start.13 = (bf16[64,384]{1,0:T(8,128)(2,1)S(1)}, bf16[64,384]{1,0:T(8,128)(2,1)S(1)}, u32[]{:S(2)}, u32[]{:S(2)}) collective-permute-start(bf16[64,384]{1,0:T(8,128)(2,1)S(1)} %shard_map.86.a), channel_id=1, source_target_pairs={{0,2},{1,3},{2,4},{3,5},{4,6},{5,7},{6,0},{7,1},{8,10},{9,11},{10,... | collective-permute-start | bytes 147464 | tf_op jit(solution)/shard_map/ppermute | solution.py:280
  171.5 5.1 %collective-permute-start.16 = (f32[64,320]{1,0:T(8,128)S(1)}, f32[64,320]{1,0:T(8,128)S(1)}, u32[]{:S(2)}, u32[]{:S(2)}) collective-permute-start(f32[64,320]{1,0:T(8,128)S(1)} %shard_map.89.own), channel_id=1, source_target_pairs={{0,1},{1,0},{2,3},{3,2},{4,5},{5,4},{6,7},{7,6},{8,9},{9,8},{10,11... | collective-permute-start | bytes 245768 | tf_op jit(solution)/shard_map/ppermute | solution.py:285
  176.8 11.1 %collective-permute-start.19 = (bf16[64,384]{1,0:T(8,128)(2,1)S(1)}, bf16[64,384]{1,0:T(8,128)(2,1)S(1)}, u32[]{:S(2)}, u32[]{:S(2)}) collective-permute-start(bf16[64,384]{1,0:T(8,128)(2,1)S(1)} %shard_map.90.a), channel_id=1, source_target_pairs={{0,4},{1,5},{2,6},{3,7},{4,0},{5,1},{6,2},{7,3},{8,12},{9,13},{10,... | collective-permute-start | bytes 147464 | tf_op jit(solution)/shard_map/ppermute | solution.py:280
  177.7 10.1 %collective-permute-start.18 = (bf16[64,384]{1,0:T(8,128)(2,1)S(1)}, bf16[64,384]{1,0:T(8,128)(2,1)S(1)}, u32[]{:S(2)}, u32[]{:S(2)}) collective-permute-start(bf16[64,384]{1,0:T(8,128)(2,1)S(1)} %shard_map.90.a), channel_id=1, source_target_pairs={{0,6},{1,7},{2,0},{3,1},{4,2},{5,3},{6,4},{7,5},{8,14},{9,15},{10,... | collective-permute-start | bytes 147464 | tf_op jit(solution)/shard_map/ppermute | solution.py:280
  178.7 12.8 %collective-permute-start.17 = (bf16[64,384]{1,0:T(8,128)(2,1)S(1)}, bf16[64,384]{1,0:T(8,128)(2,1)S(1)}, u32[]{:S(2)}, u32[]{:S(2)}) collective-permute-start(bf16[64,384]{1,0:T(8,128)(2,1)S(1)} %shard_map.90.a), channel_id=1, source_target_pairs={{0,2},{1,3},{2,4},{3,5},{4,6},{5,7},{6,0},{7,1},{8,10},{9,11},{10,... | collective-permute-start | bytes 147464 | tf_op jit(solution)/shard_map/ppermute | solution.py:280
  220.4 5.7 %collective-permute-start.20 = (f32[64,320]{1,0:T(8,128)S(1)}, f32[64,320]{1,0:T(8,128)S(1)}, u32[]{:S(2)}, u32[]{:S(2)}) collective-permute-start(f32[64,320]{1,0:T(8,128)S(1)} %shard_map.93.own), channel_id=1, source_target_pairs={{0,1},{1,0},{2,3},{3,2},{4,5},{5,4},{6,7},{7,6},{8,9},{9,8},{10,11... | collective-permute-start | bytes 245768 | tf_op jit(solution)/shard_map/ppermute | solution.py:285
  226.2 4.5 %collective-permute-start.23 = (bf16[64,384]{1,0:T(8,128)(2,1)S(1)}, bf16[64,384]{1,0:T(8,128)(2,1)S(1)}, u32[]{:S(2)}, u32[]{:S(2)}) collective-permute-start(bf16[64,384]{1,0:T(8,128)(2,1)S(1)} %shard_map.94.a), channel_id=1, source_target_pairs={{0,4},{1,5},{2,6},{3,7},{4,0},{5,1},{6,2},{7,3},{8,12},{9,13},{10,... | collective-permute-start | bytes 147464 | tf_op jit(solution)/shard_map/ppermute | solution.py:280
  226.2 4.4 %collective-permute-start.22 = (bf16[64,384]{1,0:T(8,128)(2,1)S(1)}, bf16[64,384]{1,0:T(8,128)(2,1)S(1)}, u32[]{:S(2)}, u32[]{:S(2)}) collective-permute-start(bf16[64,384]{1,0:T(8,128)(2,1)S(1)} %shard_map.94.a), channel_id=1, source_target_pairs={{0,6},{1,7},{2,0},{3,1},{4,2},{5,3},{6,4},{7,5},{8,14},{9,15},{10,... | collective-permute-start | bytes 147464 | tf_op jit(solution)/shard_map/ppermute | solution.py:280
  227.8 4.2 %collective-permute-start.21 = (bf16[64,384]{1,0:T(8,128)(2,1)S(1)}, bf16[64,384]{1,0:T(8,128)(2,1)S(1)}, u32[]{:S(2)}, u32[]{:S(2)}) collective-permute-start(bf16[64,384]{1,0:T(8,128)(2,1)S(1)} %shard_map.94.a), channel_id=1, source_target_pairs={{0,2},{1,3},{2,4},{3,5},{4,6},{5,7},{6,0},{7,1},{8,10},{9,11},{10,... | collective-permute-start | bytes 147464 | tf_op jit(solution)/shard_map/ppermute | solution.py:280
  235.7 26.5 %copy-start.3 = (bf16[512,1024]{1,0:T(8,128)(2,1)S(1)}, bf16[512,1024]{1,0:T(8,128)(2,1)}, u32[]{:S(2)}) copy-start(bf16[512,1024]{1,0:T(8,128)(2,1)} %prompts.1) | copy-start | bytes 3145732
  248.9 13.3 %all-to-all-start.11 = ((bf16[32,16,128]{2,1,0:T(8,128)(2,1)}), bf16[32,16,128]{2,1,0:T(8,128)(2,1)S(1)}, u32[]{:S(2)}, u32[]{:S(2)}) async-start(bf16[32,16,128]{2,1,0:T(8,128)(2,1)} %shard_map.96), calls=%async_computation.11 | async-start | bytes 262144 | tf_op jit(solution)/shard_map/all_to_all | solution.py:312
  279.4 7.5 %collective-permute-start.24 = (f32[64,640]{1,0:T(8,128)S(1)}, f32[64,640]{1,0:T(8,128)S(1)}, u32[]{:S(2)}, u32[]{:S(2)}) collective-permute-start(f32[64,640]{1,0:T(8,128)S(1)} %get-tuple-element.42.own), channel_id=1, source_target_pairs={{0,1},{1,0},{2,3},{3,2},{4,5},{5,4},{6,7},{7,6},{8,9},{9,8},{10,11... | collective-permute-start | bytes 491528 | tf_op jit(solution)/shard_map/ppermute | solution.py:285
  287.0 5.5 %collective-permute-start.27 = (bf16[64,704]{1,0:T(8,128)(2,1)S(1)}, bf16[64,704]{1,0:T(8,128)(2,1)S(1)}, u32[]{:S(2)}, u32[]{:S(2)}) collective-permute-start(bf16[64,704]{1,0:T(8,128)(2,1)S(1)} %shard_map.99.a), channel_id=1, source_target_pairs={{0,4},{1,5},{2,6},{3,7},{4,0},{5,1},{6,2},{7,3},{8,12},{9,13},{10,... | collective-permute-start | bytes 270344 | tf_op jit(solution)/shard_map/ppermute | solution.py:280
  287.3 5.3 %collective-permute-start.26 = (bf16[64,704]{1,0:T(8,128)(2,1)S(1)}, bf16[64,704]{1,0:T(8,128)(2,1)S(1)}, u32[]{:S(2)}, u32[]{:S(2)}) collective-permute-start(bf16[64,704]{1,0:T(8,128)(2,1)S(1)} %shard_map.99.a), channel_id=1, source_target_pairs={{0,6},{1,7},{2,0},{3,1},{4,2},{5,3},{6,4},{7,5},{8,14},{9,15},{10,... | collective-permute-start | bytes 270344 | tf_op jit(solution)/shard_map/ppermute | solution.py:280
  288.9 5.7 %collective-permute-start.25 = (bf16[64,704]{1,0:T(8,128)(2,1)S(1)}, bf16[64,704]{1,0:T(8,128)(2,1)S(1)}, u32[]{:S(2)}, u32[]{:S(2)}) collective-permute-start(bf16[64,704]{1,0:T(8,128)(2,1)S(1)} %shard_map.99.a), channel_id=1, source_target_pairs={{0,2},{1,3},{2,4},{3,5},{4,6},{5,7},{6,0},{7,1},{8,10},{9,11},{10,... | collective-permute-start | bytes 270344 | tf_op jit(solution)/shard_map/ppermute | solution.py:280
where the time goes:
time: 305 us; the launch traced here: 300 us
  blocking collectives  143 us (47%)
  starting transfers between devices  70.7 us (23%)
  waiting for transfers between devices  52.6 us (17%)
  Pallas kernels  30 us (10%)
    all_to_all x11, blocking collectives, swap(): return lax.all_to_all(parts, 'adapter', 0, 0, tiled=True)  143 us
    ppermute x7, starting transfers between devices, other_core(): return lax.ppermute(value, 'feature', [(i, i ^ 1) for i in range(size)])  32.4 us
    pallas_call x28, Pallas kernels, call(): pl.pallas_call(body, out_shape=outs, in_specs=[whole] * len(args), out_sp...  30 us
    ppermute x21, waiting for transfers between devices, around_y(): lax.ppermute(value, 'feature', [(i, (i + d * CORES) % size) for i in rang...  28.2 us
    ppermute x21, starting transfers between devices, around_y(): lax.ppermute(value, 'feature', [(i, (i + d * CORES) % size) for i in rang...  23.2 us
    all_to_all x2, waiting for transfers between devices, swap(): return lax.all_to_all(parts, 'adapter', 0, 0, tiled=True)  17.7 us
    all_to_all x2, starting transfers between devices, swap(): return lax.all_to_all(parts, 'adapter', 0, 0, tiled=True)  15 us
    ppermute x7, waiting for transfers between devices, other_core(): return lax.ppermute(value, 'feature', [(i, i ^ 1) for i in range(size)])  6.74 us
  transfers between devices with their start and end apart: 30, of which 24 were waited for; matrix products, arithmetic and copies ran while one was open for 0% of the time, Pallas kernels for 0%

commit v1 on v0

--- a/solution.py
+++ b/solution.py
@@ -10,16 +10,16 @@
 CORES = 2
 BF = jnp.bfloat16
 F32 = jnp.float32
-highest = lax.Precision.HIGHEST
 
 
 def call(body, outs, *args):
     whole = pl.BlockSpec(memory_space=pltpu.VMEM)
+    scalar = pl.BlockSpec(memory_space=pltpu.SMEM)
     single = not isinstance(outs, (list, tuple))
     return pl.pallas_call(
         body,
         out_shape=outs,
-        in_specs=[whole] * len(args),
+        in_specs=[scalar if arg.shape == (1,) else whole for arg in args],
         out_specs=whole if single else [whole] * len(outs),
         compiler_params=pltpu.CompilerParams(vmem_limit_bytes=40 * 1024 * 1024),
     )(*args)
@@ -43,6 +43,13 @@
 
 def dot_nn(a, b, precision=None):
     return jnp.dot(a, b, preferred_element_type=F32, precision=precision)
+
+
+def in_three(product, a, b):
+    a_high, b_high = a.astype(BF), b.astype(BF)
+    a_low = (a - a_high.astype(F32)).astype(BF)
+    b_low = (b - b_high.astype(F32)).astype(BF)
+    return product(a_high, b_high) + (product(a_high, b_low) + product(a_low, b_high))
 
 
 def inverse_factor(gram):
@@ -121,11 +128,11 @@
 
 def weighted_terms(fresh, other, fisher_row):
     count = fresh.shape[1]
-    inner = dot_tn(fresh, fresh, highest)
+    inner = in_three(dot_tn, fresh, fresh)
     a = lax.broadcasted_iota(jnp.int32, (count, count), 0) // RANK
     b = lax.broadcasted_iota(jnp.int32, (count, count), 1) // RANK
     inner = jnp.where(a == b, inner, 0.0)
-    return (dot_nn(other, inner, highest) * fisher_row).astype(BF)
+    return (in_three(dot_nn, other, inner) * fisher_row).astype(BF)
 
 
 def added(refs):
@@ -213,7 +220,7 @@
     total = added(parts)
     size, count = other.shape
     inverse = inverse_factor(split_gram(total, count, size))
-    fresh = dot_nn(inverse, total[:, :count], highest)
+    fresh = in_three(dot_nn, inverse, total[:, :count])
     fresh_out[...] = fresh
     terms = weighted_terms(fresh, other[...], fisher_row[...])
     write_tiles(tiles, dot_nn(terms, stack[...]))
@@ -229,48 +236,77 @@
 ):
     inverse = renew((a, b, c, d), other, stack, fisher_row, tiles, fresh_out)
     numer = read_tiles(numer_tiles, stack.shape[1]).astype(F32)
-    basis_out[...] = dot_nn(inverse, numer, highest).astype(BF)
-
-
-def pick_body(tiles, stack, prompts, q_ref, ids, picked, hidden_out, gram_out):
+    basis_out[...] = in_three(dot_nn, inverse, numer).astype(BF)
+
+
+def side_by_side(value):
+    half = value.shape[0] // 2
+    lanes = lax.broadcasted_iota(jnp.int32, (half, value.shape[1]), 1)
+    return jnp.where(lanes < value.shape[1] // 2, value[:half], value[half:])
+
+
+def one_below_other(value):
+    half = value.shape[1] // 2
+    return jnp.concatenate([value[:, :half], value[:, half:]], axis=0)
+
+
+def pick_body(core, tiles, stack, prompts, q_ref, ids, picked, hidden_out, gram_out):
     numer = read_tiles(tiles, stack.shape[1])
     z = dot_nt(stack[...], numer).astype(BF)
     q = q_ref[...].T.astype(BF)
-    both = jnp.concatenate([z, q], axis=1)
-    count = both.shape[0]
-    wanted = picked.shape[0] * picked.shape[1]
+    count, size = z.shape
+    ways = picked.shape[0]
+    wanted = ids.shape[0]
     r = lax.broadcasted_iota(jnp.int32, (wanted, count), 0)
     c = lax.broadcasted_iota(jnp.int32, (wanted, count), 1)
-    hot = ids[...] * RANK + (r & (RANK - 1)) == c
-    chosen = dot_nn(hot.astype(F32).astype(BF), both).astype(BF)
-    each = picked.shape[1]
-    for i in range(picked.shape[0]):
-        picked[i] = chosen[i * each : (i + 1) * each]
+    hot = (ids[...] * RANK + (r & (RANK - 1)) == c).astype(F32).astype(BF)
+    chosen_z = dot_nn(hot, jnp.concatenate([z, z], axis=1))
+    chosen_q = dot_nn(hot, jnp.concatenate([q, q], axis=1))
+    each = wanted // ways
+    for i in range(ways):
+        at = i * each
+        first = chosen_q[at : at + each // 2]
+        second = chosen_q[at + each // 2 : at + each]
+        mine = jnp.where(core[0] == 0, first, second)
+        picked[i] = jnp.concatenate(
+            [side_by_side(chosen_z[at : at + each]), side_by_side(mine)], axis=0
+        ).astype(BF)
     hidden_out[...] = dot_nt(numer, prompts[...])
     gram_out[...] = dot_nt(numer, numer)
 
 
-def join_body(parts, hidden, gram, out, own):
+def join_body(core, parts, hidden, gram, out):
     total = summed(parts)
-    own[...] = total
     size = gram.shape[1]
-    out[...] = jnp.concatenate([hidden[...], total[:, :size], gram[...]], axis=1)
-
-
-def serve_body(a, b, c, d, own, basis, out):
+    cut = total.shape[0] * 2 // 3
+    z = one_below_other(total[:cut])
+    q = one_below_other(total[cut:])
+    none = jnp.zeros_like(q)
+    q = jnp.where(
+        core[0] == 0, jnp.concatenate([q, none], axis=0), jnp.concatenate([none, q], axis=0)
+    )
+    out[...] = jnp.concatenate([hidden[...], z, q, gram[...]], axis=1)
+
+
+def serve_body(a, b, c, d, basis, out):
     total = added((a, b, c, d))
     size = total.shape[0]
     rows = out.shape[0]
-    inverse = inverse_factor(split_gram(total, rows + size, size))
-    hidden = dot_nn(inverse, total[:, :rows], highest).astype(BF)
+    asked = size // RANK
+    each = rows // asked
     z = total[:, rows : rows + size]
-    p = dot_nt(z, inverse, highest)
-    q = own[...][:, size:]
-    blocks = own.shape[0] // RANK
-    each = rows // blocks
-    for j in range(blocks):
+    q = a[:, rows + size : rows + 2 * size]
+    z_high = z.astype(BF)
+    z_low = (z - z_high.astype(F32)).astype(BF)
+    crossed = []
+    for j in range(asked):
         take = slice(j * RANK, (j + 1) * RANK)
-        core = dot_tn(q[take], p[take], highest).astype(BF)
+        crossed.append(dot_tn(q[take], z_high[take]) + dot_tn(q[take], z_low[take]))
+    inverse = inverse_factor(split_gram(total, rows + 2 * size, size))
+    cores = in_three(dot_nt, jnp.concatenate(crossed, axis=0), inverse).astype(BF)
+    hidden = in_three(dot_nn, inverse, total[:, :rows]).astype(BF)
+    for j in range(asked):
+        core = cores[j * size : (j + 1) * size]
         mixed = dot_nn(core, hidden[:, j * each : (j + 1) * each]).astype(BF)
         out[j * each : (j + 1) * each, :] = dot_tn(mixed, basis[...]).astype(BF)
 
@@ -359,24 +395,22 @@
                 numer,
             )
     pick_rows = jnp.repeat(every_id[0, : ways * blocks] - position * fisher.shape[0], RANK)[:, None]
-    asked = blocks * RANK
+    core = jnp.full((1,), lax.axis_index("feature") % CORES, jnp.int32)
+    packed = blocks * RANK * 3 // 4
     picked, hidden, gram = call(
         pick_body,
-        [shape((ways, asked, 2 * size), BF), shape((size, rows), F32), shape((size, size), F32)],
+        [shape((ways, packed, 2 * size), BF), shape((size, rows), F32), shape((size, size), F32)],
+        core,
         reduced(tiles),
         down,
         prompt_rows,
         q,
         pick_rows,
     )
-    value, own = call(
-        join_body,
-        [shape((size, rows + 2 * size), F32), shape((asked, 2 * size), F32)],
-        swap(picked),
-        hidden,
-        gram,
-    )
-    return call(serve_body, shape((rows, width), BF), *over_feature(value, size), own, basis)
+    value = call(
+        join_body, shape((size, rows + 3 * size), F32), core, swap(picked), hidden, gram
+    )
+    return call(serve_body, shape((rows, width), BF), *over_feature(value, size), basis)
 
 
 def solution(mesh):

time: 305 us -> 302 us (level)
    pallas_call x28, Pallas kernels: 30 us -> 27 us  [call(): pl.pallas_call(body, out_shape=outs, in_specs=[scalar if arg.shape == (1,...]
where the time goes in v1:
time: 302 us; the launch traced here: 297 us
  blocking collectives  141 us (47%)
  starting transfers between devices  71.1 us (24%)
  waiting for transfers between devices  53.6 us (18%)
  Pallas kernels  27 us (9%)
    all_to_all x11, blocking collectives, swap(): return lax.all_to_all(parts, 'adapter', 0, 0, tiled=True)  141 us
    ppermute x7, starting transfers between devices, other_core(): return lax.ppermute(value, 'feature', [(i, i ^ 1) for i in range(size)])  32.2 us
    ppermute x21, waiting for transfers between devices, around_y(): lax.ppermute(value, 'feature', [(i, (i + d * CORES) % size) for i in rang...  29.1 us
    pallas_call x28, Pallas kernels, call(): pl.pallas_call(body, out_shape=outs, in_specs=[scalar if arg.shape == (1,...  27 us
    ppermute x21, starting transfers between devices, around_y(): lax.ppermute(value, 'feature', [(i, (i + d * CORES) % size) for i in rang...  23.9 us
    all_to_all x2, waiting for transfers between devices, swap(): return lax.all_to_all(parts, 'adapter', 0, 0, tiled=True)  17.7 us
    all_to_all x2, starting transfers between devices, swap(): return lax.all_to_all(parts, 'adapter', 0, 0, tiled=True)  15 us
    ppermute x7, waiting for transfers between devices, other_core(): return lax.ppermute(value, 'feature', [(i, i ^ 1) for i in range(size)])  6.78 us
  transfers between devices with their start and end apart: 30, of which 24 were waited for; matrix products, arithmetic and copies ran while one was open for 0% of the time, Pallas kernels for 0%

profile of v1, /device:TPU:1, one launch (start us, length us, event | category | flops | bytes accessed | tf_op | source)
XLA Modules:
  0.0 297.4 jit_solution(13737178183287701656)
XLA Ops:
  2.7 3.3 %collective-permute-start = (f32[64,512]{1,0:T(8,128)S(1)}, f32[64,512]{1,0:T(8,128)S(1)}, u32[]{:S(2)}, u32[]{:S(2)}) collective-permute-start(f32[64,512]{1,0:T(8,128)S(1)} %shard_map.73.own), channel_id=1, source_target_pairs={{0,1},{1,0},{2,3},{3,2},{4,5},{5,4},{6,7},{7,6},{8,9},{9,8},{10,11... | collective-permute-start | bytes 393224 | tf_op jit(solution)/shard_map/ppermute | solution.py:321
  7.0 1.3 collective-permute-start.3
  10.6 1.2 collective-permute-done.3.d
  12.2 1.2 collective-permute-done.1.b
  13.4 1.4 shard_map.75
  14.8 11.2 %all-to-all-start = ((bf16[32,16,128]{2,1,0:T(8,128)(2,1)}), bf16[32,16,128]{2,1,0:T(8,128)(2,1)S(1)}, u32[]{:S(2)}, u32[]{:S(2)}) async-start(bf16[32,16,128]{2,1,0:T(8,128)(2,1)} %get-tuple-element.23), calls=%async_computation | async-start | bytes 262144 | tf_op jit(solution)/shard_map/all_to_all | solution.py:348
  26.4 9.0 %all-to-all-done.parts = bf16[32,16,128]{2,1,0:T(8,128)(2,1)S(1)} async-done(((bf16[32,16,128]{2,1,0:T(8,128)(2,1)}), bf16[32,16,128]{2,1,0:T(8,128)(2,1)S(1)}, u32[]{:S(2)}, u32[]{:S(2)}) %all-to-all-start) | async-done | bytes 131104 | tf_op jit(solution)/shard_map/all_to_all | solution.py:348
  35.4 13.7 %all_to_all.65.tiles = bf16[32,32,128]{2,1,0:T(8,128)(2,1)S(1)} all-to-all(bf16[32,32,128]{2,1,0:T(8,128)(2,1)S(1)} %shard_map.76), channel_id=1, replica_groups=mesh['adapter'=32,'feature'=8] {'adapter'}, dimensions={0} | all-to-all | bytes 524288 | tf_op jit(solution)/shard_map/all_to_all | solution.py:348
  49.5 4.6 %collective-permute-start.4 = (f32[64,320]{1,0:T(8,128)S(1)}, f32[64,320]{1,0:T(8,128)S(1)}, u32[]{:S(2)}, u32[]{:S(2)}) collective-permute-start(f32[64,320]{1,0:T(8,128)S(1)} %get-tuple-element.24.own), channel_id=1, source_target_pairs={{0,1},{1,0},{2,3},{3,2},{4,5},{5,4},{6,7},{7,6},{8,9},{9,8},{10,11... | collective-permute-start | bytes 245768 | tf_op jit(solution)/shard_map/ppermute | solution.py:321
  55.6 1.5 collective-permute-start.6
  57.1 2.5 collective-permute-done.7.d
  59.6 1.6 collective-permute-done.5.b
  61.2 3.1 %shard_map.79 = (bf16[32,16,128]{2,1,0:T(8,128)(2,1)S(1)}, f32[64,256]{1,0:T(8,128)S(1)}) custom-call(bf16[64,384]{1,0:T(8,128)(2,1)S(1)} %shard_map.78.a, bf16[64,384]{1,0:T(8,128)(2,1)S(1)} %collective-permute-done.5.b, bf16[64,384]{1,0:T(8,128)(2,1)S(1)} %collective-permute-done.6.c, bf16[64,384]{1,0:T(8,128)(2,1)S(1)} %collective-permute-done.7.d, ...), custom_call_target="tpu_custom_call" | custom-call | tf_op jit(solution)/shard_map/pallas_call | solution.py:19
  64.4 12.7 %all_to_all.66.parts = bf16[32,16,128]{2,1,0:T(8,128)(2,1)S(1)} all-to-all(bf16[32,16,128]{2,1,0:T(8,128)(2,1)S(1)} %get-tuple-element.26), channel_id=1, replica_groups=mesh['adapter'=32,'feature'=8] {'adapter'}, dimensions={0} | all-to-all | bytes 262144 | tf_op jit(solution)/shard_map/all_to_all | solution.py:348
  77.1 12.6 %all_to_all.67.tiles = bf16[32,16,128]{2,1,0:T(8,128)(2,1)S(1)} all-to-all(bf16[32,16,128]{2,1,0:T(8,128)(2,1)S(1)} %shard_map.80), channel_id=1, replica_groups=mesh['adapter'=32,'feature'=8] {'adapter'}, dimensions={0} | all-to-all | bytes 262144 | tf_op jit(solution)/shard_map/all_to_all | solution.py:348
  90.1 4.7 %collective-permute-start.8 = (f32[64,320]{1,0:T(8,128)S(1)}, f32[64,320]{1,0:T(8,128)S(1)}, u32[]{:S(2)}, u32[]{:S(2)}) collective-permute-start(f32[64,320]{1,0:T(8,128)S(1)} %shard_map.81.own), channel_id=1, source_target_pairs={{0,1},{1,0},{2,3},{3,2},{4,5},{5,4},{6,7},{7,6},{8,9},{9,8},{10,11... | collective-permute-start | bytes 245768 | tf_op jit(solution)/shard_map/ppermute | solution.py:321
  97.7 2.6 collective-permute-done.11.d
  100.3 1.3 collective-permute-done.9.b
  101.7 3.1 %shard_map.83 = (bf16[32,16,128]{2,1,0:T(8,128)(2,1)S(1)}, f32[64,256]{1,0:T(8,128)S(1)}) custom-call(bf16[64,384]{1,0:T(8,128)(2,1)S(1)} %shard_map.82.a, bf16[64,384]{1,0:T(8,128)(2,1)S(1)} %collective-permute-done.9.b, bf16[64,384]{1,0:T(8,128)(2,1)S(1)} %collective-permute-done.10.c, bf16[64,384]{1,0:T(8,128)(2,1)S(1)} %collective-permute-done.11.d, ...), custom_call_target="tpu_custom_call" | custom-call | tf_op jit(solution)/shard_map/pallas_call | solution.py:19
  104.8 12.4 %all_to_all.68.parts = bf16[32,16,128]{2,1,0:T(8,128)(2,1)S(1)} all-to-all(bf16[32,16,128]{2,1,0:T(8,128)(2,1)S(1)} %get-tuple-element.28), channel_id=1, replica_groups=mesh['adapter'=32,'feature'=8] {'adapter'}, dimensions={0} | all-to-all | bytes 262144 | tf_op jit(solution)/shard_map/all_to_all | solution.py:348
  117.2 12.6 %all_to_all.69.tiles = bf16[32,16,128]{2,1,0:T(8,128)(2,1)S(1)} all-to-all(bf16[32,16,128]{2,1,0:T(8,128)(2,1)S(1)} %shard_map.84), channel_id=1, replica_groups=mesh['adapter'=32,'feature'=8] {'adapter'}, dimensions={0} | all-to-all | bytes 262144 | tf_op jit(solution)/shard_map/all_to_all | solution.py:348
  130.2 4.4 %collective-permute-start.12 = (f32[64,320]{1,0:T(8,128)S(1)}, f32[64,320]{1,0:T(8,128)S(1)}, u32[]{:S(2)}, u32[]{:S(2)}) collective-permute-start(f32[64,320]{1,0:T(8,128)S(1)} %shard_map.85.own), channel_id=1, source_target_pairs={{0,1},{1,0},{2,3},{3,2},{4,5},{5,4},{6,7},{7,6},{8,9},{9,8},{10,11... | collective-permute-start | bytes 245768 | tf_op jit(solution)/shard_map/ppermute | solution.py:321
  136.0 1.2 collective-permute-start.14
  137.5 2.5 collective-permute-done.15.d
  140.1 1.3 collective-permute-done.13.b
  141.4 3.1 %shard_map.87 = (bf16[32,16,128]{2,1,0:T(8,128)(2,1)S(1)}, f32[64,256]{1,0:T(8,128)S(1)}) custom-call(bf16[64,384]{1,0:T(8,128)(2,1)S(1)} %shard_map.86.a, bf16[64,384]{1,0:T(8,128)(2,1)S(1)} %collective-permute-done.13.b, bf16[64,384]{1,0:T(8,128)(2,1)S(1)} %collective-permute-done.14.c, bf16[64,384]{1,0:T(8,128)(2,1)S(1)} %collective-permute-done.15.d, ...), custom_call_target="tpu_custom_call" | custom-call | tf_op jit(solution)/shard_map/pallas_call | solution.py:19
  144.5 12.4 %all_to_all.70.parts = bf16[32,16,128]{2,1,0:T(8,128)(2,1)S(1)} all-to-all(bf16[32,16,128]{2,1,0:T(8,128)(2,1)S(1)} %get-tuple-element.30), channel_id=1, replica_groups=mesh['adapter'=32,'feature'=8] {'adapter'}, dimensions={0} | all-to-all | bytes 262144 | tf_op jit(solution)/shard_map/all_to_all | solution.py:348
  157.0 12.6 %all_to_all.71.tiles = bf16[32,16,128]{2,1,0:T(8,128)(2,1)S(1)} all-to-all(bf16[32,16,128]{2,1,0:T(8,128)(2,1)S(1)} %shard_map.88), channel_id=1, replica_groups=mesh['adapter'=32,'feature'=8] {'adapter'}, dimensions={0} | all-to-all | bytes 262144 | tf_op jit(solution)/shard_map/all_to_all | solution.py:348
  170.0 4.3 %collective-permute-start.16 = (f32[64,320]{1,0:T(8,128)S(1)}, f32[64,320]{1,0:T(8,128)S(1)}, u32[]{:S(2)}, u32[]{:S(2)}) collective-permute-start(f32[64,320]{1,0:T(8,128)S(1)} %shard_map.89.own), channel_id=1, source_target_pairs={{0,1},{1,0},{2,3},{3,2},{4,5},{5,4},{6,7},{7,6},{8,9},{9,8},{10,11... | collective-permute-start | bytes 245768 | tf_op jit(solution)/shard_map/ppermute | solution.py:321
  177.2 10.4 %collective-permute-start.17 = (bf16[64,384]{1,0:T(8,128)(2,1)S(1)}, bf16[64,384]{1,0:T(8,128)(2,1)S(1)}, u32[]{:S(2)}, u32[]{:S(2)}) collective-permute-start(bf16[64,384]{1,0:T(8,128)(2,1)S(1)} %shard_map.90.a), channel_id=1, source_target_pairs={{0,2},{1,3},{2,4},{3,5},{4,6},{5,7},{6,0},{7,1},{8,10},{9,11},{10,... | collective-permute-start | bytes 147464 | tf_op jit(solution)/shard_map/ppermute | solution.py:316
  187.6 3.7 %collective-permute-done.17.b = bf16[64,384]{1,0:T(8,128)(2,1)S(1)} collective-permute-done((bf16[64,384]{1,0:T(8,128)(2,1)S(1)}, bf16[64,384]{1,0:T(8,128)(2,1)S(1)}, u32[]{:S(2)}, u32[]{:S(2)}) %collective-permute-start.17) | collective-permute-done | bytes 49184 | tf_op jit(solution)/shard_map/ppermute | solution.py:316
  191.3 3.1 %shard_map.91 = (bf16[32,16,128]{2,1,0:T(8,128)(2,1)S(1)}, f32[64,256]{1,0:T(8,128)S(1)}) custom-call(bf16[64,384]{1,0:T(8,128)(2,1)S(1)} %shard_map.90.a, bf16[64,384]{1,0:T(8,128)(2,1)S(1)} %collective-permute-done.17.b, bf16[64,384]{1,0:T(8,128)(2,1)S(1)} %collective-permute-done.18.c, bf16[64,384]{1,0:T(8,128)(2,1)S(1)} %collective-permute-done.19.d, ...), custom_call_target="tpu_custom_call" | custom-call | tf_op jit(solution)/shard_map/pallas_call | solution.py:19
  194.4 12.4 %all_to_all.72.parts = bf16[32,16,128]{2,1,0:T(8,128)(2,1)S(1)} all-to-all(bf16[32,16,128]{2,1,0:T(8,128)(2,1)S(1)} %get-tuple-element.32), channel_id=1, replica_groups=mesh['adapter'=32,'feature'=8] {'adapter'}, dimensions={0} | all-to-all | bytes 262144 | tf_op jit(solution)/shard_map/all_to_all | solution.py:348
  206.8 12.6 %all_to_all.73.tiles.numer_tiles = bf16[32,16,128]{2,1,0:T(8,128)(2,1)S(1)} all-to-all(bf16[32,16,128]{2,1,0:T(8,128)(2,1)S(1)} %shard_map.92), channel_id=1, replica_groups=mesh['adapter'=32,'feature'=8] {'adapter'}, dimensions={0} | all-to-all | bytes 262144 | tf_op jit(solution)/shard_map/all_to_all | solution.py:348
  219.8 4.7 %collective-permute-start.20 = (f32[64,320]{1,0:T(8,128)S(1)}, f32[64,320]{1,0:T(8,128)S(1)}, u32[]{:S(2)}, u32[]{:S(2)}) collective-permute-start(f32[64,320]{1,0:T(8,128)S(1)} %shard_map.93.own), channel_id=1, source_target_pairs={{0,1},{1,0},{2,3},{3,2},{4,5},{5,4},{6,7},{7,6},{8,9},{9,8},{10,11... | collective-permute-start | bytes 245768 | tf_op jit(solution)/shard_map/ppermute | solution.py:321
  225.7 1.6 collective-permute-start.22
  227.2 2.8 collective-permute-done.23.d
  230.0 1.4 collective-permute-done.21.b
  231.4 3.2 %shard_map.95 = (bf16[32,16,128]{2,1,0:T(8,128)(2,1)S(1)}, f32[64,256]{1,0:T(8,128)S(1)}, bf16[64,1024]{1,0:T(8,128)(2,1)S(1)}) custom-call(bf16[64,384]{1,0:T(8,128)(2,1)S(1)} %shard_map.94.a, bf16[64,384]{1,0:T(8,128)(2,1)S(1)} %collective-permute-done.21.b, bf16[64,384]{1,0:T(8,128)(2,1)S(1)} %collective-permute-done.22.c, ...), custom_call_target="tpu_custom_call" | custom-call | tf_op jit(solution)/shard_map/pallas_call | solution.py:19
  234.6 12.5 %all_to_all.74.parts = bf16[32,16,128]{2,1,0:T(8,128)(2,1)S(1)} all-to-all(bf16[32,16,128]{2,1,0:T(8,128)(2,1)S(1)} %get-tuple-element.34), channel_id=1, replica_groups=mesh['adapter'=32,'feature'=8] {'adapter'}, dimensions={0} | all-to-all | bytes 262144 | tf_op jit(solution)/shard_map/all_to_all | solution.py:348
  247.8 3.9 %all-to-all-start.11 = ((bf16[32,16,128]{2,1,0:T(8,128)(2,1)}), bf16[32,16,128]{2,1,0:T(8,128)(2,1)S(1)}, u32[]{:S(2)}, u32[]{:S(2)}) async-start(bf16[32,16,128]{2,1,0:T(8,128)(2,1)} %shard_map.96), calls=%async_computation.11 | async-start | bytes 262144 | tf_op jit(solution)/shard_map/all_to_all | solution.py:348
  252.3 8.7 %all-to-all-done.11.tiles = bf16[32,16,128]{2,1,0:T(8,128)(2,1)S(1)} async-done(((bf16[32,16,128]{2,1,0:T(8,128)(2,1)}), bf16[32,16,128]{2,1,0:T(8,128)(2,1)S(1)}, u32[]{:S(2)}, u32[]{:S(2)}) %all-to-all-start.11) | async-done | bytes 131104 | tf_op jit(solution)/shard_map/all_to_all | solution.py:348
  261.1 1.5 shard_map.97
  262.6 14.6 %all_to_all.75.parts = bf16[32,48,128]{2,1,0:T(8,128)(2,1)S(1)} all-to-all(bf16[32,48,128]{2,1,0:T(8,128)(2,1)S(1)} %get-tuple-element.37), channel_id=1, replica_groups=mesh['adapter'=32,'feature'=8] {'adapter'}, dimensions={0} | all-to-all | bytes 786432 | tf_op jit(solution)/shard_map/all_to_all | solution.py:348
  277.4 6.1 %collective-permute-start.24 = (f32[64,704]{1,0:T(8,128)S(1)}, f32[64,704]{1,0:T(8,128)S(1)}, u32[]{:S(2)}, u32[]{:S(2)}) collective-permute-start(f32[64,704]{1,0:T(8,128)S(1)} %shard_map.98.own), channel_id=1, source_target_pairs={{0,1},{1,0},{2,3},{3,2},{4,5},{5,4},{6,7},{7,6},{8,9},{9,8},{10,11... | collective-permute-start | bytes 540680 | tf_op jit(solution)/shard_map/ppermute | solution.py:321
  286.2 4.0 %collective-permute-done.27.d = bf16[64,768]{1,0:T(8,128)(2,1)S(1)} collective-permute-done((bf16[64,768]{1,0:T(8,128)(2,1)S(1)}, bf16[64,768]{1,0:T(8,128)(2,1)S(1)}, u32[]{:S(2)}, u32[]{:S(2)}) %collective-permute-start.27) | collective-permute-done | bytes 98336 | tf_op jit(solution)/shard_map/ppermute | solution.py:316
  290.3 2.4 collective-permute-done.25.b
  292.6 4.5 %shard_map.100 = bf16[512,1024]{1,0:T(8,128)(2,1)} custom-call(bf16[64,768]{1,0:T(8,128)(2,1)S(1)} %shard_map.99.a, bf16[64,768]{1,0:T(8,128)(2,1)S(1)} %collective-permute-done.25.b, bf16[64,768]{1,0:T(8,128)(2,1)S(1)} %collective-permute-done.26.c, bf16[64,768]{1,0:T(8,128)(2,1)S(1)} %collective-permute-done.27.d, bf16[64,1024]{1,0:T(8,128)(2,1)S(1)} %get-tuple-element.40.basis), custom_call_target="tpu_custom_call" | custom-call | tf_op jit(solution)/shard_map/pallas_call | solution.py:19
  (73 shorter events, 23.1 us)
Async XLA Ops:
  0.0 1.2 copy-start
  1.2 1.0 copy-start.1
  2.7 4.3 %collective-permute-start = (f32[64,512]{1,0:T(8,128)S(1)}, f32[64,512]{1,0:T(8,128)S(1)}, u32[]{:S(2)}, u32[]{:S(2)}) collective-permute-start(f32[64,512]{1,0:T(8,128)S(1)} %shard_map.73.own), channel_id=1, source_target_pairs={{0,1},{1,0},{2,3},{3,2},{4,5},{5,4},{6,7},{7,6},{8,9},{9,8},{10,11... | collective-permute-start | bytes 393224 | tf_op jit(solution)/shard_map/ppermute | solution.py:321
  7.0 4.7 %collective-permute-start.3 = (bf16[64,512]{1,0:T(8,128)(2,1)S(1)}, bf16[64,512]{1,0:T(8,128)(2,1)S(1)}, u32[]{:S(2)}, u32[]{:S(2)}) collective-permute-start(bf16[64,512]{1,0:T(8,128)(2,1)S(1)} %shard_map.74.a), channel_id=1, source_target_pairs={{0,4},{1,5},{2,6},{3,7},{4,0},{5,1},{6,2},{7,3},{8,12},{9,13},{10,... | collective-permute-start | bytes 196616 | tf_op jit(solution)/shard_map/ppermute | solution.py:316
  8.3 3.9 %collective-permute-start.2 = (bf16[64,512]{1,0:T(8,128)(2,1)S(1)}, bf16[64,512]{1,0:T(8,128)(2,1)S(1)}, u32[]{:S(2)}, u32[]{:S(2)}) collective-permute-start(bf16[64,512]{1,0:T(8,128)(2,1)S(1)} %shard_map.74.a), channel_id=1, source_target_pairs={{0,6},{1,7},{2,0},{3,1},{4,2},{5,3},{6,4},{7,5},{8,14},{9,15},{10,... | collective-permute-start | bytes 196616 | tf_op jit(solution)/shard_map/ppermute | solution.py:316
  9.1 4.3 %collective-permute-start.1 = (bf16[64,512]{1,0:T(8,128)(2,1)S(1)}, bf16[64,512]{1,0:T(8,128)(2,1)S(1)}, u32[]{:S(2)}, u32[]{:S(2)}) collective-permute-start(bf16[64,512]{1,0:T(8,128)(2,1)S(1)} %shard_map.74.a), channel_id=1, source_target_pairs={{0,2},{1,3},{2,4},{3,5},{4,6},{5,7},{6,0},{7,1},{8,10},{9,11},{10,... | collective-permute-start | bytes 196616 | tf_op jit(solution)/shard_map/ppermute | solution.py:316
  9.7 0.7 copy-start.4
  14.8 11.2 %copy-start.5 = (s32[4]{0:T(128)S(1)}, s32[4]{0:T(128)}, u32[]{:S(2)}) copy-start(s32[4]{0:T(128)} %param.13) | copy-start | bytes 52
  14.8 20.5 %all-to-all-start = ((bf16[32,16,128]{2,1,0:T(8,128)(2,1)}), bf16[32,16,128]{2,1,0:T(8,128)(2,1)S(1)}, u32[]{:S(2)}, u32[]{:S(2)}) async-start(bf16[32,16,128]{2,1,0:T(8,128)(2,1)} %get-tuple-element.23), calls=%async_computation | async-start | bytes 262144 | tf_op jit(solution)/shard_map/all_to_all | solution.py:348
  49.1 12.1 %copy-start.2 = (bf16[16,16,1024]{2,1,0:T(8,128)(2,1)S(1)}, bf16[16,16,1024]{2,1,0:T(8,128)(2,1)}, u32[]{:S(2)}) copy-start(bf16[16,16,1024]{2,1,0:T(8,128)(2,1)} %param.7) | copy-start | bytes 1572868
  49.5 5.6 %collective-permute-start.4 = (f32[64,320]{1,0:T(8,128)S(1)}, f32[64,320]{1,0:T(8,128)S(1)}, u32[]{:S(2)}, u32[]{:S(2)}) collective-permute-start(f32[64,320]{1,0:T(8,128)S(1)} %get-tuple-element.24.own), channel_id=1, source_target_pairs={{0,1},{1,0},{2,3},{3,2},{4,5},{5,4},{6,7},{7,6},{8,9},{9,8},{10,11... | collective-permute-start | bytes 245768 | tf_op jit(solution)/shard_map/ppermute | solution.py:321
  55.1 4.5 %collective-permute-start.7 = (bf16[64,384]{1,0:T(8,128)(2,1)S(1)}, bf16[64,384]{1,0:T(8,128)(2,1)S(1)}, u32[]{:S(2)}, u32[]{:S(2)}) collective-permute-start(bf16[64,384]{1,0:T(8,128)(2,1)S(1)} %shard_map.78.a), channel_id=1, source_target_pairs={{0,4},{1,5},{2,6},{3,7},{4,0},{5,1},{6,2},{7,3},{8,12},{9,13},{10,... | collective-permute-start | bytes 147464 | tf_op jit(solution)/shard_map/ppermute | solution.py:316
  55.6 4.0 %collective-permute-start.6 = (bf16[64,384]{1,0:T(8,128)(2,1)S(1)}, bf16[64,384]{1,0:T(8,128)(2,1)S(1)}, u32[]{:S(2)}, u32[]{:S(2)}) collective-permute-start(bf16[64,384]{1,0:T(8,128)(2,1)S(1)} %shard_map.78.a), channel_id=1, source_target_pairs={{0,6},{1,7},{2,0},{3,1},{4,2},{5,3},{6,4},{7,5},{8,14},{9,15},{10,... | collective-permute-start | bytes 147464 | tf_op jit(solution)/shard_map/ppermute | solution.py:316
  57.1 4.2 %collective-permute-start.5 = (bf16[64,384]{1,0:T(8,128)(2,1)S(1)}, bf16[64,384]{1,0:T(8,128)(2,1)S(1)}, u32[]{:S(2)}, u32[]{:S(2)}) collective-permute-start(bf16[64,384]{1,0:T(8,128)(2,1)S(1)} %shard_map.78.a), channel_id=1, source_target_pairs={{0,2},{1,3},{2,4},{3,5},{4,6},{5,7},{6,0},{7,1},{8,10},{9,11},{10,... | collective-permute-start | bytes 147464 | tf_op jit(solution)/shard_map/ppermute | solution.py:316
  90.1 5.7 %collective-permute-start.8 = (f32[64,320]{1,0:T(8,128)S(1)}, f32[64,320]{1,0:T(8,128)S(1)}, u32[]{:S(2)}, u32[]{:S(2)}) collective-permute-start(f32[64,320]{1,0:T(8,128)S(1)} %shard_map.81.own), channel_id=1, source_target_pairs={{0,1},{1,0},{2,3},{3,2},{4,5},{5,4},{6,7},{7,6},{8,9},{9,8},{10,11... | collective-permute-start | bytes 245768 | tf_op jit(solution)/shard_map/ppermute | solution.py:321
  95.8 4.5 %collective-permute-start.11 = (bf16[64,384]{1,0:T(8,128)(2,1)S(1)}, bf16[64,384]{1,0:T(8,128)(2,1)S(1)}, u32[]{:S(2)}, u32[]{:S(2)}) collective-permute-start(bf16[64,384]{1,0:T(8,128)(2,1)S(1)} %shard_map.82.a), channel_id=1, source_target_pairs={{0,4},{1,5},{2,6},{3,7},{4,0},{5,1},{6,2},{7,3},{8,12},{9,13},{10,... | collective-permute-start | bytes 147464 | tf_op jit(solution)/shard_map/ppermute | solution.py:316
  95.9 4.4 %collective-permute-start.10 = (bf16[64,384]{1,0:T(8,128)(2,1)S(1)}, bf16[64,384]{1,0:T(8,128)(2,1)S(1)}, u32[]{:S(2)}, u32[]{:S(2)}) collective-permute-start(bf16[64,384]{1,0:T(8,128)(2,1)S(1)} %shard_map.82.a), channel_id=1, source_target_pairs={{0,6},{1,7},{2,0},{3,1},{4,2},{5,3},{6,4},{7,5},{8,14},{9,15},{10,... | collective-permute-start | bytes 147464 | tf_op jit(solution)/shard_map/ppermute | solution.py:316
  97.0 4.7 %collective-permute-start.9 = (bf16[64,384]{1,0:T(8,128)(2,1)S(1)}, bf16[64,384]{1,0:T(8,128)(2,1)S(1)}, u32[]{:S(2)}, u32[]{:S(2)}) collective-permute-start(bf16[64,384]{1,0:T(8,128)(2,1)S(1)} %shard_map.82.a), channel_id=1, source_target_pairs={{0,2},{1,3},{2,4},{3,5},{4,6},{5,7},{6,0},{7,1},{8,10},{9,11},{10,... | collective-permute-start | bytes 147464 | tf_op jit(solution)/shard_map/ppermute | solution.py:316
  130.2 5.3 %collective-permute-start.12 = (f32[64,320]{1,0:T(8,128)S(1)}, f32[64,320]{1,0:T(8,128)S(1)}, u32[]{:S(2)}, u32[]{:S(2)}) collective-permute-start(f32[64,320]{1,0:T(8,128)S(1)} %shard_map.85.own), channel_id=1, source_target_pairs={{0,1},{1,0},{2,3},{3,2},{4,5},{5,4},{6,7},{7,6},{8,9},{9,8},{10,11... | collective-permute-start | bytes 245768 | tf_op jit(solution)/shard_map/ppermute | solution.py:321
  135.6 4.5 %collective-permute-start.15 = (bf16[64,384]{1,0:T(8,128)(2,1)S(1)}, bf16[64,384]{1,0:T(8,128)(2,1)S(1)}, u32[]{:S(2)}, u32[]{:S(2)}) collective-permute-start(bf16[64,384]{1,0:T(8,128)(2,1)S(1)} %shard_map.86.a), channel_id=1, source_target_pairs={{0,4},{1,5},{2,6},{3,7},{4,0},{5,1},{6,2},{7,3},{8,12},{9,13},{10,... | collective-permute-start | bytes 147464 | tf_op jit(solution)/shard_map/ppermute | solution.py:316
  136.0 4.0 %collective-permute-start.14 = (bf16[64,384]{1,0:T(8,128)(2,1)S(1)}, bf16[64,384]{1,0:T(8,128)(2,1)S(1)}, u32[]{:S(2)}, u32[]{:S(2)}) collective-permute-start(bf16[64,384]{1,0:T(8,128)(2,1)S(1)} %shard_map.86.a), channel_id=1, source_target_pairs={{0,6},{1,7},{2,0},{3,1},{4,2},{5,3},{6,4},{7,5},{8,14},{9,15},{10,... | collective-permute-start | bytes 147464 | tf_op jit(solution)/shard_map/ppermute | solution.py:316
  137.2 4.2 %collective-permute-start.13 = (bf16[64,384]{1,0:T(8,128)(2,1)S(1)}, bf16[64,384]{1,0:T(8,128)(2,1)S(1)}, u32[]{:S(2)}, u32[]{:S(2)}) collective-permute-start(bf16[64,384]{1,0:T(8,128)(2,1)S(1)} %shard_map.86.a), channel_id=1, source_target_pairs={{0,2},{1,3},{2,4},{3,5},{4,6},{5,7},{6,0},{7,1},{8,10},{9,11},{10,... | collective-permute-start | bytes 147464 | tf_op jit(solution)/shard_map/ppermute | solution.py:316
  170.0 5.3 %collective-permute-start.16 = (f32[64,320]{1,0:T(8,128)S(1)}, f32[64,320]{1,0:T(8,128)S(1)}, u32[]{:S(2)}, u32[]{:S(2)}) collective-permute-start(f32[64,320]{1,0:T(8,128)S(1)} %shard_map.89.own), channel_id=1, source_target_pairs={{0,1},{1,0},{2,3},{3,2},{4,5},{5,4},{6,7},{7,6},{8,9},{9,8},{10,11... | collective-permute-start | bytes 245768 | tf_op jit(solution)/shard_map/ppermute | solution.py:321
  175.4 12.2 %collective-permute-start.19 = (bf16[64,384]{1,0:T(8,128)(2,1)S(1)}, bf16[64,384]{1,0:T(8,128)(2,1)S(1)}, u32[]{:S(2)}, u32[]{:S(2)}) collective-permute-start(bf16[64,384]{1,0:T(8,128)(2,1)S(1)} %shard_map.90.a), channel_id=1, source_target_pairs={{0,4},{1,5},{2,6},{3,7},{4,0},{5,1},{6,2},{7,3},{8,12},{9,13},{10,... | collective-permute-start | bytes 147464 | tf_op jit(solution)/shard_map/ppermute | solution.py:316
  176.2 11.4 %collective-permute-start.18 = (bf16[64,384]{1,0:T(8,128)(2,1)S(1)}, bf16[64,384]{1,0:T(8,128)(2,1)S(1)}, u32[]{:S(2)}, u32[]{:S(2)}) collective-permute-start(bf16[64,384]{1,0:T(8,128)(2,1)S(1)} %shard_map.90.a), channel_id=1, source_target_pairs={{0,6},{1,7},{2,0},{3,1},{4,2},{5,3},{6,4},{7,5},{8,14},{9,15},{10,... | collective-permute-start | bytes 147464 | tf_op jit(solution)/shard_map/ppermute | solution.py:316
  177.2 14.0 %collective-permute-start.17 = (bf16[64,384]{1,0:T(8,128)(2,1)S(1)}, bf16[64,384]{1,0:T(8,128)(2,1)S(1)}, u32[]{:S(2)}, u32[]{:S(2)}) collective-permute-start(bf16[64,384]{1,0:T(8,128)(2,1)S(1)} %shard_map.90.a), channel_id=1, source_target_pairs={{0,2},{1,3},{2,4},{3,5},{4,6},{5,7},{6,0},{7,1},{8,10},{9,11},{10,... | collective-permute-start | bytes 147464 | tf_op jit(solution)/shard_map/ppermute | solution.py:316
  219.8 5.7 %collective-permute-start.20 = (f32[64,320]{1,0:T(8,128)S(1)}, f32[64,320]{1,0:T(8,128)S(1)}, u32[]{:S(2)}, u32[]{:S(2)}) collective-permute-start(f32[64,320]{1,0:T(8,128)S(1)} %shard_map.93.own), channel_id=1, source_target_pairs={{0,1},{1,0},{2,3},{3,2},{4,5},{5,4},{6,7},{7,6},{8,9},{9,8},{10,11... | collective-permute-start | bytes 245768 | tf_op jit(solution)/shard_map/ppermute | solution.py:321
  225.5 4.5 %collective-permute-start.23 = (bf16[64,384]{1,0:T(8,128)(2,1)S(1)}, bf16[64,384]{1,0:T(8,128)(2,1)S(1)}, u32[]{:S(2)}, u32[]{:S(2)}) collective-permute-start(bf16[64,384]{1,0:T(8,128)(2,1)S(1)} %shard_map.94.a), channel_id=1, source_target_pairs={{0,4},{1,5},{2,6},{3,7},{4,0},{5,1},{6,2},{7,3},{8,12},{9,13},{10,... | collective-permute-start | bytes 147464 | tf_op jit(solution)/shard_map/ppermute | solution.py:316
  225.7 4.4 %collective-permute-start.22 = (bf16[64,384]{1,0:T(8,128)(2,1)S(1)}, bf16[64,384]{1,0:T(8,128)(2,1)S(1)}, u32[]{:S(2)}, u32[]{:S(2)}) collective-permute-start(bf16[64,384]{1,0:T(8,128)(2,1)S(1)} %shard_map.94.a), channel_id=1, source_target_pairs={{0,6},{1,7},{2,0},{3,1},{4,2},{5,3},{6,4},{7,5},{8,14},{9,15},{10,... | collective-permute-start | bytes 147464 | tf_op jit(solution)/shard_map/ppermute | solution.py:316
  227.2 4.2 %collective-permute-start.21 = (bf16[64,384]{1,0:T(8,128)(2,1)S(1)}, bf16[64,384]{1,0:T(8,128)(2,1)S(1)}, u32[]{:S(2)}, u32[]{:S(2)}) collective-permute-start(bf16[64,384]{1,0:T(8,128)(2,1)S(1)} %shard_map.94.a), channel_id=1, source_target_pairs={{0,2},{1,3},{2,4},{3,5},{4,6},{5,7},{6,0},{7,1},{8,10},{9,11},{10,... | collective-permute-start | bytes 147464 | tf_op jit(solution)/shard_map/ppermute | solution.py:316
  234.6 26.5 %copy-start.3 = (bf16[512,1024]{1,0:T(8,128)(2,1)S(1)}, bf16[512,1024]{1,0:T(8,128)(2,1)}, u32[]{:S(2)}) copy-start(bf16[512,1024]{1,0:T(8,128)(2,1)} %prompts.1) | copy-start | bytes 3145732
  247.8 13.3 %all-to-all-start.11 = ((bf16[32,16,128]{2,1,0:T(8,128)(2,1)}), bf16[32,16,128]{2,1,0:T(8,128)(2,1)S(1)}, u32[]{:S(2)}, u32[]{:S(2)}) async-start(bf16[32,16,128]{2,1,0:T(8,128)(2,1)} %shard_map.96), calls=%async_computation.11 | async-start | bytes 262144 | tf_op jit(solution)/shard_map/all_to_all | solution.py:348
  277.4 7.2 %collective-permute-start.24 = (f32[64,704]{1,0:T(8,128)S(1)}, f32[64,704]{1,0:T(8,128)S(1)}, u32[]{:S(2)}, u32[]{:S(2)}) collective-permute-start(f32[64,704]{1,0:T(8,128)S(1)} %shard_map.98.own), channel_id=1, source_target_pairs={{0,1},{1,0},{2,3},{3,2},{4,5},{5,4},{6,7},{7,6},{8,9},{9,8},{10,11... | collective-permute-start | bytes 540680 | tf_op jit(solution)/shard_map/ppermute | solution.py:321
  284.6 5.5 %collective-permute-start.27 = (bf16[64,768]{1,0:T(8,128)(2,1)S(1)}, bf16[64,768]{1,0:T(8,128)(2,1)S(1)}, u32[]{:S(2)}, u32[]{:S(2)}) collective-permute-start(bf16[64,768]{1,0:T(8,128)(2,1)S(1)} %shard_map.99.a), channel_id=1, source_target_pairs={{0,4},{1,5},{2,6},{3,7},{4,0},{5,1},{6,2},{7,3},{8,12},{9,13},{10,... | collective-permute-start | bytes 294920 | tf_op jit(solution)/shard_map/ppermute | solution.py:316
  284.7 5.6 %collective-permute-start.26 = (bf16[64,768]{1,0:T(8,128)(2,1)S(1)}, bf16[64,768]{1,0:T(8,128)(2,1)S(1)}, u32[]{:S(2)}, u32[]{:S(2)}) collective-permute-start(bf16[64,768]{1,0:T(8,128)(2,1)S(1)} %shard_map.99.a), channel_id=1, source_target_pairs={{0,6},{1,7},{2,0},{3,1},{4,2},{5,3},{6,4},{7,5},{8,14},{9,15},{10,... | collective-permute-start | bytes 294920 | tf_op jit(solution)/shard_map/ppermute | solution.py:316
  285.7 6.9 %collective-permute-start.25 = (bf16[64,768]{1,0:T(8,128)(2,1)S(1)}, bf16[64,768]{1,0:T(8,128)(2,1)S(1)}, u32[]{:S(2)}, u32[]{:S(2)}) collective-permute-start(bf16[64,768]{1,0:T(8,128)(2,1)S(1)} %shard_map.99.a), channel_id=1, source_target_pairs={{0,2},{1,3},{2,4},{3,5},{4,6},{5,7},{6,0},{7,1},{8,10},{9,11},{10,... | collective-permute-start | bytes 294920 | tf_op jit(solution)/shard_map/ppermute | solution.py:316

commit v2 on v1

--- a/solution.py
+++ b/solution.py
@@ -260,8 +260,8 @@
     r = lax.broadcasted_iota(jnp.int32, (wanted, count), 0)
     c = lax.broadcasted_iota(jnp.int32, (wanted, count), 1)
     hot = (ids[...] * RANK + (r & (RANK - 1)) == c).astype(F32).astype(BF)
-    chosen_z = dot_nn(hot, jnp.concatenate([z, z], axis=1))
-    chosen_q = dot_nn(hot, jnp.concatenate([q, q], axis=1))
+    chosen = dot_nn(hot, jnp.concatenate([z, z, q, q], axis=1))
+    chosen_z, chosen_q = chosen[:, : 2 * size], chosen[:, 2 * size :]
     each = wanted // ways
     for i in range(ways):
         at = i * each
@@ -324,7 +324,7 @@
 def over_feature(value, gram_size):
     rows, lanes = value.shape
     pair = call(pair_body, shape((rows, lanes + gram_size), BF), value, other_core(value))
-    return [pair] + [around_y(pair, d) for d in (1, 3, 2)]
+    return [pair] + [around_y(pair, d) for d in (1, 2, 3)]
 
 
 def on_device(adapter_down, adapter_up, fisher, init_v, init_u, prompt_rows, request_ids):

time: 302 us -> 303 us (level)
  transfers between devices with their start and end apart: 30 -> 30, of which waited for: 24 -> 28; matrix products, arithmetic and copies ran while one was open for 0% -> 0% of each run, Pallas kernels for 0% -> 0%
where the time goes in v2:
time: 303 us; the launch traced here: 298 us
  blocking collectives  142 us (47%)
  starting transfers between devices  69.5 us (23%)
  waiting for transfers between devices  56.2 us (19%)
  Pallas kernels  26.6 us (9%)
    all_to_all x11, blocking collectives, swap(): return lax.all_to_all(parts, 'adapter', 0, 0, tiled=True)  142 us
    ppermute x21, waiting for transfers between devices, around_y(): lax.ppermute(value, 'feature', [(i, (i + d * CORES) % size) for i in rang...  31.7 us
    ppermute x7, starting transfers between devices, other_core(): return lax.ppermute(value, 'feature', [(i, i ^ 1) for i in range(size)])  29.5 us
    pallas_call x28, Pallas kernels, call(): pl.pallas_call(body, out_shape=outs, in_specs=[scalar if arg.shape == (1,...  26.6 us
    ppermute x21, starting transfers between devices, around_y(): lax.ppermute(value, 'feature', [(i, (i + d * CORES) % size) for i in rang...  24.7 us
    all_to_all x2, waiting for transfers between devices, swap(): return lax.all_to_all(parts, 'adapter', 0, 0, tiled=True)  17.7 us
    all_to_all x2, starting transfers between devices, swap(): return lax.all_to_all(parts, 'adapter', 0, 0, tiled=True)  15.3 us
    ppermute x7, waiting for transfers between devices, other_core(): return lax.ppermute(value, 'feature', [(i, i ^ 1) for i in range(size)])  6.78 us
  transfers between devices with their start and end apart: 30, of which 28 were waited for; matrix products, arithmetic and copies ran while one was open for 0% of the time, Pallas kernels for 0%

profile of v2, /device:TPU:1, one launch (start us, length us, event | category | flops | bytes accessed | tf_op | source)
XLA Modules:
  0.0 298.4 jit_solution(337653585757181397)
XLA Ops:
  0.0 1.1 convert_bitcast_fusion
  2.7 3.3 %collective-permute-start = (f32[64,512]{1,0:T(8,128)S(1)}, f32[64,512]{1,0:T(8,128)S(1)}, u32[]{:S(2)}, u32[]{:S(2)}) collective-permute-start(f32[64,512]{1,0:T(8,128)S(1)} %shard_map.73.own), channel_id=1, source_target_pairs={{0,1},{1,0},{2,3},{3,2},{4,5},{5,4},{6,7},{7,6},{8,9},{9,8},{10,11... | collective-permute-start | bytes 393224 | tf_op jit(solution)/shard_map/ppermute | solution.py:321
  10.2 2.6 collective-permute-done.2.c
  12.8 1.4 collective-permute-done.1.b
  14.2 1.4 shard_map.75
  15.6 11.5 %all-to-all-start = ((bf16[32,16,128]{2,1,0:T(8,128)(2,1)}), bf16[32,16,128]{2,1,0:T(8,128)(2,1)S(1)}, u32[]{:S(2)}, u32[]{:S(2)}) async-start(bf16[32,16,128]{2,1,0:T(8,128)(2,1)} %get-tuple-element.23), calls=%async_computation | async-start | bytes 262144 | tf_op jit(solution)/shard_map/all_to_all | solution.py:348
  27.5 9.0 %all-to-all-done.parts = bf16[32,16,128]{2,1,0:T(8,128)(2,1)S(1)} async-done(((bf16[32,16,128]{2,1,0:T(8,128)(2,1)}), bf16[32,16,128]{2,1,0:T(8,128)(2,1)S(1)}, u32[]{:S(2)}, u32[]{:S(2)}) %all-to-all-start) | async-done | bytes 131104 | tf_op jit(solution)/shard_map/all_to_all | solution.py:348
  36.5 13.7 %all_to_all.65.tiles = bf16[32,32,128]{2,1,0:T(8,128)(2,1)S(1)} all-to-all(bf16[32,32,128]{2,1,0:T(8,128)(2,1)S(1)} %shard_map.76), channel_id=1, replica_groups=mesh['adapter'=32,'feature'=8] {'adapter'}, dimensions={0} | all-to-all | bytes 524288 | tf_op jit(solution)/shard_map/all_to_all | solution.py:348
  50.6 3.8 %collective-permute-start.4 = (f32[64,320]{1,0:T(8,128)S(1)}, f32[64,320]{1,0:T(8,128)S(1)}, u32[]{:S(2)}, u32[]{:S(2)}) collective-permute-start(f32[64,320]{1,0:T(8,128)S(1)} %get-tuple-element.24.own), channel_id=1, source_target_pairs={{0,1},{1,0},{2,3},{3,2},{4,5},{5,4},{6,7},{7,6},{8,9},{9,8},{10,11... | collective-permute-start | bytes 245768 | tf_op jit(solution)/shard_map/ppermute | solution.py:321
  57.0 1.4 collective-permute-done.7.d
  58.4 1.7 collective-permute-done.6.c
  60.1 1.4 collective-permute-done.5.b
  61.5 3.1 %shard_map.79 = (bf16[32,16,128]{2,1,0:T(8,128)(2,1)S(1)}, f32[64,256]{1,0:T(8,128)S(1)}) custom-call(bf16[64,384]{1,0:T(8,128)(2,1)S(1)} %shard_map.78.a, bf16[64,384]{1,0:T(8,128)(2,1)S(1)} %collective-permute-done.5.b, bf16[64,384]{1,0:T(8,128)(2,1)S(1)} %collective-permute-done.6.c, bf16[64,384]{1,0:T(8,128)(2,1)S(1)} %collective-permute-done.7.d, ...), custom_call_target="tpu_custom_call" | custom-call | tf_op jit(solution)/shard_map/pallas_call | solution.py:19
  64.6 12.6 %all_to_all.66.parts = bf16[32,16,128]{2,1,0:T(8,128)(2,1)S(1)} all-to-all(bf16[32,16,128]{2,1,0:T(8,128)(2,1)S(1)} %get-tuple-element.26), channel_id=1, replica_groups=mesh['adapter'=32,'feature'=8] {'adapter'}, dimensions={0} | all-to-all | bytes 262144 | tf_op jit(solution)/shard_map/all_to_all | solution.py:348
  77.3 12.5 %all_to_all.67.tiles = bf16[32,16,128]{2,1,0:T(8,128)(2,1)S(1)} all-to-all(bf16[32,16,128]{2,1,0:T(8,128)(2,1)S(1)} %shard_map.80), channel_id=1, replica_groups=mesh['adapter'=32,'feature'=8] {'adapter'}, dimensions={0} | all-to-all | bytes 262144 | tf_op jit(solution)/shard_map/all_to_all | solution.py:348
  90.2 3.8 %collective-permute-start.8 = (f32[64,320]{1,0:T(8,128)S(1)}, f32[64,320]{1,0:T(8,128)S(1)}, u32[]{:S(2)}, u32[]{:S(2)}) collective-permute-start(f32[64,320]{1,0:T(8,128)S(1)} %shard_map.81.own), channel_id=1, source_target_pairs={{0,1},{1,0},{2,3},{3,2},{4,5},{5,4},{6,7},{7,6},{8,9},{9,8},{10,11... | collective-permute-start | bytes 245768 | tf_op jit(solution)/shard_map/ppermute | solution.py:321
  95.0 1.6 collective-permute-start.11
  98.0 3.1 %collective-permute-done.10.c = bf16[64,384]{1,0:T(8,128)(2,1)S(1)} collective-permute-done((bf16[64,384]{1,0:T(8,128)(2,1)S(1)}, bf16[64,384]{1,0:T(8,128)(2,1)S(1)}, u32[]{:S(2)}, u32[]{:S(2)}) %collective-permute-start.10) | collective-permute-done | bytes 49184 | tf_op jit(solution)/shard_map/ppermute | solution.py:316
  101.7 3.1 %shard_map.83 = (bf16[32,16,128]{2,1,0:T(8,128)(2,1)S(1)}, f32[64,256]{1,0:T(8,128)S(1)}) custom-call(bf16[64,384]{1,0:T(8,128)(2,1)S(1)} %shard_map.82.a, bf16[64,384]{1,0:T(8,128)(2,1)S(1)} %collective-permute-done.9.b, bf16[64,384]{1,0:T(8,128)(2,1)S(1)} %collective-permute-done.10.c, bf16[64,384]{1,0:T(8,128)(2,1)S(1)} %collective-permute-done.11.d, ...), custom_call_target="tpu_custom_call" | custom-call | tf_op jit(solution)/shard_map/pallas_call | solution.py:19
  104.8 12.8 %all_to_all.68.parts = bf16[32,16,128]{2,1,0:T(8,128)(2,1)S(1)} all-to-all(bf16[32,16,128]{2,1,0:T(8,128)(2,1)S(1)} %get-tuple-element.28), channel_id=1, replica_groups=mesh['adapter'=32,'feature'=8] {'adapter'}, dimensions={0} | all-to-all | bytes 262144 | tf_op jit(solution)/shard_map/all_to_all | solution.py:348
  117.6 12.7 %all_to_all.69.tiles = bf16[32,16,128]{2,1,0:T(8,128)(2,1)S(1)} all-to-all(bf16[32,16,128]{2,1,0:T(8,128)(2,1)S(1)} %shard_map.84), channel_id=1, replica_groups=mesh['adapter'=32,'feature'=8] {'adapter'}, dimensions={0} | all-to-all | bytes 262144 | tf_op jit(solution)/shard_map/all_to_all | solution.py:348
  130.7 4.2 %collective-permute-start.12 = (f32[64,320]{1,0:T(8,128)S(1)}, f32[64,320]{1,0:T(8,128)S(1)}, u32[]{:S(2)}, u32[]{:S(2)}) collective-permute-start(f32[64,320]{1,0:T(8,128)S(1)} %shard_map.85.own), channel_id=1, source_target_pairs={{0,1},{1,0},{2,3},{3,2},{4,5},{5,4},{6,7},{7,6},{8,9},{9,8},{10,11... | collective-permute-start | bytes 245768 | tf_op jit(solution)/shard_map/ppermute | solution.py:321
  138.9 1.8 collective-permute-done.14.c
  140.8 1.4 collective-permute-done.13.b
  142.2 3.1 %shard_map.87 = (bf16[32,16,128]{2,1,0:T(8,128)(2,1)S(1)}, f32[64,256]{1,0:T(8,128)S(1)}) custom-call(bf16[64,384]{1,0:T(8,128)(2,1)S(1)} %shard_map.86.a, bf16[64,384]{1,0:T(8,128)(2,1)S(1)} %collective-permute-done.13.b, bf16[64,384]{1,0:T(8,128)(2,1)S(1)} %collective-permute-done.14.c, bf16[64,384]{1,0:T(8,128)(2,1)S(1)} %collective-permute-done.15.d, ...), custom_call_target="tpu_custom_call" | custom-call | tf_op jit(solution)/shard_map/pallas_call | solution.py:19
  145.3 12.3 %all_to_all.70.parts = bf16[32,16,128]{2,1,0:T(8,128)(2,1)S(1)} all-to-all(bf16[32,16,128]{2,1,0:T(8,128)(2,1)S(1)} %get-tuple-element.30), channel_id=1, replica_groups=mesh['adapter'=32,'feature'=8] {'adapter'}, dimensions={0} | all-to-all | bytes 262144 | tf_op jit(solution)/shard_map/all_to_all | solution.py:348
  157.7 12.7 %all_to_all.71.tiles = bf16[32,16,128]{2,1,0:T(8,128)(2,1)S(1)} all-to-all(bf16[32,16,128]{2,1,0:T(8,128)(2,1)S(1)} %shard_map.88), channel_id=1, replica_groups=mesh['adapter'=32,'feature'=8] {'adapter'}, dimensions={0} | all-to-all | bytes 262144 | tf_op jit(solution)/shard_map/all_to_all | solution.py:348
  170.7 3.8 %collective-permute-start.16 = (f32[64,320]{1,0:T(8,128)S(1)}, f32[64,320]{1,0:T(8,128)S(1)}, u32[]{:S(2)}, u32[]{:S(2)}) collective-permute-start(f32[64,320]{1,0:T(8,128)S(1)} %shard_map.89.own), channel_id=1, source_target_pairs={{0,1},{1,0},{2,3},{3,2},{4,5},{5,4},{6,7},{7,6},{8,9},{9,8},{10,11... | collective-permute-start | bytes 245768 | tf_op jit(solution)/shard_map/ppermute | solution.py:321
  175.5 1.5 collective-permute-start.19
  177.7 9.8 %collective-permute-start.17 = (bf16[64,384]{1,0:T(8,128)(2,1)S(1)}, bf16[64,384]{1,0:T(8,128)(2,1)S(1)}, u32[]{:S(2)}, u32[]{:S(2)}) collective-permute-start(bf16[64,384]{1,0:T(8,128)(2,1)S(1)} %shard_map.90.a), channel_id=1, source_target_pairs={{0,2},{1,3},{2,4},{3,5},{4,6},{5,7},{6,0},{7,1},{8,10},{9,11},{10,... | collective-permute-start | bytes 147464 | tf_op jit(solution)/shard_map/ppermute | solution.py:316
  187.5 4.1 %collective-permute-done.17.b = bf16[64,384]{1,0:T(8,128)(2,1)S(1)} collective-permute-done((bf16[64,384]{1,0:T(8,128)(2,1)S(1)}, bf16[64,384]{1,0:T(8,128)(2,1)S(1)}, u32[]{:S(2)}, u32[]{:S(2)}) %collective-permute-start.17) | collective-permute-done | bytes 49184 | tf_op jit(solution)/shard_map/ppermute | solution.py:316
  191.6 3.1 %shard_map.91 = (bf16[32,16,128]{2,1,0:T(8,128)(2,1)S(1)}, f32[64,256]{1,0:T(8,128)S(1)}) custom-call(bf16[64,384]{1,0:T(8,128)(2,1)S(1)} %shard_map.90.a, bf16[64,384]{1,0:T(8,128)(2,1)S(1)} %collective-permute-done.17.b, bf16[64,384]{1,0:T(8,128)(2,1)S(1)} %collective-permute-done.18.c, bf16[64,384]{1,0:T(8,128)(2,1)S(1)} %collective-permute-done.19.d, ...), custom_call_target="tpu_custom_call" | custom-call | tf_op jit(solution)/shard_map/pallas_call | solution.py:19
  194.7 12.4 %all_to_all.72.parts = bf16[32,16,128]{2,1,0:T(8,128)(2,1)S(1)} all-to-all(bf16[32,16,128]{2,1,0:T(8,128)(2,1)S(1)} %get-tuple-element.32), channel_id=1, replica_groups=mesh['adapter'=32,'feature'=8] {'adapter'}, dimensions={0} | all-to-all | bytes 262144 | tf_op jit(solution)/shard_map/all_to_all | solution.py:348
  207.2 12.6 %all_to_all.73.tiles.numer_tiles = bf16[32,16,128]{2,1,0:T(8,128)(2,1)S(1)} all-to-all(bf16[32,16,128]{2,1,0:T(8,128)(2,1)S(1)} %shard_map.92), channel_id=1, replica_groups=mesh['adapter'=32,'feature'=8] {'adapter'}, dimensions={0} | all-to-all | bytes 262144 | tf_op jit(solution)/shard_map/all_to_all | solution.py:348
  220.2 4.7 %collective-permute-start.20 = (f32[64,320]{1,0:T(8,128)S(1)}, f32[64,320]{1,0:T(8,128)S(1)}, u32[]{:S(2)}, u32[]{:S(2)}) collective-permute-start(f32[64,320]{1,0:T(8,128)S(1)} %shard_map.93.own), channel_id=1, source_target_pairs={{0,1},{1,0},{2,3},{3,2},{4,5},{5,4},{6,7},{7,6},{8,9},{9,8},{10,11... | collective-permute-start | bytes 245768 | tf_op jit(solution)/shard_map/ppermute | solution.py:321
  228.9 1.9 collective-permute-done.22.c
  231.4 3.2 %shard_map.95 = (bf16[32,16,128]{2,1,0:T(8,128)(2,1)S(1)}, f32[64,256]{1,0:T(8,128)S(1)}, bf16[64,1024]{1,0:T(8,128)(2,1)S(1)}) custom-call(bf16[64,384]{1,0:T(8,128)(2,1)S(1)} %shard_map.94.a, bf16[64,384]{1,0:T(8,128)(2,1)S(1)} %collective-permute-done.21.b, bf16[64,384]{1,0:T(8,128)(2,1)S(1)} %collective-permute-done.22.c, ...), custom_call_target="tpu_custom_call" | custom-call | tf_op jit(solution)/shard_map/pallas_call | solution.py:19
  234.6 12.6 %all_to_all.74.parts = bf16[32,16,128]{2,1,0:T(8,128)(2,1)S(1)} all-to-all(bf16[32,16,128]{2,1,0:T(8,128)(2,1)S(1)} %get-tuple-element.34), channel_id=1, replica_groups=mesh['adapter'=32,'feature'=8] {'adapter'}, dimensions={0} | all-to-all | bytes 262144 | tf_op jit(solution)/shard_map/all_to_all | solution.py:348
  247.9 3.9 %all-to-all-start.11 = ((bf16[32,16,128]{2,1,0:T(8,128)(2,1)}), bf16[32,16,128]{2,1,0:T(8,128)(2,1)S(1)}, u32[]{:S(2)}, u32[]{:S(2)}) async-start(bf16[32,16,128]{2,1,0:T(8,128)(2,1)} %shard_map.96), calls=%async_computation.11 | async-start | bytes 262144 | tf_op jit(solution)/shard_map/all_to_all | solution.py:348
  252.4 8.7 %all-to-all-done.11.tiles = bf16[32,16,128]{2,1,0:T(8,128)(2,1)S(1)} async-done(((bf16[32,16,128]{2,1,0:T(8,128)(2,1)}), bf16[32,16,128]{2,1,0:T(8,128)(2,1)S(1)}, u32[]{:S(2)}, u32[]{:S(2)}) %all-to-all-start.11) | async-done | bytes 131104 | tf_op jit(solution)/shard_map/all_to_all | solution.py:348
  261.1 1.1 shard_map.97
  262.3 14.7 %all_to_all.75.parts = bf16[32,48,128]{2,1,0:T(8,128)(2,1)S(1)} all-to-all(bf16[32,48,128]{2,1,0:T(8,128)(2,1)S(1)} %get-tuple-element.37), channel_id=1, replica_groups=mesh['adapter'=32,'feature'=8] {'adapter'}, dimensions={0} | all-to-all | bytes 786432 | tf_op jit(solution)/shard_map/all_to_all | solution.py:348
  277.1 5.7 %collective-permute-start.24 = (f32[64,704]{1,0:T(8,128)S(1)}, f32[64,704]{1,0:T(8,128)S(1)}, u32[]{:S(2)}, u32[]{:S(2)}) collective-permute-start(f32[64,704]{1,0:T(8,128)S(1)} %shard_map.98.own), channel_id=1, source_target_pairs={{0,1},{1,0},{2,3},{3,2},{4,5},{5,4},{6,7},{7,6},{8,9},{9,8},{10,11... | collective-permute-start | bytes 540680 | tf_op jit(solution)/shard_map/ppermute | solution.py:321
  284.0 1.7 collective-permute-start.27
  286.4 1.7 collective-permute-done.27.d
  288.1 2.7 collective-permute-done.26.c
  290.7 3.0 collective-permute-done.25.b
  293.7 4.5 %shard_map.100 = bf16[512,1024]{1,0:T(8,128)(2,1)} custom-call(bf16[64,768]{1,0:T(8,128)(2,1)S(1)} %shard_map.99.a, bf16[64,768]{1,0:T(8,128)(2,1)S(1)} %collective-permute-done.25.b, bf16[64,768]{1,0:T(8,128)(2,1)S(1)} %collective-permute-done.26.c, bf16[64,768]{1,0:T(8,128)(2,1)S(1)} %collective-permute-done.27.d, bf16[64,1024]{1,0:T(8,128)(2,1)S(1)} %get-tuple-element.40.basis), custom_call_target="tpu_custom_call" | custom-call | tf_op jit(solution)/shard_map/pallas_call | solution.py:19
  (73 shorter events, 27.0 us)
Async XLA Ops:
  0.0 1.2 copy-start
  1.2 1.0 copy-start.1
  2.7 4.3 %collective-permute-start = (f32[64,512]{1,0:T(8,128)S(1)}, f32[64,512]{1,0:T(8,128)S(1)}, u32[]{:S(2)}, u32[]{:S(2)}) collective-permute-start(f32[64,512]{1,0:T(8,128)S(1)} %shard_map.73.own), channel_id=1, source_target_pairs={{0,1},{1,0},{2,3},{3,2},{4,5},{5,4},{6,7},{7,6},{8,9},{9,8},{10,11... | collective-permute-start | bytes 393224 | tf_op jit(solution)/shard_map/ppermute | solution.py:321
  7.0 3.2 %collective-permute-start.3 = (bf16[64,512]{1,0:T(8,128)(2,1)S(1)}, bf16[64,512]{1,0:T(8,128)(2,1)S(1)}, u32[]{:S(2)}, u32[]{:S(2)}) collective-permute-start(bf16[64,512]{1,0:T(8,128)(2,1)S(1)} %shard_map.74.a), channel_id=1, source_target_pairs={{0,6},{1,7},{2,0},{3,1},{4,2},{5,3},{6,4},{7,5},{8,14},{9,15},{10,... | collective-permute-start | bytes 196616 | tf_op jit(solution)/shard_map/ppermute | solution.py:316
  8.1 4.7 %collective-permute-start.2 = (bf16[64,512]{1,0:T(8,128)(2,1)S(1)}, bf16[64,512]{1,0:T(8,128)(2,1)S(1)}, u32[]{:S(2)}, u32[]{:S(2)}) collective-permute-start(bf16[64,512]{1,0:T(8,128)(2,1)S(1)} %shard_map.74.a), channel_id=1, source_target_pairs={{0,4},{1,5},{2,6},{3,7},{4,0},{5,1},{6,2},{7,3},{8,12},{9,13},{10,... | collective-permute-start | bytes 196616 | tf_op jit(solution)/shard_map/ppermute | solution.py:316
  8.4 5.7 %collective-permute-start.1 = (bf16[64,512]{1,0:T(8,128)(2,1)S(1)}, bf16[64,512]{1,0:T(8,128)(2,1)S(1)}, u32[]{:S(2)}, u32[]{:S(2)}) collective-permute-start(bf16[64,512]{1,0:T(8,128)(2,1)S(1)} %shard_map.74.a), channel_id=1, source_target_pairs={{0,2},{1,3},{2,4},{3,5},{4,6},{5,7},{6,0},{7,1},{8,10},{9,11},{10,... | collective-permute-start | bytes 196616 | tf_op jit(solution)/shard_map/ppermute | solution.py:316
  9.1 0.7 copy-start.4
  15.6 11.5 %copy-start.5 = (s32[4]{0:T(128)S(1)}, s32[4]{0:T(128)}, u32[]{:S(2)}) copy-start(s32[4]{0:T(128)} %param.13) | copy-start | bytes 52
  15.6 20.8 %all-to-all-start = ((bf16[32,16,128]{2,1,0:T(8,128)(2,1)}), bf16[32,16,128]{2,1,0:T(8,128)(2,1)S(1)}, u32[]{:S(2)}, u32[]{:S(2)}) async-start(bf16[32,16,128]{2,1,0:T(8,128)(2,1)} %get-tuple-element.23), calls=%async_computation | async-start | bytes 262144 | tf_op jit(solution)/shard_map/all_to_all | solution.py:348
  50.2 11.2 %copy-start.2 = (bf16[16,16,1024]{2,1,0:T(8,128)(2,1)S(1)}, bf16[16,16,1024]{2,1,0:T(8,128)(2,1)}, u32[]{:S(2)}) copy-start(bf16[16,16,1024]{2,1,0:T(8,128)(2,1)} %param.7) | copy-start | bytes 1572868
  50.6 4.8 %collective-permute-start.4 = (f32[64,320]{1,0:T(8,128)S(1)}, f32[64,320]{1,0:T(8,128)S(1)}, u32[]{:S(2)}, u32[]{:S(2)}) collective-permute-start(f32[64,320]{1,0:T(8,128)S(1)} %get-tuple-element.24.own), channel_id=1, source_target_pairs={{0,1},{1,0},{2,3},{3,2},{4,5},{5,4},{6,7},{7,6},{8,9},{9,8},{10,11... | collective-permute-start | bytes 245768 | tf_op jit(solution)/shard_map/ppermute | solution.py:321
  55.4 3.0 collective-permute-start.7
  55.6 4.4 %collective-permute-start.6 = (bf16[64,384]{1,0:T(8,128)(2,1)S(1)}, bf16[64,384]{1,0:T(8,128)(2,1)S(1)}, u32[]{:S(2)}, u32[]{:S(2)}) collective-permute-start(bf16[64,384]{1,0:T(8,128)(2,1)S(1)} %shard_map.78.a), channel_id=1, source_target_pairs={{0,4},{1,5},{2,6},{3,7},{4,0},{5,1},{6,2},{7,3},{8,12},{9,13},{10,... | collective-permute-start | bytes 147464 | tf_op jit(solution)/shard_map/ppermute | solution.py:316
  56.2 5.2 %collective-permute-start.5 = (bf16[64,384]{1,0:T(8,128)(2,1)S(1)}, bf16[64,384]{1,0:T(8,128)(2,1)S(1)}, u32[]{:S(2)}, u32[]{:S(2)}) collective-permute-start(bf16[64,384]{1,0:T(8,128)(2,1)S(1)} %shard_map.78.a), channel_id=1, source_target_pairs={{0,2},{1,3},{2,4},{3,5},{4,6},{5,7},{6,0},{7,1},{8,10},{9,11},{10,... | collective-permute-start | bytes 147464 | tf_op jit(solution)/shard_map/ppermute | solution.py:316
  90.2 4.7 %collective-permute-start.8 = (f32[64,320]{1,0:T(8,128)S(1)}, f32[64,320]{1,0:T(8,128)S(1)}, u32[]{:S(2)}, u32[]{:S(2)}) collective-permute-start(f32[64,320]{1,0:T(8,128)S(1)} %shard_map.81.own), channel_id=1, source_target_pairs={{0,1},{1,0},{2,3},{3,2},{4,5},{5,4},{6,7},{7,6},{8,9},{9,8},{10,11... | collective-permute-start | bytes 245768 | tf_op jit(solution)/shard_map/ppermute | solution.py:321
  95.0 3.0 collective-permute-start.11
  96.6 4.4 %collective-permute-start.10 = (bf16[64,384]{1,0:T(8,128)(2,1)S(1)}, bf16[64,384]{1,0:T(8,128)(2,1)S(1)}, u32[]{:S(2)}, u32[]{:S(2)}) collective-permute-start(bf16[64,384]{1,0:T(8,128)(2,1)S(1)} %shard_map.82.a), channel_id=1, source_target_pairs={{0,4},{1,5},{2,6},{3,7},{4,0},{5,1},{6,2},{7,3},{8,12},{9,13},{10,... | collective-permute-start | bytes 147464 | tf_op jit(solution)/shard_map/ppermute | solution.py:316
  97.3 4.4 %collective-permute-start.9 = (bf16[64,384]{1,0:T(8,128)(2,1)S(1)}, bf16[64,384]{1,0:T(8,128)(2,1)S(1)}, u32[]{:S(2)}, u32[]{:S(2)}) collective-permute-start(bf16[64,384]{1,0:T(8,128)(2,1)S(1)} %shard_map.82.a), channel_id=1, source_target_pairs={{0,2},{1,3},{2,4},{3,5},{4,6},{5,7},{6,0},{7,1},{8,10},{9,11},{10,... | collective-permute-start | bytes 147464 | tf_op jit(solution)/shard_map/ppermute | solution.py:316
  130.7 5.2 %collective-permute-start.12 = (f32[64,320]{1,0:T(8,128)S(1)}, f32[64,320]{1,0:T(8,128)S(1)}, u32[]{:S(2)}, u32[]{:S(2)}) collective-permute-start(f32[64,320]{1,0:T(8,128)S(1)} %shard_map.85.own), channel_id=1, source_target_pairs={{0,1},{1,0},{2,3},{3,2},{4,5},{5,4},{6,7},{7,6},{8,9},{9,8},{10,11... | collective-permute-start | bytes 245768 | tf_op jit(solution)/shard_map/ppermute | solution.py:321
  136.0 3.0 collective-permute-start.15
  136.3 4.4 %collective-permute-start.14 = (bf16[64,384]{1,0:T(8,128)(2,1)S(1)}, bf16[64,384]{1,0:T(8,128)(2,1)S(1)}, u32[]{:S(2)}, u32[]{:S(2)}) collective-permute-start(bf16[64,384]{1,0:T(8,128)(2,1)S(1)} %shard_map.86.a), channel_id=1, source_target_pairs={{0,4},{1,5},{2,6},{3,7},{4,0},{5,1},{6,2},{7,3},{8,12},{9,13},{10,... | collective-permute-start | bytes 147464 | tf_op jit(solution)/shard_map/ppermute | solution.py:316
  137.3 4.8 %collective-permute-start.13 = (bf16[64,384]{1,0:T(8,128)(2,1)S(1)}, bf16[64,384]{1,0:T(8,128)(2,1)S(1)}, u32[]{:S(2)}, u32[]{:S(2)}) collective-permute-start(bf16[64,384]{1,0:T(8,128)(2,1)S(1)} %shard_map.86.a), channel_id=1, source_target_pairs={{0,2},{1,3},{2,4},{3,5},{4,6},{5,7},{6,0},{7,1},{8,10},{9,11},{10,... | collective-permute-start | bytes 147464 | tf_op jit(solution)/shard_map/ppermute | solution.py:316
  170.7 4.8 %collective-permute-start.16 = (f32[64,320]{1,0:T(8,128)S(1)}, f32[64,320]{1,0:T(8,128)S(1)}, u32[]{:S(2)}, u32[]{:S(2)}) collective-permute-start(f32[64,320]{1,0:T(8,128)S(1)} %shard_map.89.own), channel_id=1, source_target_pairs={{0,1},{1,0},{2,3},{3,2},{4,5},{5,4},{6,7},{7,6},{8,9},{9,8},{10,11... | collective-permute-start | bytes 245768 | tf_op jit(solution)/shard_map/ppermute | solution.py:321
  175.5 12.0 %collective-permute-start.19 = (bf16[64,384]{1,0:T(8,128)(2,1)S(1)}, bf16[64,384]{1,0:T(8,128)(2,1)S(1)}, u32[]{:S(2)}, u32[]{:S(2)}) collective-permute-start(bf16[64,384]{1,0:T(8,128)(2,1)S(1)} %shard_map.90.a), channel_id=1, source_target_pairs={{0,6},{1,7},{2,0},{3,1},{4,2},{5,3},{6,4},{7,5},{8,14},{9,15},{10,... | collective-permute-start | bytes 147464 | tf_op jit(solution)/shard_map/ppermute | solution.py:316
  177.1 10.5 %collective-permute-start.18 = (bf16[64,384]{1,0:T(8,128)(2,1)S(1)}, bf16[64,384]{1,0:T(8,128)(2,1)S(1)}, u32[]{:S(2)}, u32[]{:S(2)}) collective-permute-start(bf16[64,384]{1,0:T(8,128)(2,1)S(1)} %shard_map.90.a), channel_id=1, source_target_pairs={{0,4},{1,5},{2,6},{3,7},{4,0},{5,1},{6,2},{7,3},{8,12},{9,13},{10,... | collective-permute-start | bytes 147464 | tf_op jit(solution)/shard_map/ppermute | solution.py:316
  177.7 13.9 %collective-permute-start.17 = (bf16[64,384]{1,0:T(8,128)(2,1)S(1)}, bf16[64,384]{1,0:T(8,128)(2,1)S(1)}, u32[]{:S(2)}, u32[]{:S(2)}) collective-permute-start(bf16[64,384]{1,0:T(8,128)(2,1)S(1)} %shard_map.90.a), channel_id=1, source_target_pairs={{0,2},{1,3},{2,4},{3,5},{4,6},{5,7},{6,0},{7,1},{8,10},{9,11},{10,... | collective-permute-start | bytes 147464 | tf_op jit(solution)/shard_map/ppermute | solution.py:316
  220.2 5.7 %collective-permute-start.20 = (f32[64,320]{1,0:T(8,128)S(1)}, f32[64,320]{1,0:T(8,128)S(1)}, u32[]{:S(2)}, u32[]{:S(2)}) collective-permute-start(f32[64,320]{1,0:T(8,128)S(1)} %shard_map.93.own), channel_id=1, source_target_pairs={{0,1},{1,0},{2,3},{3,2},{4,5},{5,4},{6,7},{7,6},{8,9},{9,8},{10,11... | collective-permute-start | bytes 245768 | tf_op jit(solution)/shard_map/ppermute | solution.py:321
  226.0 3.0 collective-permute-start.23
  226.4 4.4 %collective-permute-start.22 = (bf16[64,384]{1,0:T(8,128)(2,1)S(1)}, bf16[64,384]{1,0:T(8,128)(2,1)S(1)}, u32[]{:S(2)}, u32[]{:S(2)}) collective-permute-start(bf16[64,384]{1,0:T(8,128)(2,1)S(1)} %shard_map.94.a), channel_id=1, source_target_pairs={{0,4},{1,5},{2,6},{3,7},{4,0},{5,1},{6,2},{7,3},{8,12},{9,13},{10,... | collective-permute-start | bytes 147464 | tf_op jit(solution)/shard_map/ppermute | solution.py:316
  227.2 4.2 %collective-permute-start.21 = (bf16[64,384]{1,0:T(8,128)(2,1)S(1)}, bf16[64,384]{1,0:T(8,128)(2,1)S(1)}, u32[]{:S(2)}, u32[]{:S(2)}) collective-permute-start(bf16[64,384]{1,0:T(8,128)(2,1)S(1)} %shard_map.94.a), channel_id=1, source_target_pairs={{0,2},{1,3},{2,4},{3,5},{4,6},{5,7},{6,0},{7,1},{8,10},{9,11},{10,... | collective-permute-start | bytes 147464 | tf_op jit(solution)/shard_map/ppermute | solution.py:316
  234.6 26.6 %copy-start.3 = (bf16[512,1024]{1,0:T(8,128)(2,1)S(1)}, bf16[512,1024]{1,0:T(8,128)(2,1)}, u32[]{:S(2)}) copy-start(bf16[512,1024]{1,0:T(8,128)(2,1)} %prompts.1) | copy-start | bytes 3145732
  247.9 13.3 %all-to-all-start.11 = ((bf16[32,16,128]{2,1,0:T(8,128)(2,1)}), bf16[32,16,128]{2,1,0:T(8,128)(2,1)S(1)}, u32[]{:S(2)}, u32[]{:S(2)}) async-start(bf16[32,16,128]{2,1,0:T(8,128)(2,1)} %shard_map.96), calls=%async_computation.11 | async-start | bytes 262144 | tf_op jit(solution)/shard_map/all_to_all | solution.py:348
  277.1 6.8 %collective-permute-start.24 = (f32[64,704]{1,0:T(8,128)S(1)}, f32[64,704]{1,0:T(8,128)S(1)}, u32[]{:S(2)}, u32[]{:S(2)}) collective-permute-start(f32[64,704]{1,0:T(8,128)S(1)} %shard_map.98.own), channel_id=1, source_target_pairs={{0,1},{1,0},{2,3},{3,2},{4,5},{5,4},{6,7},{7,6},{8,9},{9,8},{10,11... | collective-permute-start | bytes 540680 | tf_op jit(solution)/shard_map/ppermute | solution.py:321
  284.0 4.0 %collective-permute-start.27 = (bf16[64,768]{1,0:T(8,128)(2,1)S(1)}, bf16[64,768]{1,0:T(8,128)(2,1)S(1)}, u32[]{:S(2)}, u32[]{:S(2)}) collective-permute-start(bf16[64,768]{1,0:T(8,128)(2,1)S(1)} %shard_map.99.a), channel_id=1, source_target_pairs={{0,6},{1,7},{2,0},{3,1},{4,2},{5,3},{6,4},{7,5},{8,14},{9,15},{10,... | collective-permute-start | bytes 294920 | tf_op jit(solution)/shard_map/ppermute | solution.py:316
  285.7 5.0 %collective-permute-start.26 = (bf16[64,768]{1,0:T(8,128)(2,1)S(1)}, bf16[64,768]{1,0:T(8,128)(2,1)S(1)}, u32[]{:S(2)}, u32[]{:S(2)}) collective-permute-start(bf16[64,768]{1,0:T(8,128)(2,1)S(1)} %shard_map.99.a), channel_id=1, source_target_pairs={{0,4},{1,5},{2,6},{3,7},{4,0},{5,1},{6,2},{7,3},{8,12},{9,13},{10,... | collective-permute-start | bytes 294920 | tf_op jit(solution)/shard_map/ppermute | solution.py:316
  286.3 7.4 %collective-permute-start.25 = (bf16[64,768]{1,0:T(8,128)(2,1)S(1)}, bf16[64,768]{1,0:T(8,128)(2,1)S(1)}, u32[]{:S(2)}, u32[]{:S(2)}) collective-permute-start(bf16[64,768]{1,0:T(8,128)(2,1)S(1)} %shard_map.99.a), channel_id=1, source_target_pairs={{0,2},{1,3},{2,4},{3,5},{4,6},{5,7},{6,0},{7,1},{8,10},{9,11},{10,... | collective-permute-start | bytes 294920 | tf_op jit(solution)/shard_map/ppermute | solution.py:316

commit v3 on v2

--- a/solution.py
+++ b/solution.py
@@ -7,7 +7,7 @@
 
 SWEEPS = 3
 RANK = 16
-CORES = 2
+CORES, CHIPS = 2, 4
 BF = jnp.bfloat16
 F32 = jnp.float32
 
@@ -164,20 +164,21 @@
 def start_body(down, up, vt, ut, out):
     q = dot_nt(ut[...], up[...])
     p = dot_nt(vt[...], down[...])
-    out[...] = jnp.concatenate([q, p], axis=1)
-
-
-def pair_body(own, got, out):
+    out[...] = jnp.concatenate([q, p], axis=1).astype(BF)
+
+
+def along_y_body(a, b, c, d, out):
+    total = added((a, b, c, d))
+    extra = total.shape[1] - out.shape[1]
+    if extra:
+        plain = out.shape[1] - extra
+        gram = total[:, plain : plain + extra] + total[:, plain + extra :]
+        total = jnp.concatenate([total[:, :plain], gram], axis=1)
+    out[...] = total
+
+
+def first_body(own, got, stack, fisher_row, tiles, q_out, p_out):
     total = own[...] + got[...]
-    plain = 2 * total.shape[1] - out.shape[1]
-    if plain == total.shape[1]:
-        out[...] = total.astype(BF)
-    else:
-        out[...] = jnp.concatenate([total[:, :plain].astype(BF), halves(total[:, plain:])], axis=1)
-
-
-def first_body(a, b, c, d, stack, fisher_row, tiles, q_out, p_out):
-    total = added((a, b, c, d))
     count = total.shape[1] // 2
     q, p = total[:, :count], total[:, count:]
     q_out[...] = q
@@ -203,7 +204,8 @@
 
 def project_body(tiles, stack, out):
     numer = read_tiles(tiles, stack.shape[1])
-    out[...] = jnp.concatenate([dot_nt(numer, stack[...]), dot_nt(numer, numer)], axis=1)
+    y = dot_nt(numer, stack[...]).astype(BF)
+    out[...] = jnp.concatenate([y, halves(dot_nt(numer, numer))], axis=1)
 
 
 def project_ids_body(tiles, stack, out, ids_out):
@@ -212,14 +214,10 @@
     ids_out[...] = (ids[0:1] * RANK + ids[1:2]).astype(jnp.int32)
 
 
-def split_gram(total, at, size):
-    return total[:, at : at + size] + total[:, at + size : at + 2 * size]
-
-
 def renew(parts, other, stack, fisher_row, tiles, fresh_out):
-    total = added(parts)
+    total = parts[0][...] + parts[1][...]
     size, count = other.shape
-    inverse = inverse_factor(split_gram(total, count, size))
+    inverse = inverse_factor(total[:, count:])
     fresh = in_three(dot_nn, inverse, total[:, :count])
     fresh_out[...] = fresh
     terms = weighted_terms(fresh, other[...], fisher_row[...])
@@ -227,14 +225,14 @@
     return inverse
 
 
-def renew_body(a, b, c, d, other, stack, fisher_row, tiles, fresh_out):
-    renew((a, b, c, d), other, stack, fisher_row, tiles, fresh_out)
+def renew_body(own, got, other, stack, fisher_row, tiles, fresh_out):
+    renew((own, got), other, stack, fisher_row, tiles, fresh_out)
 
 
 def last_renew_body(
-    a, b, c, d, other, stack, fisher_row, numer_tiles, tiles, fresh_out, basis_out
+    own, got, other, stack, fisher_row, numer_tiles, tiles, fresh_out, basis_out
 ):
-    inverse = renew((a, b, c, d), other, stack, fisher_row, tiles, fresh_out)
+    inverse = renew((own, got), other, stack, fisher_row, tiles, fresh_out)
     numer = read_tiles(numer_tiles, stack.shape[1]).astype(F32)
     basis_out[...] = in_three(dot_nn, inverse, numer).astype(BF)
 
@@ -271,38 +269,37 @@
         picked[i] = jnp.concatenate(
             [side_by_side(chosen_z[at : at + each]), side_by_side(mine)], axis=0
         ).astype(BF)
-    hidden_out[...] = dot_nt(numer, prompts[...])
-    gram_out[...] = dot_nt(numer, numer)
+    hidden_out[...] = dot_nt(numer, prompts[...]).astype(BF)
+    gram_out[...] = halves(dot_nt(numer, numer))
 
 
 def join_body(core, parts, hidden, gram, out):
     total = summed(parts)
-    size = gram.shape[1]
     cut = total.shape[0] * 2 // 3
     z = one_below_other(total[:cut])
-    q = one_below_other(total[cut:])
+    q = one_below_other(total[cut:]) / CHIPS
     none = jnp.zeros_like(q)
     q = jnp.where(
         core[0] == 0, jnp.concatenate([q, none], axis=0), jnp.concatenate([none, q], axis=0)
     )
-    out[...] = jnp.concatenate([hidden[...], z, q, gram[...]], axis=1)
-
-
-def serve_body(a, b, c, d, basis, out):
-    total = added((a, b, c, d))
+    out[...] = jnp.concatenate([hidden[...], z.astype(BF), q.astype(BF), gram[...]], axis=1)
+
+
+def serve_body(own, got, basis, out):
+    total = own[...] + got[...]
     size = total.shape[0]
     rows = out.shape[0]
     asked = size // RANK
     each = rows // asked
     z = total[:, rows : rows + size]
-    q = a[:, rows + size : rows + 2 * size]
+    q = total[:, rows + size : rows + 2 * size].astype(BF)
     z_high = z.astype(BF)
     z_low = (z - z_high.astype(F32)).astype(BF)
     crossed = []
     for j in range(asked):
         take = slice(j * RANK, (j + 1) * RANK)
         crossed.append(dot_tn(q[take], z_high[take]) + dot_tn(q[take], z_low[take]))
-    inverse = inverse_factor(split_gram(total, rows + 2 * size, size))
+    inverse = inverse_factor(total[:, rows + 2 * size :])
     cores = in_three(dot_nt, jnp.concatenate(crossed, axis=0), inverse).astype(BF)
     hidden = in_three(dot_nn, inverse, total[:, :rows]).astype(BF)
     for j in range(asked):
@@ -323,8 +320,9 @@
 
 def over_feature(value, gram_size):
     rows, lanes = value.shape
-    pair = call(pair_body, shape((rows, lanes + gram_size), BF), value, other_core(value))
-    return [pair] + [around_y(pair, d) for d in (1, 2, 3)]
+    parts = [value] + [around_y(value, d) for d in (1, 3, 2)]
+    chips = call(along_y_body, shape((rows, lanes - gram_size), F32), *parts)
+    return [chips, other_core(chips)]
 
 
 def on_device(adapter_down, adapter_up, fisher, init_v, init_u, prompt_rows, request_ids):
@@ -351,12 +349,12 @@
         return swap(call(sum_body, tile_shape, swap(tiles)))
 
     def projected(numer, stack):
-        value = call(project_body, shape((size, count + size), F32), numer, stack)
+        value = call(project_body, shape((size, count + 2 * size), BF), numer, stack)
         return over_feature(value, size)
 
     value = call(
         start_body,
-        shape((size, 2 * count), F32),
+        shape((size, 2 * count), BF),
         down,
         up,
         init_v.T.astype(BF),
@@ -372,7 +370,7 @@
             )
             value, every_id = call(
                 project_ids_body,
-                [shape((size, count + size), F32), shape((1, 128), jnp.int32)],
+                [shape((size, count + 2 * size), BF), shape((1, 128), jnp.int32)],
                 swap(copies),
                 up,
             )
@@ -399,7 +397,7 @@
     packed = blocks * RANK * 3 // 4
     picked, hidden, gram = call(
         pick_body,
-        [shape((ways, packed, 2 * size), BF), shape((size, rows), F32), shape((size, size), F32)],
+        [shape((ways, packed, 2 * size), BF), shape((size, rows), BF), shape((size, 2 * size), BF)],
         core,
         reduced(tiles),
         down,
@@ -408,7 +406,7 @@
         pick_rows,
     )
     value = call(
-        join_body, shape((size, rows + 3 * size), F32), core, swap(picked), hidden, gram
+        join_body, shape((size, rows + 4 * size), BF), core, swap(picked), hidden, gram
     )
     return call(serve_body, shape((rows, width), BF), *over_feature(value, size), basis)
 

time: 303 us -> 304 us (level)
  starting transfers between devices: 69.5 us -> 75.2 us
  waiting for transfers between devices: 56.2 us -> 51 us
    ppermute x7, starting transfers between devices: 29.5 us -> 43.2 us  [other_core(): return lax.ppermute(value, 'feature', [(i, i ^ 1) for i in range(size)])]
    ppermute x21, starting transfers between devices: 24.7 us -> 16.9 us  [around_y(): lax.ppermute(value, 'feature', [(i, (i + d * CORES) % size) for i in rang...]
    ppermute x21, waiting for transfers between devices: 31.7 us -> 27.4 us  [around_y(): lax.ppermute(value, 'feature', [(i, (i + d * CORES) % size) for i in rang...]
  transfers between devices with their start and end apart: 30 -> 30, of which waited for: 28 -> 24; matrix products, arithmetic and copies ran while one was open for 0% -> 0% of each run, Pallas kernels for 0% -> 0%
where the time goes in v3:
time: 304 us; the launch traced here: 300 us
  blocking collectives  143 us (47%)
  starting transfers between devices  75.2 us (25%)
  waiting for transfers between devices  51 us (17%)
  Pallas kernels  26.5 us (9%)
    all_to_all x11, blocking collectives, swap(): return lax.all_to_all(parts, 'adapter', 0, 0, tiled=True)  143 us
    ppermute x7, starting transfers between devices, other_core(): return lax.ppermute(value, 'feature', [(i, i ^ 1) for i in range(size)])  43.2 us
    ppermute x21, waiting for transfers between devices, around_y(): lax.ppermute(value, 'feature', [(i, (i + d * CORES) % size) for i in rang...  27.4 us
    pallas_call x28, Pallas kernels, call(): pl.pallas_call(body, out_shape=outs, in_specs=[scalar if arg.shape == (1,...  26.5 us
    all_to_all x2, waiting for transfers between devices, swap(): return lax.all_to_all(parts, 'adapter', 0, 0, tiled=True)  17.6 us
    ppermute x21, starting transfers between devices, around_y(): lax.ppermute(value, 'feature', [(i, (i + d * CORES) % size) for i in rang...  16.9 us
    all_to_all x2, starting transfers between devices, swap(): return lax.all_to_all(parts, 'adapter', 0, 0, tiled=True)  15 us
  transfers between devices with their start and end apart: 30, of which 24 were waited for; matrix products, arithmetic and copies ran while one was open for 0% of the time, Pallas kernels for 0%

profile of v3, /device:TPU:1, one launch (start us, length us, event | category | flops | bytes accessed | tf_op | source)
XLA Modules:
  0.0 299.9 jit_solution(4893756139600037643)
XLA Ops:
  0.0 1.1 convert_bitcast_fusion
  1.2 1.0 copy-done.1
  2.7 3.8 %collective-permute-start.2 = (bf16[64,512]{1,0:T(8,128)(2,1)S(1)}, bf16[64,512]{1,0:T(8,128)(2,1)S(1)}, u32[]{:S(2)}, u32[]{:S(2)}) collective-permute-start(bf16[64,512]{1,0:T(8,128)(2,1)S(1)} %shard_map.73.a), channel_id=1, source_target_pairs={{0,4},{1,5},{2,6},{3,7},{4,0},{5,1},{6,2},{7,3},{8,12},{9,13},{10,... | collective-permute-start | bytes 196616 | tf_op jit(solution)/shard_map/ppermute | solution.py:313
  8.2 2.4 collective-permute-done.1.c
  10.6 1.2 collective-permute-done.b
  11.8 2.3 collective-permute-start.3
  15.1 1.4 shard_map.75
  16.6 11.2 %all-to-all-start = ((bf16[32,16,128]{2,1,0:T(8,128)(2,1)}), bf16[32,16,128]{2,1,0:T(8,128)(2,1)S(1)}, u32[]{:S(2)}, u32[]{:S(2)}) async-start(bf16[32,16,128]{2,1,0:T(8,128)(2,1)} %get-tuple-element.23), calls=%async_computation | async-start | bytes 262144 | tf_op jit(solution)/shard_map/all_to_all | solution.py:346
  28.1 9.0 %all-to-all-done.parts = bf16[32,16,128]{2,1,0:T(8,128)(2,1)S(1)} async-done(((bf16[32,16,128]{2,1,0:T(8,128)(2,1)}), bf16[32,16,128]{2,1,0:T(8,128)(2,1)S(1)}, u32[]{:S(2)}, u32[]{:S(2)}) %all-to-all-start) | async-done | bytes 131104 | tf_op jit(solution)/shard_map/all_to_all | solution.py:346
  37.1 14.1 %all_to_all.65.tiles = bf16[32,32,128]{2,1,0:T(8,128)(2,1)S(1)} all-to-all(bf16[32,32,128]{2,1,0:T(8,128)(2,1)S(1)} %shard_map.76), channel_id=1, replica_groups=mesh['adapter'=32,'feature'=8] {'adapter'}, dimensions={0} | all-to-all | bytes 524288 | tf_op jit(solution)/shard_map/all_to_all | solution.py:346
  51.9 1.7 collective-permute-start.5
  53.5 2.6 collective-permute-done.6.d
  56.1 1.6 collective-permute-done.4.b
  57.8 5.5 %collective-permute-start.7 = (f32[64,320]{1,0:T(8,128)S(1)}, f32[64,320]{1,0:T(8,128)S(1)}, u32[]{:S(2)}, u32[]{:S(2)}) collective-permute-start(f32[64,320]{1,0:T(8,128)S(1)} %shard_map.78.own), channel_id=1, source_target_pairs={{0,1},{1,0},{2,3},{3,2},{4,5},{5,4},{6,7},{7,6},{8,9},{9,8},{10,11... | collective-permute-start | bytes 245768 | tf_op jit(solution)/shard_map/ppermute | solution.py:318
  64.2 3.1 %shard_map.79 = (bf16[32,16,128]{2,1,0:T(8,128)(2,1)S(1)}, f32[64,256]{1,0:T(8,128)S(1)}) custom-call(f32[64,320]{1,0:T(8,128)S(1)} %shard_map.78.own, f32[64,320]{1,0:T(8,128)S(1)} %collective-permute-done.7.got, f32[64,256]{1,0:T(8,128)S(1)} %get-tuple-element.25.other, bf16[256,1024]{1,0:T(8,128)(2,1)S(1)} %bitcast.21, ...), custom_call_target="tpu_custom_call" | custom-call | tf_op jit(solution)/shard_map/pallas_call | solution.py:19
  67.3 12.5 %all_to_all.66.parts = bf16[32,16,128]{2,1,0:T(8,128)(2,1)S(1)} all-to-all(bf16[32,16,128]{2,1,0:T(8,128)(2,1)S(1)} %get-tuple-element.26), channel_id=1, replica_groups=mesh['adapter'=32,'feature'=8] {'adapter'}, dimensions={0} | all-to-all | bytes 262144 | tf_op jit(solution)/shard_map/all_to_all | solution.py:346
  79.8 13.0 %all_to_all.67.tiles = bf16[32,16,128]{2,1,0:T(8,128)(2,1)S(1)} all-to-all(bf16[32,16,128]{2,1,0:T(8,128)(2,1)S(1)} %shard_map.80), channel_id=1, replica_groups=mesh['adapter'=32,'feature'=8] {'adapter'}, dimensions={0} | all-to-all | bytes 262144 | tf_op jit(solution)/shard_map/all_to_all | solution.py:346
  95.1 2.7 collective-permute-done.10.d
  98.8 4.7 %collective-permute-start.11 = (f32[64,320]{1,0:T(8,128)S(1)}, f32[64,320]{1,0:T(8,128)S(1)}, u32[]{:S(2)}, u32[]{:S(2)}) collective-permute-start(f32[64,320]{1,0:T(8,128)S(1)} %shard_map.82.own), channel_id=1, source_target_pairs={{0,1},{1,0},{2,3},{3,2},{4,5},{5,4},{6,7},{7,6},{8,9},{9,8},{10,11... | collective-permute-start | bytes 245768 | tf_op jit(solution)/shard_map/ppermute | solution.py:318
  104.4 3.1 %shard_map.83 = (bf16[32,16,128]{2,1,0:T(8,128)(2,1)S(1)}, f32[64,256]{1,0:T(8,128)S(1)}) custom-call(f32[64,320]{1,0:T(8,128)S(1)} %shard_map.82.own, f32[64,320]{1,0:T(8,128)S(1)} %collective-permute-done.11.got, f32[64,256]{1,0:T(8,128)S(1)} %get-tuple-element.27.other, bf16[256,1024]{1,0:T(8,128)(2,1)S(1)} %bitcast.16, ...), custom_call_target="tpu_custom_call" | custom-call | tf_op jit(solution)/shard_map/pallas_call | solution.py:19
  107.5 12.3 %all_to_all.68.parts = bf16[32,16,128]{2,1,0:T(8,128)(2,1)S(1)} all-to-all(bf16[32,16,128]{2,1,0:T(8,128)(2,1)S(1)} %get-tuple-element.28), channel_id=1, replica_groups=mesh['adapter'=32,'feature'=8] {'adapter'}, dimensions={0} | all-to-all | bytes 262144 | tf_op jit(solution)/shard_map/all_to_all | solution.py:346
  119.8 13.0 %all_to_all.69.tiles = bf16[32,16,128]{2,1,0:T(8,128)(2,1)S(1)} all-to-all(bf16[32,16,128]{2,1,0:T(8,128)(2,1)S(1)} %shard_map.84), channel_id=1, replica_groups=mesh['adapter'=32,'feature'=8] {'adapter'}, dimensions={0} | all-to-all | bytes 262144 | tf_op jit(solution)/shard_map/all_to_all | solution.py:346
  135.3 2.5 collective-permute-done.14.d
  137.7 1.2 collective-permute-done.12.b
  139.0 4.7 %collective-permute-start.15 = (f32[64,320]{1,0:T(8,128)S(1)}, f32[64,320]{1,0:T(8,128)S(1)}, u32[]{:S(2)}, u32[]{:S(2)}) collective-permute-start(f32[64,320]{1,0:T(8,128)S(1)} %shard_map.86.own), channel_id=1, source_target_pairs={{0,1},{1,0},{2,3},{3,2},{4,5},{5,4},{6,7},{7,6},{8,9},{9,8},{10,11... | collective-permute-start | bytes 245768 | tf_op jit(solution)/shard_map/ppermute | solution.py:318
  144.7 3.1 %shard_map.87 = (bf16[32,16,128]{2,1,0:T(8,128)(2,1)S(1)}, f32[64,256]{1,0:T(8,128)S(1)}) custom-call(f32[64,320]{1,0:T(8,128)S(1)} %shard_map.86.own, f32[64,320]{1,0:T(8,128)S(1)} %collective-permute-done.15.got, f32[64,256]{1,0:T(8,128)S(1)} %get-tuple-element.29.other, bf16[256,1024]{1,0:T(8,128)(2,1)S(1)} %bitcast.23, ...), custom_call_target="tpu_custom_call" | custom-call | tf_op jit(solution)/shard_map/pallas_call | solution.py:19
  147.7 12.3 %all_to_all.70.parts = bf16[32,16,128]{2,1,0:T(8,128)(2,1)S(1)} all-to-all(bf16[32,16,128]{2,1,0:T(8,128)(2,1)S(1)} %get-tuple-element.30), channel_id=1, replica_groups=mesh['adapter'=32,'feature'=8] {'adapter'}, dimensions={0} | all-to-all | bytes 262144 | tf_op jit(solution)/shard_map/all_to_all | solution.py:346
  160.1 13.0 %all_to_all.71.tiles = bf16[32,16,128]{2,1,0:T(8,128)(2,1)S(1)} all-to-all(bf16[32,16,128]{2,1,0:T(8,128)(2,1)S(1)} %shard_map.88), channel_id=1, replica_groups=mesh['adapter'=32,'feature'=8] {'adapter'}, dimensions={0} | all-to-all | bytes 262144 | tf_op jit(solution)/shard_map/all_to_all | solution.py:346
  175.8 2.2 collective-permute-done.18.d
  178.0 1.4 collective-permute-done.16.b
  179.5 14.7 %collective-permute-start.19 = (f32[64,320]{1,0:T(8,128)S(1)}, f32[64,320]{1,0:T(8,128)S(1)}, u32[]{:S(2)}, u32[]{:S(2)}) collective-permute-start(f32[64,320]{1,0:T(8,128)S(1)} %shard_map.90.own), channel_id=1, source_target_pairs={{0,1},{1,0},{2,3},{3,2},{4,5},{5,4},{6,7},{7,6},{8,9},{9,8},{10,11... | collective-permute-start | bytes 245768 | tf_op jit(solution)/shard_map/ppermute | solution.py:318
  195.1 3.1 %shard_map.91 = (bf16[32,16,128]{2,1,0:T(8,128)(2,1)S(1)}, f32[64,256]{1,0:T(8,128)S(1)}) custom-call(f32[64,320]{1,0:T(8,128)S(1)} %shard_map.90.own, f32[64,320]{1,0:T(8,128)S(1)} %collective-permute-done.19.got, f32[64,256]{1,0:T(8,128)S(1)} %get-tuple-element.31.other, bf16[256,1024]{1,0:T(8,128)(2,1)S(1)} %bitcast.18, ...), custom_call_target="tpu_custom_call" | custom-call | tf_op jit(solution)/shard_map/pallas_call | solution.py:19
  198.2 12.3 %all_to_all.72.parts = bf16[32,16,128]{2,1,0:T(8,128)(2,1)S(1)} all-to-all(bf16[32,16,128]{2,1,0:T(8,128)(2,1)S(1)} %get-tuple-element.32), channel_id=1, replica_groups=mesh['adapter'=32,'feature'=8] {'adapter'}, dimensions={0} | all-to-all | bytes 262144 | tf_op jit(solution)/shard_map/all_to_all | solution.py:346
  210.6 13.0 %all_to_all.73.tiles.numer_tiles = bf16[32,16,128]{2,1,0:T(8,128)(2,1)S(1)} all-to-all(bf16[32,16,128]{2,1,0:T(8,128)(2,1)S(1)} %shard_map.92), channel_id=1, replica_groups=mesh['adapter'=32,'feature'=8] {'adapter'}, dimensions={0} | all-to-all | bytes 262144 | tf_op jit(solution)/shard_map/all_to_all | solution.py:346
  224.1 1.7 collective-permute-start.21
  225.7 2.7 collective-permute-done.22.d
  228.5 1.4 collective-permute-done.20.b
  230.0 4.7 %collective-permute-start.23 = (f32[64,320]{1,0:T(8,128)S(1)}, f32[64,320]{1,0:T(8,128)S(1)}, u32[]{:S(2)}, u32[]{:S(2)}) collective-permute-start(f32[64,320]{1,0:T(8,128)S(1)} %shard_map.94.own), channel_id=1, source_target_pairs={{0,1},{1,0},{2,3},{3,2},{4,5},{5,4},{6,7},{7,6},{8,9},{9,8},{10,11... | collective-permute-start | bytes 245768 | tf_op jit(solution)/shard_map/ppermute | solution.py:318
  235.6 3.1 %shard_map.95 = (bf16[32,16,128]{2,1,0:T(8,128)(2,1)S(1)}, f32[64,256]{1,0:T(8,128)S(1)}, bf16[64,1024]{1,0:T(8,128)(2,1)S(1)}) custom-call(f32[64,320]{1,0:T(8,128)S(1)} %shard_map.94.own, f32[64,320]{1,0:T(8,128)S(1)} %collective-permute-done.23.got, f32[64,256]{1,0:T(8,128)S(1)} %get-tuple-element.33.other, bf16[256,1024]{1,0:T(8,128)(2,1)S(1)} %bitcast.25, ...), custom_call_target="tpu_custom_call" | custom-call | tf_op jit(solution)/shard_map/pallas_call | solution.py:19
  238.8 12.4 %all_to_all.74.parts = bf16[32,16,128]{2,1,0:T(8,128)(2,1)S(1)} all-to-all(bf16[32,16,128]{2,1,0:T(8,128)(2,1)S(1)} %get-tuple-element.34), channel_id=1, replica_groups=mesh['adapter'=32,'feature'=8] {'adapter'}, dimensions={0} | all-to-all | bytes 262144 | tf_op jit(solution)/shard_map/all_to_all | solution.py:346
  251.9 3.9 %all-to-all-start.11 = ((bf16[32,16,128]{2,1,0:T(8,128)(2,1)}), bf16[32,16,128]{2,1,0:T(8,128)(2,1)S(1)}, u32[]{:S(2)}, u32[]{:S(2)}) async-start(bf16[32,16,128]{2,1,0:T(8,128)(2,1)} %shard_map.96), calls=%async_computation.11 | async-start | bytes 262144 | tf_op jit(solution)/shard_map/all_to_all | solution.py:346
  256.5 8.7 %all-to-all-done.11.tiles = bf16[32,16,128]{2,1,0:T(8,128)(2,1)S(1)} async-done(((bf16[32,16,128]{2,1,0:T(8,128)(2,1)}), bf16[32,16,128]{2,1,0:T(8,128)(2,1)S(1)}, u32[]{:S(2)}, u32[]{:S(2)}) %all-to-all-start.11) | async-done | bytes 131104 | tf_op jit(solution)/shard_map/all_to_all | solution.py:346
  265.2 1.2 shard_map.97
  266.4 14.8 %all_to_all.75.parts = bf16[32,48,128]{2,1,0:T(8,128)(2,1)S(1)} all-to-all(bf16[32,48,128]{2,1,0:T(8,128)(2,1)S(1)} %get-tuple-element.37), channel_id=1, replica_groups=mesh['adapter'=32,'feature'=8] {'adapter'}, dimensions={0} | all-to-all | bytes 786432 | tf_op jit(solution)/shard_map/all_to_all | solution.py:346
  282.9 3.5 %collective-permute-done.26.d = bf16[64,768]{1,0:T(8,128)(2,1)S(1)} collective-permute-done((bf16[64,768]{1,0:T(8,128)(2,1)S(1)}, bf16[64,768]{1,0:T(8,128)(2,1)S(1)}, u32[]{:S(2)}, u32[]{:S(2)}) %collective-permute-start.26) | collective-permute-done | bytes 98336 | tf_op jit(solution)/shard_map/ppermute | solution.py:313
  287.5 6.7 %collective-permute-start.27 = (f32[64,704]{1,0:T(8,128)S(1)}, f32[64,704]{1,0:T(8,128)S(1)}, u32[]{:S(2)}, u32[]{:S(2)}) collective-permute-start(f32[64,704]{1,0:T(8,128)S(1)} %shard_map.99.own), channel_id=1, source_target_pairs={{0,1},{1,0},{2,3},{3,2},{4,5},{5,4},{6,7},{7,6},{8,9},{9,8},{10,11... | collective-permute-start | bytes 540680 | tf_op jit(solution)/shard_map/ppermute | solution.py:318
  294.2 1.1 collective-permute-done.27.got
  295.3 4.5 %shard_map.100 = bf16[512,1024]{1,0:T(8,128)(2,1)} custom-call(f32[64,704]{1,0:T(8,128)S(1)} %shard_map.99.own, f32[64,704]{1,0:T(8,128)S(1)} %collective-permute-done.27.got, bf16[64,1024]{1,0:T(8,128)(2,1)S(1)} %get-tuple-element.40.basis), custom_call_target="tpu_custom_call" | custom-call | tf_op jit(solution)/shard_map/pallas_call | solution.py:19
  (73 shorter events, 22.5 us)
Async XLA Ops:
  0.0 1.2 copy-start
  1.2 1.0 copy-start.1
  2.7 5.5 %collective-permute-start.2 = (bf16[64,512]{1,0:T(8,128)(2,1)S(1)}, bf16[64,512]{1,0:T(8,128)(2,1)S(1)}, u32[]{:S(2)}, u32[]{:S(2)}) collective-permute-start(bf16[64,512]{1,0:T(8,128)(2,1)S(1)} %shard_map.73.a), channel_id=1, source_target_pairs={{0,4},{1,5},{2,6},{3,7},{4,0},{5,1},{6,2},{7,3},{8,12},{9,13},{10,... | collective-permute-start | bytes 196616 | tf_op jit(solution)/shard_map/ppermute | solution.py:313
  6.5 4.0 %collective-permute-start.1 = (bf16[64,512]{1,0:T(8,128)(2,1)S(1)}, bf16[64,512]{1,0:T(8,128)(2,1)S(1)}, u32[]{:S(2)}, u32[]{:S(2)}) collective-permute-start(bf16[64,512]{1,0:T(8,128)(2,1)S(1)} %shard_map.73.a), channel_id=1, source_target_pairs={{0,6},{1,7},{2,0},{3,1},{4,2},{5,3},{6,4},{7,5},{8,14},{9,15},{10,... | collective-permute-start | bytes 196616 | tf_op jit(solution)/shard_map/ppermute | solution.py:313
  7.3 4.5 %collective-permute-start = (bf16[64,512]{1,0:T(8,128)(2,1)S(1)}, bf16[64,512]{1,0:T(8,128)(2,1)S(1)}, u32[]{:S(2)}, u32[]{:S(2)}) collective-permute-start(bf16[64,512]{1,0:T(8,128)(2,1)S(1)} %shard_map.73.a), channel_id=1, source_target_pairs={{0,2},{1,3},{2,4},{3,5},{4,6},{5,7},{6,0},{7,1},{8,10},{9,11},{10,... | collective-permute-start | bytes 196616 | tf_op jit(solution)/shard_map/ppermute | solution.py:313
  11.8 3.3 %collective-permute-start.3 = (f32[64,512]{1,0:T(8,128)S(1)}, f32[64,512]{1,0:T(8,128)S(1)}, u32[]{:S(2)}, u32[]{:S(2)}) collective-permute-start(f32[64,512]{1,0:T(8,128)S(1)} %shard_map.74.own), channel_id=1, source_target_pairs={{0,1},{1,0},{2,3},{3,2},{4,5},{5,4},{6,7},{7,6},{8,9},{9,8},{10,11... | collective-permute-start | bytes 393224 | tf_op jit(solution)/shard_map/ppermute | solution.py:318
  14.1 0.7 copy-start.4
  16.6 11.2 %copy-start.5 = (s32[4]{0:T(128)S(1)}, s32[4]{0:T(128)}, u32[]{:S(2)}) copy-start(s32[4]{0:T(128)} %param.13) | copy-start | bytes 52
  16.6 20.5 %all-to-all-start = ((bf16[32,16,128]{2,1,0:T(8,128)(2,1)}), bf16[32,16,128]{2,1,0:T(8,128)(2,1)S(1)}, u32[]{:S(2)}, u32[]{:S(2)}) async-start(bf16[32,16,128]{2,1,0:T(8,128)(2,1)} %get-tuple-element.23), calls=%async_computation | async-start | bytes 262144 | tf_op jit(solution)/shard_map/all_to_all | solution.py:346
  51.2 13.0 %copy-start.2 = (bf16[16,16,1024]{2,1,0:T(8,128)(2,1)S(1)}, bf16[16,16,1024]{2,1,0:T(8,128)(2,1)}, u32[]{:S(2)}) copy-start(bf16[16,16,1024]{2,1,0:T(8,128)(2,1)} %param.7) | copy-start | bytes 1572868
  51.6 4.5 %collective-permute-start.6 = (bf16[64,384]{1,0:T(8,128)(2,1)S(1)}, bf16[64,384]{1,0:T(8,128)(2,1)S(1)}, u32[]{:S(2)}, u32[]{:S(2)}) collective-permute-start(bf16[64,384]{1,0:T(8,128)(2,1)S(1)} %get-tuple-element.24.a), channel_id=1, source_target_pairs={{0,4},{1,5},{2,6},{3,7},{4,0},{5,1},{6,2},{7,3},{8,12},{9,13},{10,... | collective-permute-start | bytes 147464 | tf_op jit(solution)/shard_map/ppermute | solution.py:313
  51.9 4.2 %collective-permute-start.5 = (bf16[64,384]{1,0:T(8,128)(2,1)S(1)}, bf16[64,384]{1,0:T(8,128)(2,1)S(1)}, u32[]{:S(2)}, u32[]{:S(2)}) collective-permute-start(bf16[64,384]{1,0:T(8,128)(2,1)S(1)} %get-tuple-element.24.a), channel_id=1, source_target_pairs={{0,6},{1,7},{2,0},{3,1},{4,2},{5,3},{6,4},{7,5},{8,14},{9,15},{10,... | collective-permute-start | bytes 147464 | tf_op jit(solution)/shard_map/ppermute | solution.py:313
  53.5 4.2 %collective-permute-start.4 = (bf16[64,384]{1,0:T(8,128)(2,1)S(1)}, bf16[64,384]{1,0:T(8,128)(2,1)S(1)}, u32[]{:S(2)}, u32[]{:S(2)}) collective-permute-start(bf16[64,384]{1,0:T(8,128)(2,1)S(1)} %get-tuple-element.24.a), channel_id=1, source_target_pairs={{0,2},{1,3},{2,4},{3,5},{4,6},{5,7},{6,0},{7,1},{8,10},{9,11},{10,... | collective-permute-start | bytes 147464 | tf_op jit(solution)/shard_map/ppermute | solution.py:313
  57.8 6.5 %collective-permute-start.7 = (f32[64,320]{1,0:T(8,128)S(1)}, f32[64,320]{1,0:T(8,128)S(1)}, u32[]{:S(2)}, u32[]{:S(2)}) collective-permute-start(f32[64,320]{1,0:T(8,128)S(1)} %shard_map.78.own), channel_id=1, source_target_pairs={{0,1},{1,0},{2,3},{3,2},{4,5},{5,4},{6,7},{7,6},{8,9},{9,8},{10,11... | collective-permute-start | bytes 245768 | tf_op jit(solution)/shard_map/ppermute | solution.py:318
  93.2 4.5 %collective-permute-start.10 = (bf16[64,384]{1,0:T(8,128)(2,1)S(1)}, bf16[64,384]{1,0:T(8,128)(2,1)S(1)}, u32[]{:S(2)}, u32[]{:S(2)}) collective-permute-start(bf16[64,384]{1,0:T(8,128)(2,1)S(1)} %shard_map.81.a), channel_id=1, source_target_pairs={{0,4},{1,5},{2,6},{3,7},{4,0},{5,1},{6,2},{7,3},{8,12},{9,13},{10,... | collective-permute-start | bytes 147464 | tf_op jit(solution)/shard_map/ppermute | solution.py:313
  93.3 4.4 %collective-permute-start.9 = (bf16[64,384]{1,0:T(8,128)(2,1)S(1)}, bf16[64,384]{1,0:T(8,128)(2,1)S(1)}, u32[]{:S(2)}, u32[]{:S(2)}) collective-permute-start(bf16[64,384]{1,0:T(8,128)(2,1)S(1)} %shard_map.81.a), channel_id=1, source_target_pairs={{0,6},{1,7},{2,0},{3,1},{4,2},{5,3},{6,4},{7,5},{8,14},{9,15},{10,... | collective-permute-start | bytes 147464 | tf_op jit(solution)/shard_map/ppermute | solution.py:313
  94.3 4.4 %collective-permute-start.8 = (bf16[64,384]{1,0:T(8,128)(2,1)S(1)}, bf16[64,384]{1,0:T(8,128)(2,1)S(1)}, u32[]{:S(2)}, u32[]{:S(2)}) collective-permute-start(bf16[64,384]{1,0:T(8,128)(2,1)S(1)} %shard_map.81.a), channel_id=1, source_target_pairs={{0,2},{1,3},{2,4},{3,5},{4,6},{5,7},{6,0},{7,1},{8,10},{9,11},{10,... | collective-permute-start | bytes 147464 | tf_op jit(solution)/shard_map/ppermute | solution.py:313
  98.8 5.6 %collective-permute-start.11 = (f32[64,320]{1,0:T(8,128)S(1)}, f32[64,320]{1,0:T(8,128)S(1)}, u32[]{:S(2)}, u32[]{:S(2)}) collective-permute-start(f32[64,320]{1,0:T(8,128)S(1)} %shard_map.82.own), channel_id=1, source_target_pairs={{0,1},{1,0},{2,3},{3,2},{4,5},{5,4},{6,7},{7,6},{8,9},{9,8},{10,11... | collective-permute-start | bytes 245768 | tf_op jit(solution)/shard_map/ppermute | solution.py:318
  133.2 4.5 %collective-permute-start.14 = (bf16[64,384]{1,0:T(8,128)(2,1)S(1)}, bf16[64,384]{1,0:T(8,128)(2,1)S(1)}, u32[]{:S(2)}, u32[]{:S(2)}) collective-permute-start(bf16[64,384]{1,0:T(8,128)(2,1)S(1)} %shard_map.85.a), channel_id=1, source_target_pairs={{0,4},{1,5},{2,6},{3,7},{4,0},{5,1},{6,2},{7,3},{8,12},{9,13},{10,... | collective-permute-start | bytes 147464 | tf_op jit(solution)/shard_map/ppermute | solution.py:313
  133.8 3.9 %collective-permute-start.13 = (bf16[64,384]{1,0:T(8,128)(2,1)S(1)}, bf16[64,384]{1,0:T(8,128)(2,1)S(1)}, u32[]{:S(2)}, u32[]{:S(2)}) collective-permute-start(bf16[64,384]{1,0:T(8,128)(2,1)S(1)} %shard_map.85.a), channel_id=1, source_target_pairs={{0,6},{1,7},{2,0},{3,1},{4,2},{5,3},{6,4},{7,5},{8,14},{9,15},{10,... | collective-permute-start | bytes 147464 | tf_op jit(solution)/shard_map/ppermute | solution.py:313
  134.8 4.2 %collective-permute-start.12 = (bf16[64,384]{1,0:T(8,128)(2,1)S(1)}, bf16[64,384]{1,0:T(8,128)(2,1)S(1)}, u32[]{:S(2)}, u32[]{:S(2)}) collective-permute-start(bf16[64,384]{1,0:T(8,128)(2,1)S(1)} %shard_map.85.a), channel_id=1, source_target_pairs={{0,2},{1,3},{2,4},{3,5},{4,6},{5,7},{6,0},{7,1},{8,10},{9,11},{10,... | collective-permute-start | bytes 147464 | tf_op jit(solution)/shard_map/ppermute | solution.py:313
  139.0 5.6 %collective-permute-start.15 = (f32[64,320]{1,0:T(8,128)S(1)}, f32[64,320]{1,0:T(8,128)S(1)}, u32[]{:S(2)}, u32[]{:S(2)}) collective-permute-start(f32[64,320]{1,0:T(8,128)S(1)} %shard_map.86.own), channel_id=1, source_target_pairs={{0,1},{1,0},{2,3},{3,2},{4,5},{5,4},{6,7},{7,6},{8,9},{9,8},{10,11... | collective-permute-start | bytes 245768 | tf_op jit(solution)/shard_map/ppermute | solution.py:318
  173.5 4.5 %collective-permute-start.18 = (bf16[64,384]{1,0:T(8,128)(2,1)S(1)}, bf16[64,384]{1,0:T(8,128)(2,1)S(1)}, u32[]{:S(2)}, u32[]{:S(2)}) collective-permute-start(bf16[64,384]{1,0:T(8,128)(2,1)S(1)} %shard_map.89.a), channel_id=1, source_target_pairs={{0,4},{1,5},{2,6},{3,7},{4,0},{5,1},{6,2},{7,3},{8,12},{9,13},{10,... | collective-permute-start | bytes 147464 | tf_op jit(solution)/shard_map/ppermute | solution.py:313
  174.3 3.7 %collective-permute-start.17 = (bf16[64,384]{1,0:T(8,128)(2,1)S(1)}, bf16[64,384]{1,0:T(8,128)(2,1)S(1)}, u32[]{:S(2)}, u32[]{:S(2)}) collective-permute-start(bf16[64,384]{1,0:T(8,128)(2,1)S(1)} %shard_map.89.a), channel_id=1, source_target_pairs={{0,6},{1,7},{2,0},{3,1},{4,2},{5,3},{6,4},{7,5},{8,14},{9,15},{10,... | collective-permute-start | bytes 147464 | tf_op jit(solution)/shard_map/ppermute | solution.py:313
  175.2 4.2 %collective-permute-start.16 = (bf16[64,384]{1,0:T(8,128)(2,1)S(1)}, bf16[64,384]{1,0:T(8,128)(2,1)S(1)}, u32[]{:S(2)}, u32[]{:S(2)}) collective-permute-start(bf16[64,384]{1,0:T(8,128)(2,1)S(1)} %shard_map.89.a), channel_id=1, source_target_pairs={{0,2},{1,3},{2,4},{3,5},{4,6},{5,7},{6,0},{7,1},{8,10},{9,11},{10,... | collective-permute-start | bytes 147464 | tf_op jit(solution)/shard_map/ppermute | solution.py:313
  179.5 15.6 %collective-permute-start.19 = (f32[64,320]{1,0:T(8,128)S(1)}, f32[64,320]{1,0:T(8,128)S(1)}, u32[]{:S(2)}, u32[]{:S(2)}) collective-permute-start(f32[64,320]{1,0:T(8,128)S(1)} %shard_map.90.own), channel_id=1, source_target_pairs={{0,1},{1,0},{2,3},{3,2},{4,5},{5,4},{6,7},{7,6},{8,9},{9,8},{10,11... | collective-permute-start | bytes 245768 | tf_op jit(solution)/shard_map/ppermute | solution.py:318
  224.0 4.5 %collective-permute-start.22 = (bf16[64,384]{1,0:T(8,128)(2,1)S(1)}, bf16[64,384]{1,0:T(8,128)(2,1)S(1)}, u32[]{:S(2)}, u32[]{:S(2)}) collective-permute-start(bf16[64,384]{1,0:T(8,128)(2,1)S(1)} %shard_map.93.a), channel_id=1, source_target_pairs={{0,4},{1,5},{2,6},{3,7},{4,0},{5,1},{6,2},{7,3},{8,12},{9,13},{10,... | collective-permute-start | bytes 147464 | tf_op jit(solution)/shard_map/ppermute | solution.py:313
  224.1 4.4 %collective-permute-start.21 = (bf16[64,384]{1,0:T(8,128)(2,1)S(1)}, bf16[64,384]{1,0:T(8,128)(2,1)S(1)}, u32[]{:S(2)}, u32[]{:S(2)}) collective-permute-start(bf16[64,384]{1,0:T(8,128)(2,1)S(1)} %shard_map.93.a), channel_id=1, source_target_pairs={{0,6},{1,7},{2,0},{3,1},{4,2},{5,3},{6,4},{7,5},{8,14},{9,15},{10,... | collective-permute-start | bytes 147464 | tf_op jit(solution)/shard_map/ppermute | solution.py:313
  225.7 4.2 %collective-permute-start.20 = (bf16[64,384]{1,0:T(8,128)(2,1)S(1)}, bf16[64,384]{1,0:T(8,128)(2,1)S(1)}, u32[]{:S(2)}, u32[]{:S(2)}) collective-permute-start(bf16[64,384]{1,0:T(8,128)(2,1)S(1)} %shard_map.93.a), channel_id=1, source_target_pairs={{0,2},{1,3},{2,4},{3,5},{4,6},{5,7},{6,0},{7,1},{8,10},{9,11},{10,... | collective-permute-start | bytes 147464 | tf_op jit(solution)/shard_map/ppermute | solution.py:313
  230.0 5.6 %collective-permute-start.23 = (f32[64,320]{1,0:T(8,128)S(1)}, f32[64,320]{1,0:T(8,128)S(1)}, u32[]{:S(2)}, u32[]{:S(2)}) collective-permute-start(f32[64,320]{1,0:T(8,128)S(1)} %shard_map.94.own), channel_id=1, source_target_pairs={{0,1},{1,0},{2,3},{3,2},{4,5},{5,4},{6,7},{7,6},{8,9},{9,8},{10,11... | collective-permute-start | bytes 245768 | tf_op jit(solution)/shard_map/ppermute | solution.py:318
  238.8 26.4 %copy-start.3 = (bf16[512,1024]{1,0:T(8,128)(2,1)S(1)}, bf16[512,1024]{1,0:T(8,128)(2,1)}, u32[]{:S(2)}) copy-start(bf16[512,1024]{1,0:T(8,128)(2,1)} %prompts.1) | copy-start | bytes 3145732
  251.9 13.2 %all-to-all-start.11 = ((bf16[32,16,128]{2,1,0:T(8,128)(2,1)}), bf16[32,16,128]{2,1,0:T(8,128)(2,1)S(1)}, u32[]{:S(2)}, u32[]{:S(2)}) async-start(bf16[32,16,128]{2,1,0:T(8,128)(2,1)} %shard_map.96), calls=%async_computation.11 | async-start | bytes 262144 | tf_op jit(solution)/shard_map/all_to_all | solution.py:346
  281.3 5.0 %collective-permute-start.26 = (bf16[64,768]{1,0:T(8,128)(2,1)S(1)}, bf16[64,768]{1,0:T(8,128)(2,1)S(1)}, u32[]{:S(2)}, u32[]{:S(2)}) collective-permute-start(bf16[64,768]{1,0:T(8,128)(2,1)S(1)} %shard_map.98.a), channel_id=1, source_target_pairs={{0,4},{1,5},{2,6},{3,7},{4,0},{5,1},{6,2},{7,3},{8,12},{9,13},{10,... | collective-permute-start | bytes 294920 | tf_op jit(solution)/shard_map/ppermute | solution.py:313
  281.4 5.0 %collective-permute-start.25 = (bf16[64,768]{1,0:T(8,128)(2,1)S(1)}, bf16[64,768]{1,0:T(8,128)(2,1)S(1)}, u32[]{:S(2)}, u32[]{:S(2)}) collective-permute-start(bf16[64,768]{1,0:T(8,128)(2,1)S(1)} %shard_map.98.a), channel_id=1, source_target_pairs={{0,6},{1,7},{2,0},{3,1},{4,2},{5,3},{6,4},{7,5},{8,14},{9,15},{10,... | collective-permute-start | bytes 294920 | tf_op jit(solution)/shard_map/ppermute | solution.py:313
  282.3 5.1 %collective-permute-start.24 = (bf16[64,768]{1,0:T(8,128)(2,1)S(1)}, bf16[64,768]{1,0:T(8,128)(2,1)S(1)}, u32[]{:S(2)}, u32[]{:S(2)}) collective-permute-start(bf16[64,768]{1,0:T(8,128)(2,1)S(1)} %shard_map.98.a), channel_id=1, source_target_pairs={{0,2},{1,3},{2,4},{3,5},{4,6},{5,7},{6,0},{7,1},{8,10},{9,11},{10,... | collective-permute-start | bytes 294920 | tf_op jit(solution)/shard_map/ppermute | solution.py:313
  287.5 7.8 %collective-permute-start.27 = (f32[64,704]{1,0:T(8,128)S(1)}, f32[64,704]{1,0:T(8,128)S(1)}, u32[]{:S(2)}, u32[]{:S(2)}) collective-permute-start(f32[64,704]{1,0:T(8,128)S(1)} %shard_map.99.own), channel_id=1, source_target_pairs={{0,1},{1,0},{2,3},{3,2},{4,5},{5,4},{6,7},{7,6},{8,9},{9,8},{10,11... | collective-permute-start | bytes 540680 | tf_op jit(solution)/shard_map/ppermute | solution.py:318

commit v4 on v2

--- a/solution.py
+++ b/solution.py
@@ -288,7 +288,7 @@
     out[...] = jnp.concatenate([hidden[...], z, q, gram[...]], axis=1)
 
 
-def serve_body(a, b, c, d, basis, out):
+def serve_body(a, b, c, d, basis, out, hold, sent):
     total = added((a, b, c, d))
     size = total.shape[0]
     rows = out.shape[0]
@@ -305,10 +305,17 @@
     inverse = inverse_factor(split_gram(total, rows + 2 * size, size))
     cores = in_three(dot_nt, jnp.concatenate(crossed, axis=0), inverse).astype(BF)
     hidden = in_three(dot_nn, inverse, total[:, :rows]).astype(BF)
+    copies = []
     for j in range(asked):
         core = cores[j * size : (j + 1) * size]
         mixed = dot_nn(core, hidden[:, j * each : (j + 1) * each]).astype(BF)
-        out[j * each : (j + 1) * each, :] = dot_tn(mixed, basis[...]).astype(BF)
+        hold[j] = dot_tn(mixed, basis[...]).astype(BF)
+        copies.append(
+            pltpu.make_async_copy(hold.at[j], out.at[pl.ds(j * each, each)], sent.at[j])
+        )
+        copies[j].start()
+    for copy in copies:
+        copy.wait()
 
 
 def around_y(value, d):
@@ -324,7 +331,7 @@
 def over_feature(value, gram_size):
     rows, lanes = value.shape
     pair = call(pair_body, shape((rows, lanes + gram_size), BF), value, other_core(value))
-    return [pair] + [around_y(pair, d) for d in (1, 2, 3)]
+    return [pair] + [around_y(pair, d) for d in (1, 3, 2)]
 
 
 def on_device(adapter_down, adapter_up, fisher, init_v, init_u, prompt_rows, request_ids):
@@ -362,9 +369,8 @@
         init_v.T.astype(BF),
         init_u.T.astype(BF),
     )
-    tiles, q, p = call(
-        first_body, [tile_shape, flat, flat], *over_feature(value, 0), up, fisher_row
-    )
+    parts, id_tile = lax.optimization_barrier((over_feature(value, 0), id_tile))
+    tiles, q, p = call(first_body, [tile_shape, flat, flat], *parts, up, fisher_row)
     for sweep in range(SWEEPS):
         if sweep == 0:
             copies = call(
@@ -376,7 +382,10 @@
                 swap(copies),
                 up,
             )
-            parts = over_feature(value, size)
+            local_id = every_id[0, : ways * blocks] - position * fisher.shape[0]
+            parts, pick_rows = lax.optimization_barrier(
+                (over_feature(value, size), jnp.repeat(local_id, RANK)[:, None])
+            )
         else:
             numer = reduced(tiles)
             parts = projected(numer, up)
@@ -394,7 +403,6 @@
                 fisher_row,
                 numer,
             )
-    pick_rows = jnp.repeat(every_id[0, : ways * blocks] - position * fisher.shape[0], RANK)[:, None]
     core = jnp.full((1,), lax.axis_index("feature") % CORES, jnp.int32)
     packed = blocks * RANK * 3 // 4
     picked, hidden, gram = call(
@@ -410,7 +418,19 @@
     value = call(
         join_body, shape((size, rows + 3 * size), F32), core, swap(picked), hidden, gram
     )
-    return call(serve_body, shape((rows, width), BF), *over_feature(value, size), basis)
+    whole = pl.BlockSpec(memory_space=pltpu.VMEM)
+    parts = over_feature(value, size)
+    return pl.pallas_call(
+        serve_body,
+        out_shape=shape((rows, width), BF),
+        in_specs=[whole] * (len(parts) + 1),
+        out_specs=pl.BlockSpec(memory_space=pl.ANY),
+        scratch_shapes=[
+            pltpu.VMEM((blocks, rows // blocks, width), BF),
+            pltpu.SemaphoreType.DMA((blocks,)),
+        ],
+        compiler_params=pltpu.CompilerParams(vmem_limit_bytes=40 * 1024 * 1024),
+    )(*parts, basis)
 
 
 def solution(mesh):

time: 303 us -> 300 us (0.990)
  blocking collectives: 142 us -> 161 us
  waiting for transfers between devices: 56.2 us -> 43.2 us
  starting transfers between devices: 69.5 us -> 60.1 us
    all_to_all x11 -> x12, blocking collectives: 142 us -> 161 us  [swap(): return lax.all_to_all(parts, 'adapter', 0, 0, tiled=True)]
    all_to_all x2 -> x1, starting transfers between devices: 15.3 us -> 3.86 us  [swap(): return lax.all_to_all(parts, 'adapter', 0, 0, tiled=True)]
    all_to_all x2 -> x1, waiting for transfers between devices: 17.7 us -> 9.02 us  [swap(): return lax.all_to_all(parts, 'adapter', 0, 0, tiled=True)]
    pallas_call x28 -> x27, Pallas kernels: 26.6 us -> 21.6 us  [call(): pl.pallas_call(body, out_shape=outs, in_specs=[scalar if arg.shape == (1,...]
    pallas_call x0 -> x1, Pallas kernels: none -> 4.29 us  [on_device(): pl.pallas_call(serve_body, out_shape=shape((rows, width), BF), in_specs=[...]
    ppermute x21, waiting for transfers between devices: 31.7 us -> 28.4 us  [around_y(): lax.ppermute(value, 'feature', [(i, (i + d * CORES) % size) for i in rang...]
  transfers between devices with their start and end apart: 30 -> 29, of which waited for: 28 -> 22; matrix products, arithmetic and copies ran while one was open for 0% -> 0% of each run, Pallas kernels for 0% -> 0%
where the time goes in v4:
time: 300 us; the launch traced here: 295 us
  blocking collectives  161 us (54%)
  starting transfers between devices  60.1 us (20%)
  waiting for transfers between devices  43.2 us (14%)
  Pallas kernels  25.8 us (9%)
  local copies, waits for them, and re-layouts  3.43 us (1%)
    all_to_all x12, blocking collectives, swap(): return lax.all_to_all(parts, 'adapter', 0, 0, tiled=True)  161 us
    ppermute x7, starting transfers between devices, other_core(): return lax.ppermute(value, 'feature', [(i, i ^ 1) for i in range(size)])  31.8 us
    ppermute x21, waiting for transfers between devices, around_y(): lax.ppermute(value, 'feature', [(i, (i + d * CORES) % size) for i in rang...  28.4 us
    ppermute x21, starting transfers between devices, around_y(): lax.ppermute(value, 'feature', [(i, (i + d * CORES) % size) for i in rang...  24.4 us
    pallas_call x27, Pallas kernels, call(): pl.pallas_call(body, out_shape=outs, in_specs=[scalar if arg.shape == (1,...  21.6 us
    all_to_all x1, waiting for transfers between devices, swap(): return lax.all_to_all(parts, 'adapter', 0, 0, tiled=True)  9.02 us
  transfers between devices with their start and end apart: 29, of which 22 were waited for; matrix products, arithmetic and copies ran while one was open for 0% of the time, Pallas kernels for 0%

profile of v4, /device:TPU:1, one launch (start us, length us, event | category | flops | bytes accessed | tf_op | source)
XLA Modules:
  0.0 295.4 jit_solution(16217915242897117610)
XLA Ops:
  0.0 1.1 convert_bitcast_fusion
  2.7 3.3 %collective-permute-start = (f32[64,512]{1,0:T(8,128)S(1)}, f32[64,512]{1,0:T(8,128)S(1)}, u32[]{:S(2)}, u32[]{:S(2)}) collective-permute-start(f32[64,512]{1,0:T(8,128)S(1)} %shard_map.73.own), channel_id=1, source_target_pairs={{0,1},{1,0},{2,3},{3,2},{4,5},{5,4},{6,7},{7,6},{8,9},{9,8},{10,11... | collective-permute-start | bytes 393224 | tf_op jit(solution)/shard_map/ppermute | solution.py:328
  7.5 1.3 collective-permute-start.3
  10.6 2.2 collective-permute-done.3.d
  14.9 20.2 %all_to_all.65.parts = bf16[32,16,128]{2,1,0:T(8,128)(2,1)S(1)} all-to-all(bf16[32,16,128]{2,1,0:T(8,128)(2,1)S(1)} %get-tuple-element.37), channel_id=1, replica_groups=mesh['adapter'=32,'feature'=8] {'adapter'}, dimensions={0} | all-to-all | bytes 262144 | tf_op jit(solution)/shard_map/all_to_all | solution.py:355
  35.1 13.7 %all_to_all.66.tiles = bf16[32,32,128]{2,1,0:T(8,128)(2,1)S(1)} all-to-all(bf16[32,32,128]{2,1,0:T(8,128)(2,1)S(1)} %shard_map.76), channel_id=1, replica_groups=mesh['adapter'=32,'feature'=8] {'adapter'}, dimensions={0} | all-to-all | bytes 524288 | tf_op jit(solution)/shard_map/all_to_all | solution.py:355
  49.1 4.3 %collective-permute-start.4 = (f32[64,320]{1,0:T(8,128)S(1)}, f32[64,320]{1,0:T(8,128)S(1)}, u32[]{:S(2)}, u32[]{:S(2)}) collective-permute-start(f32[64,320]{1,0:T(8,128)S(1)} %get-tuple-element.39.own), channel_id=1, source_target_pairs={{0,1},{1,0},{2,3},{3,2},{4,5},{5,4},{6,7},{7,6},{8,9},{9,8},{10,11... | collective-permute-start | bytes 245768 | tf_op jit(solution)/shard_map/ppermute | solution.py:328
  54.5 1.1 collective-permute-start.7
  57.3 1.7 collective-permute-done.7.d
  59.2 1.6 collective-permute-done.5.b
  60.8 3.1 %shard_map.79 = (bf16[32,16,128]{2,1,0:T(8,128)(2,1)S(1)}, f32[64,256]{1,0:T(8,128)S(1)}) custom-call(bf16[64,384]{1,0:T(8,128)(2,1)S(1)} %shard_map.78.a, bf16[64,384]{1,0:T(8,128)(2,1)S(1)} %collective-permute-done.5.b, bf16[64,384]{1,0:T(8,128)(2,1)S(1)} %collective-permute-done.6.c, bf16[64,384]{1,0:T(8,128)(2,1)S(1)} %collective-permute-done.7.d, ...), custom_call_target="tpu_custom_call" | custom-call | tf_op jit(solution)/shard_map/pallas_call | solution.py:19
  63.9 12.4 %all_to_all.67.parts = bf16[32,16,128]{2,1,0:T(8,128)(2,1)S(1)} all-to-all(bf16[32,16,128]{2,1,0:T(8,128)(2,1)S(1)} %get-tuple-element.46), channel_id=1, replica_groups=mesh['adapter'=32,'feature'=8] {'adapter'}, dimensions={0} | all-to-all | bytes 262144 | tf_op jit(solution)/shard_map/all_to_all | solution.py:355
  76.4 12.6 %all_to_all.68.tiles = bf16[32,16,128]{2,1,0:T(8,128)(2,1)S(1)} all-to-all(bf16[32,16,128]{2,1,0:T(8,128)(2,1)S(1)} %shard_map.80), channel_id=1, replica_groups=mesh['adapter'=32,'feature'=8] {'adapter'}, dimensions={0} | all-to-all | bytes 262144 | tf_op jit(solution)/shard_map/all_to_all | solution.py:355
  89.4 4.7 %collective-permute-start.8 = (f32[64,320]{1,0:T(8,128)S(1)}, f32[64,320]{1,0:T(8,128)S(1)}, u32[]{:S(2)}, u32[]{:S(2)}) collective-permute-start(f32[64,320]{1,0:T(8,128)S(1)} %shard_map.81.own), channel_id=1, source_target_pairs={{0,1},{1,0},{2,3},{3,2},{4,5},{5,4},{6,7},{7,6},{8,9},{9,8},{10,11... | collective-permute-start | bytes 245768 | tf_op jit(solution)/shard_map/ppermute | solution.py:328
  95.3 1.5 collective-permute-start.10
  97.0 2.6 collective-permute-done.11.d
  99.6 1.5 collective-permute-done.9.b
  101.1 3.1 %shard_map.83 = (bf16[32,16,128]{2,1,0:T(8,128)(2,1)S(1)}, f32[64,256]{1,0:T(8,128)S(1)}) custom-call(bf16[64,384]{1,0:T(8,128)(2,1)S(1)} %shard_map.82.a, bf16[64,384]{1,0:T(8,128)(2,1)S(1)} %collective-permute-done.9.b, bf16[64,384]{1,0:T(8,128)(2,1)S(1)} %collective-permute-done.10.c, bf16[64,384]{1,0:T(8,128)(2,1)S(1)} %collective-permute-done.11.d, ...), custom_call_target="tpu_custom_call" | custom-call | tf_op jit(solution)/shard_map/pallas_call | solution.py:19
  104.3 12.5 %all_to_all.69.parts = bf16[32,16,128]{2,1,0:T(8,128)(2,1)S(1)} all-to-all(bf16[32,16,128]{2,1,0:T(8,128)(2,1)S(1)} %get-tuple-element.48), channel_id=1, replica_groups=mesh['adapter'=32,'feature'=8] {'adapter'}, dimensions={0} | all-to-all | bytes 262144 | tf_op jit(solution)/shard_map/all_to_all | solution.py:355
  116.8 12.6 %all_to_all.70.tiles = bf16[32,16,128]{2,1,0:T(8,128)(2,1)S(1)} all-to-all(bf16[32,16,128]{2,1,0:T(8,128)(2,1)S(1)} %shard_map.84), channel_id=1, replica_groups=mesh['adapter'=32,'feature'=8] {'adapter'}, dimensions={0} | all-to-all | bytes 262144 | tf_op jit(solution)/shard_map/all_to_all | solution.py:355
  129.8 4.7 %collective-permute-start.12 = (f32[64,320]{1,0:T(8,128)S(1)}, f32[64,320]{1,0:T(8,128)S(1)}, u32[]{:S(2)}, u32[]{:S(2)}) collective-permute-start(f32[64,320]{1,0:T(8,128)S(1)} %shard_map.85.own), channel_id=1, source_target_pairs={{0,1},{1,0},{2,3},{3,2},{4,5},{5,4},{6,7},{7,6},{8,9},{9,8},{10,11... | collective-permute-start | bytes 245768 | tf_op jit(solution)/shard_map/ppermute | solution.py:328
  137.1 2.9 collective-permute-done.15.d
  140.0 1.3 collective-permute-done.13.b
  141.3 3.1 %shard_map.87 = (bf16[32,16,128]{2,1,0:T(8,128)(2,1)S(1)}, f32[64,256]{1,0:T(8,128)S(1)}) custom-call(bf16[64,384]{1,0:T(8,128)(2,1)S(1)} %shard_map.86.a, bf16[64,384]{1,0:T(8,128)(2,1)S(1)} %collective-permute-done.13.b, bf16[64,384]{1,0:T(8,128)(2,1)S(1)} %collective-permute-done.14.c, bf16[64,384]{1,0:T(8,128)(2,1)S(1)} %collective-permute-done.15.d, ...), custom_call_target="tpu_custom_call" | custom-call | tf_op jit(solution)/shard_map/pallas_call | solution.py:19
  144.4 12.4 %all_to_all.71.parts = bf16[32,16,128]{2,1,0:T(8,128)(2,1)S(1)} all-to-all(bf16[32,16,128]{2,1,0:T(8,128)(2,1)S(1)} %get-tuple-element.50), channel_id=1, replica_groups=mesh['adapter'=32,'feature'=8] {'adapter'}, dimensions={0} | all-to-all | bytes 262144 | tf_op jit(solution)/shard_map/all_to_all | solution.py:355
  156.9 12.7 %all_to_all.72.tiles = bf16[32,16,128]{2,1,0:T(8,128)(2,1)S(1)} all-to-all(bf16[32,16,128]{2,1,0:T(8,128)(2,1)S(1)} %shard_map.88), channel_id=1, replica_groups=mesh['adapter'=32,'feature'=8] {'adapter'}, dimensions={0} | all-to-all | bytes 262144 | tf_op jit(solution)/shard_map/all_to_all | solution.py:355
  170.0 4.1 %collective-permute-start.16 = (f32[64,320]{1,0:T(8,128)S(1)}, f32[64,320]{1,0:T(8,128)S(1)}, u32[]{:S(2)}, u32[]{:S(2)}) collective-permute-start(f32[64,320]{1,0:T(8,128)S(1)} %shard_map.89.own), channel_id=1, source_target_pairs={{0,1},{1,0},{2,3},{3,2},{4,5},{5,4},{6,7},{7,6},{8,9},{9,8},{10,11... | collective-permute-start | bytes 245768 | tf_op jit(solution)/shard_map/ppermute | solution.py:328
  175.4 1.2 collective-permute-start.18
  176.6 10.0 %collective-permute-start.17 = (bf16[64,384]{1,0:T(8,128)(2,1)S(1)}, bf16[64,384]{1,0:T(8,128)(2,1)S(1)}, u32[]{:S(2)}, u32[]{:S(2)}) collective-permute-start(bf16[64,384]{1,0:T(8,128)(2,1)S(1)} %shard_map.90.a), channel_id=1, source_target_pairs={{0,2},{1,3},{2,4},{3,5},{4,6},{5,7},{6,0},{7,1},{8,10},{9,11},{10,... | collective-permute-start | bytes 147464 | tf_op jit(solution)/shard_map/ppermute | solution.py:323
  186.6 3.9 %collective-permute-done.17.b = bf16[64,384]{1,0:T(8,128)(2,1)S(1)} collective-permute-done((bf16[64,384]{1,0:T(8,128)(2,1)S(1)}, bf16[64,384]{1,0:T(8,128)(2,1)S(1)}, u32[]{:S(2)}, u32[]{:S(2)}) %collective-permute-start.17) | collective-permute-done | bytes 49184 | tf_op jit(solution)/shard_map/ppermute | solution.py:323
  190.5 3.1 %shard_map.91 = (bf16[32,16,128]{2,1,0:T(8,128)(2,1)S(1)}, f32[64,256]{1,0:T(8,128)S(1)}) custom-call(bf16[64,384]{1,0:T(8,128)(2,1)S(1)} %shard_map.90.a, bf16[64,384]{1,0:T(8,128)(2,1)S(1)} %collective-permute-done.17.b, bf16[64,384]{1,0:T(8,128)(2,1)S(1)} %collective-permute-done.18.c, bf16[64,384]{1,0:T(8,128)(2,1)S(1)} %collective-permute-done.19.d, ...), custom_call_target="tpu_custom_call" | custom-call | tf_op jit(solution)/shard_map/pallas_call | solution.py:19
  193.6 12.4 %all_to_all.73.parts = bf16[32,16,128]{2,1,0:T(8,128)(2,1)S(1)} all-to-all(bf16[32,16,128]{2,1,0:T(8,128)(2,1)S(1)} %get-tuple-element.52), channel_id=1, replica_groups=mesh['adapter'=32,'feature'=8] {'adapter'}, dimensions={0} | all-to-all | bytes 262144 | tf_op jit(solution)/shard_map/all_to_all | solution.py:355
  206.0 12.5 %all_to_all.74.tiles.numer_tiles = bf16[32,16,128]{2,1,0:T(8,128)(2,1)S(1)} all-to-all(bf16[32,16,128]{2,1,0:T(8,128)(2,1)S(1)} %shard_map.92), channel_id=1, replica_groups=mesh['adapter'=32,'feature'=8] {'adapter'}, dimensions={0} | all-to-all | bytes 262144 | tf_op jit(solution)/shard_map/all_to_all | solution.py:355
  218.9 4.6 %collective-permute-start.20 = (f32[64,320]{1,0:T(8,128)S(1)}, f32[64,320]{1,0:T(8,128)S(1)}, u32[]{:S(2)}, u32[]{:S(2)}) collective-permute-start(f32[64,320]{1,0:T(8,128)S(1)} %shard_map.93.own), channel_id=1, source_target_pairs={{0,1},{1,0},{2,3},{3,2},{4,5},{5,4},{6,7},{7,6},{8,9},{9,8},{10,11... | collective-permute-start | bytes 245768 | tf_op jit(solution)/shard_map/ppermute | solution.py:328
  226.8 2.1 collective-permute-done.23.d
  229.0 1.5 collective-permute-done.21.b
  230.5 3.2 %shard_map.95 = (bf16[32,16,128]{2,1,0:T(8,128)(2,1)S(1)}, f32[64,256]{1,0:T(8,128)S(1)}, bf16[64,1024]{1,0:T(8,128)(2,1)S(1)}) custom-call(bf16[64,384]{1,0:T(8,128)(2,1)S(1)} %shard_map.94.a, bf16[64,384]{1,0:T(8,128)(2,1)S(1)} %collective-permute-done.21.b, bf16[64,384]{1,0:T(8,128)(2,1)S(1)} %collective-permute-done.22.c, ...), custom_call_target="tpu_custom_call" | custom-call | tf_op jit(solution)/shard_map/pallas_call | solution.py:19
  233.7 12.5 %all_to_all.75.parts = bf16[32,16,128]{2,1,0:T(8,128)(2,1)S(1)} all-to-all(bf16[32,16,128]{2,1,0:T(8,128)(2,1)S(1)} %get-tuple-element.54), channel_id=1, replica_groups=mesh['adapter'=32,'feature'=8] {'adapter'}, dimensions={0} | all-to-all | bytes 262144 | tf_op jit(solution)/shard_map/all_to_all | solution.py:355
  246.9 3.9 %all-to-all-start.11 = ((bf16[32,16,128]{2,1,0:T(8,128)(2,1)}), bf16[32,16,128]{2,1,0:T(8,128)(2,1)S(1)}, u32[]{:S(2)}, u32[]{:S(2)}) async-start(bf16[32,16,128]{2,1,0:T(8,128)(2,1)} %shard_map.96), calls=%async_computation.11 | async-start | bytes 262144 | tf_op jit(solution)/shard_map/all_to_all | solution.py:355
  251.1 9.0 %all-to-all-done.11.tiles = bf16[32,16,128]{2,1,0:T(8,128)(2,1)S(1)} async-done(((bf16[32,16,128]{2,1,0:T(8,128)(2,1)}), bf16[32,16,128]{2,1,0:T(8,128)(2,1)S(1)}, u32[]{:S(2)}, u32[]{:S(2)}) %all-to-all-start.11) | async-done | bytes 131104 | tf_op jit(solution)/shard_map/all_to_all | solution.py:355
  260.1 1.1 shard_map.97
  261.3 14.6 %all_to_all.76.parts = bf16[32,48,128]{2,1,0:T(8,128)(2,1)S(1)} all-to-all(bf16[32,48,128]{2,1,0:T(8,128)(2,1)S(1)} %get-tuple-element.57), channel_id=1, replica_groups=mesh['adapter'=32,'feature'=8] {'adapter'}, dimensions={0} | all-to-all | bytes 786432 | tf_op jit(solution)/shard_map/all_to_all | solution.py:355
  276.1 6.1 %collective-permute-start.24 = (f32[64,704]{1,0:T(8,128)S(1)}, f32[64,704]{1,0:T(8,128)S(1)}, u32[]{:S(2)}, u32[]{:S(2)}) collective-permute-start(f32[64,704]{1,0:T(8,128)S(1)} %shard_map.98.own), channel_id=1, source_target_pairs={{0,1},{1,0},{2,3},{3,2},{4,5},{5,4},{6,7},{7,6},{8,9},{9,8},{10,11... | collective-permute-start | bytes 540680 | tf_op jit(solution)/shard_map/ppermute | solution.py:328
  282.1 1.1 collective-permute-done.24.got
  283.4 1.6 collective-permute-start.26
  285.1 3.7 %collective-permute-done.27.d = bf16[64,768]{1,0:T(8,128)(2,1)S(1)} collective-permute-done((bf16[64,768]{1,0:T(8,128)(2,1)S(1)}, bf16[64,768]{1,0:T(8,128)(2,1)S(1)}, u32[]{:S(2)}, u32[]{:S(2)}) %collective-permute-start.27) | collective-permute-done | bytes 98336 | tf_op jit(solution)/shard_map/ppermute | solution.py:323
  288.9 2.0 collective-permute-done.25.b
  290.9 4.3 %shard_map.100 = bf16[512,1024]{1,0:T(8,128)(2,1)} custom-call(bf16[64,768]{1,0:T(8,128)(2,1)S(1)} %shard_map.99.a, bf16[64,768]{1,0:T(8,128)(2,1)S(1)} %collective-permute-done.25.b, bf16[64,768]{1,0:T(8,128)(2,1)S(1)} %collective-permute-done.26.c, bf16[64,768]{1,0:T(8,128)(2,1)S(1)} %collective-permute-done.27.d, bf16[64,1024]{1,0:T(8,128)(2,1)S(1)} %get-tuple-element.60.basis), custom_call_target="tpu_custom_call" | custom-call | tf_op jit(solution)/shard_map/pallas_call | solution.py:423
  (73 shorter events, 22.1 us)
Async XLA Ops:
  0.0 1.2 copy-start
  1.2 1.0 copy-start.1
  2.7 4.8 %collective-permute-start = (f32[64,512]{1,0:T(8,128)S(1)}, f32[64,512]{1,0:T(8,128)S(1)}, u32[]{:S(2)}, u32[]{:S(2)}) collective-permute-start(f32[64,512]{1,0:T(8,128)S(1)} %shard_map.73.own), channel_id=1, source_target_pairs={{0,1},{1,0},{2,3},{3,2},{4,5},{5,4},{6,7},{7,6},{8,9},{9,8},{10,11... | collective-permute-start | bytes 393224 | tf_op jit(solution)/shard_map/ppermute | solution.py:328
  6.0 0.7 copy-start.4
  6.8 0.7 copy-start.5
  7.5 5.3 %collective-permute-start.3 = (bf16[64,512]{1,0:T(8,128)(2,1)S(1)}, bf16[64,512]{1,0:T(8,128)(2,1)S(1)}, u32[]{:S(2)}, u32[]{:S(2)}) collective-permute-start(bf16[64,512]{1,0:T(8,128)(2,1)S(1)} %shard_map.74.a), channel_id=1, source_target_pairs={{0,4},{1,5},{2,6},{3,7},{4,0},{5,1},{6,2},{7,3},{8,12},{9,13},{10,... | collective-permute-start | bytes 196616 | tf_op jit(solution)/shard_map/ppermute | solution.py:323
  8.8 4.1 %collective-permute-start.2 = (bf16[64,512]{1,0:T(8,128)(2,1)S(1)}, bf16[64,512]{1,0:T(8,128)(2,1)S(1)}, u32[]{:S(2)}, u32[]{:S(2)}) collective-permute-start(bf16[64,512]{1,0:T(8,128)(2,1)S(1)} %shard_map.74.a), channel_id=1, source_target_pairs={{0,6},{1,7},{2,0},{3,1},{4,2},{5,3},{6,4},{7,5},{8,14},{9,15},{10,... | collective-permute-start | bytes 196616 | tf_op jit(solution)/shard_map/ppermute | solution.py:323
  9.6 4.3 %collective-permute-start.1 = (bf16[64,512]{1,0:T(8,128)(2,1)S(1)}, bf16[64,512]{1,0:T(8,128)(2,1)S(1)}, u32[]{:S(2)}, u32[]{:S(2)}) collective-permute-start(bf16[64,512]{1,0:T(8,128)(2,1)S(1)} %shard_map.74.a), channel_id=1, source_target_pairs={{0,2},{1,3},{2,4},{3,5},{4,6},{5,7},{6,0},{7,1},{8,10},{9,11},{10,... | collective-permute-start | bytes 196616 | tf_op jit(solution)/shard_map/ppermute | solution.py:323
  48.8 12.0 %copy-start.2 = (bf16[16,16,1024]{2,1,0:T(8,128)(2,1)S(1)}, bf16[16,16,1024]{2,1,0:T(8,128)(2,1)}, u32[]{:S(2)}) copy-start(bf16[16,16,1024]{2,1,0:T(8,128)(2,1)} %param.7) | copy-start | bytes 1572868
  49.1 5.3 %collective-permute-start.4 = (f32[64,320]{1,0:T(8,128)S(1)}, f32[64,320]{1,0:T(8,128)S(1)}, u32[]{:S(2)}, u32[]{:S(2)}) collective-permute-start(f32[64,320]{1,0:T(8,128)S(1)} %get-tuple-element.39.own), channel_id=1, source_target_pairs={{0,1},{1,0},{2,3},{3,2},{4,5},{5,4},{6,7},{7,6},{8,9},{9,8},{10,11... | collective-permute-start | bytes 245768 | tf_op jit(solution)/shard_map/ppermute | solution.py:328
  54.5 4.5 %collective-permute-start.7 = (bf16[64,384]{1,0:T(8,128)(2,1)S(1)}, bf16[64,384]{1,0:T(8,128)(2,1)S(1)}, u32[]{:S(2)}, u32[]{:S(2)}) collective-permute-start(bf16[64,384]{1,0:T(8,128)(2,1)S(1)} %shard_map.78.a), channel_id=1, source_target_pairs={{0,4},{1,5},{2,6},{3,7},{4,0},{5,1},{6,2},{7,3},{8,12},{9,13},{10,... | collective-permute-start | bytes 147464 | tf_op jit(solution)/shard_map/ppermute | solution.py:323
  55.6 3.6 %collective-permute-start.6 = (bf16[64,384]{1,0:T(8,128)(2,1)S(1)}, bf16[64,384]{1,0:T(8,128)(2,1)S(1)}, u32[]{:S(2)}, u32[]{:S(2)}) collective-permute-start(bf16[64,384]{1,0:T(8,128)(2,1)S(1)} %shard_map.78.a), channel_id=1, source_target_pairs={{0,6},{1,7},{2,0},{3,1},{4,2},{5,3},{6,4},{7,5},{8,14},{9,15},{10,... | collective-permute-start | bytes 147464 | tf_op jit(solution)/shard_map/ppermute | solution.py:323
  56.6 4.2 %collective-permute-start.5 = (bf16[64,384]{1,0:T(8,128)(2,1)S(1)}, bf16[64,384]{1,0:T(8,128)(2,1)S(1)}, u32[]{:S(2)}, u32[]{:S(2)}) collective-permute-start(bf16[64,384]{1,0:T(8,128)(2,1)S(1)} %shard_map.78.a), channel_id=1, source_target_pairs={{0,2},{1,3},{2,4},{3,5},{4,6},{5,7},{6,0},{7,1},{8,10},{9,11},{10,... | collective-permute-start | bytes 147464 | tf_op jit(solution)/shard_map/ppermute | solution.py:323
  89.4 5.7 %collective-permute-start.8 = (f32[64,320]{1,0:T(8,128)S(1)}, f32[64,320]{1,0:T(8,128)S(1)}, u32[]{:S(2)}, u32[]{:S(2)}) collective-permute-start(f32[64,320]{1,0:T(8,128)S(1)} %shard_map.81.own), channel_id=1, source_target_pairs={{0,1},{1,0},{2,3},{3,2},{4,5},{5,4},{6,7},{7,6},{8,9},{9,8},{10,11... | collective-permute-start | bytes 245768 | tf_op jit(solution)/shard_map/ppermute | solution.py:328
  95.1 4.5 %collective-permute-start.11 = (bf16[64,384]{1,0:T(8,128)(2,1)S(1)}, bf16[64,384]{1,0:T(8,128)(2,1)S(1)}, u32[]{:S(2)}, u32[]{:S(2)}) collective-permute-start(bf16[64,384]{1,0:T(8,128)(2,1)S(1)} %shard_map.82.a), channel_id=1, source_target_pairs={{0,4},{1,5},{2,6},{3,7},{4,0},{5,1},{6,2},{7,3},{8,12},{9,13},{10,... | collective-permute-start | bytes 147464 | tf_op jit(solution)/shard_map/ppermute | solution.py:323
  95.3 4.3 %collective-permute-start.10 = (bf16[64,384]{1,0:T(8,128)(2,1)S(1)}, bf16[64,384]{1,0:T(8,128)(2,1)S(1)}, u32[]{:S(2)}, u32[]{:S(2)}) collective-permute-start(bf16[64,384]{1,0:T(8,128)(2,1)S(1)} %shard_map.82.a), channel_id=1, source_target_pairs={{0,6},{1,7},{2,0},{3,1},{4,2},{5,3},{6,4},{7,5},{8,14},{9,15},{10,... | collective-permute-start | bytes 147464 | tf_op jit(solution)/shard_map/ppermute | solution.py:323
  96.8 4.4 %collective-permute-start.9 = (bf16[64,384]{1,0:T(8,128)(2,1)S(1)}, bf16[64,384]{1,0:T(8,128)(2,1)S(1)}, u32[]{:S(2)}, u32[]{:S(2)}) collective-permute-start(bf16[64,384]{1,0:T(8,128)(2,1)S(1)} %shard_map.82.a), channel_id=1, source_target_pairs={{0,2},{1,3},{2,4},{3,5},{4,6},{5,7},{6,0},{7,1},{8,10},{9,11},{10,... | collective-permute-start | bytes 147464 | tf_op jit(solution)/shard_map/ppermute | solution.py:323
  129.8 5.7 %collective-permute-start.12 = (f32[64,320]{1,0:T(8,128)S(1)}, f32[64,320]{1,0:T(8,128)S(1)}, u32[]{:S(2)}, u32[]{:S(2)}) collective-permute-start(f32[64,320]{1,0:T(8,128)S(1)} %shard_map.85.own), channel_id=1, source_target_pairs={{0,1},{1,0},{2,3},{3,2},{4,5},{5,4},{6,7},{7,6},{8,9},{9,8},{10,11... | collective-permute-start | bytes 245768 | tf_op jit(solution)/shard_map/ppermute | solution.py:328
  135.6 4.5 %collective-permute-start.15 = (bf16[64,384]{1,0:T(8,128)(2,1)S(1)}, bf16[64,384]{1,0:T(8,128)(2,1)S(1)}, u32[]{:S(2)}, u32[]{:S(2)}) collective-permute-start(bf16[64,384]{1,0:T(8,128)(2,1)S(1)} %shard_map.86.a), channel_id=1, source_target_pairs={{0,4},{1,5},{2,6},{3,7},{4,0},{5,1},{6,2},{7,3},{8,12},{9,13},{10,... | collective-permute-start | bytes 147464 | tf_op jit(solution)/shard_map/ppermute | solution.py:323
  135.6 4.4 %collective-permute-start.14 = (bf16[64,384]{1,0:T(8,128)(2,1)S(1)}, bf16[64,384]{1,0:T(8,128)(2,1)S(1)}, u32[]{:S(2)}, u32[]{:S(2)}) collective-permute-start(bf16[64,384]{1,0:T(8,128)(2,1)S(1)} %shard_map.86.a), channel_id=1, source_target_pairs={{0,6},{1,7},{2,0},{3,1},{4,2},{5,3},{6,4},{7,5},{8,14},{9,15},{10,... | collective-permute-start | bytes 147464 | tf_op jit(solution)/shard_map/ppermute | solution.py:323
  136.6 4.7 %collective-permute-start.13 = (bf16[64,384]{1,0:T(8,128)(2,1)S(1)}, bf16[64,384]{1,0:T(8,128)(2,1)S(1)}, u32[]{:S(2)}, u32[]{:S(2)}) collective-permute-start(bf16[64,384]{1,0:T(8,128)(2,1)S(1)} %shard_map.86.a), channel_id=1, source_target_pairs={{0,2},{1,3},{2,4},{3,5},{4,6},{5,7},{6,0},{7,1},{8,10},{9,11},{10,... | collective-permute-start | bytes 147464 | tf_op jit(solution)/shard_map/ppermute | solution.py:323
  170.0 5.0 %collective-permute-start.16 = (f32[64,320]{1,0:T(8,128)S(1)}, f32[64,320]{1,0:T(8,128)S(1)}, u32[]{:S(2)}, u32[]{:S(2)}) collective-permute-start(f32[64,320]{1,0:T(8,128)S(1)} %shard_map.89.own), channel_id=1, source_target_pairs={{0,1},{1,0},{2,3},{3,2},{4,5},{5,4},{6,7},{7,6},{8,9},{9,8},{10,11... | collective-permute-start | bytes 245768 | tf_op jit(solution)/shard_map/ppermute | solution.py:328
  175.1 11.5 %collective-permute-start.19 = (bf16[64,384]{1,0:T(8,128)(2,1)S(1)}, bf16[64,384]{1,0:T(8,128)(2,1)S(1)}, u32[]{:S(2)}, u32[]{:S(2)}) collective-permute-start(bf16[64,384]{1,0:T(8,128)(2,1)S(1)} %shard_map.90.a), channel_id=1, source_target_pairs={{0,4},{1,5},{2,6},{3,7},{4,0},{5,1},{6,2},{7,3},{8,12},{9,13},{10,... | collective-permute-start | bytes 147464 | tf_op jit(solution)/shard_map/ppermute | solution.py:323
  175.4 11.2 %collective-permute-start.18 = (bf16[64,384]{1,0:T(8,128)(2,1)S(1)}, bf16[64,384]{1,0:T(8,128)(2,1)S(1)}, u32[]{:S(2)}, u32[]{:S(2)}) collective-permute-start(bf16[64,384]{1,0:T(8,128)(2,1)S(1)} %shard_map.90.a), channel_id=1, source_target_pairs={{0,6},{1,7},{2,0},{3,1},{4,2},{5,3},{6,4},{7,5},{8,14},{9,15},{10,... | collective-permute-start | bytes 147464 | tf_op jit(solution)/shard_map/ppermute | solution.py:323
  176.6 13.8 %collective-permute-start.17 = (bf16[64,384]{1,0:T(8,128)(2,1)S(1)}, bf16[64,384]{1,0:T(8,128)(2,1)S(1)}, u32[]{:S(2)}, u32[]{:S(2)}) collective-permute-start(bf16[64,384]{1,0:T(8,128)(2,1)S(1)} %shard_map.90.a), channel_id=1, source_target_pairs={{0,2},{1,3},{2,4},{3,5},{4,6},{5,7},{6,0},{7,1},{8,10},{9,11},{10,... | collective-permute-start | bytes 147464 | tf_op jit(solution)/shard_map/ppermute | solution.py:323
  218.9 5.5 %collective-permute-start.20 = (f32[64,320]{1,0:T(8,128)S(1)}, f32[64,320]{1,0:T(8,128)S(1)}, u32[]{:S(2)}, u32[]{:S(2)}) collective-permute-start(f32[64,320]{1,0:T(8,128)S(1)} %shard_map.93.own), channel_id=1, source_target_pairs={{0,1},{1,0},{2,3},{3,2},{4,5},{5,4},{6,7},{7,6},{8,9},{9,8},{10,11... | collective-permute-start | bytes 245768 | tf_op jit(solution)/shard_map/ppermute | solution.py:328
  224.5 4.5 %collective-permute-start.23 = (bf16[64,384]{1,0:T(8,128)(2,1)S(1)}, bf16[64,384]{1,0:T(8,128)(2,1)S(1)}, u32[]{:S(2)}, u32[]{:S(2)}) collective-permute-start(bf16[64,384]{1,0:T(8,128)(2,1)S(1)} %shard_map.94.a), channel_id=1, source_target_pairs={{0,4},{1,5},{2,6},{3,7},{4,0},{5,1},{6,2},{7,3},{8,12},{9,13},{10,... | collective-permute-start | bytes 147464 | tf_op jit(solution)/shard_map/ppermute | solution.py:323
  225.4 3.6 %collective-permute-start.22 = (bf16[64,384]{1,0:T(8,128)(2,1)S(1)}, bf16[64,384]{1,0:T(8,128)(2,1)S(1)}, u32[]{:S(2)}, u32[]{:S(2)}) collective-permute-start(bf16[64,384]{1,0:T(8,128)(2,1)S(1)} %shard_map.94.a), channel_id=1, source_target_pairs={{0,6},{1,7},{2,0},{3,1},{4,2},{5,3},{6,4},{7,5},{8,14},{9,15},{10,... | collective-permute-start | bytes 147464 | tf_op jit(solution)/shard_map/ppermute | solution.py:323
  226.3 4.2 %collective-permute-start.21 = (bf16[64,384]{1,0:T(8,128)(2,1)S(1)}, bf16[64,384]{1,0:T(8,128)(2,1)S(1)}, u32[]{:S(2)}, u32[]{:S(2)}) collective-permute-start(bf16[64,384]{1,0:T(8,128)(2,1)S(1)} %shard_map.94.a), channel_id=1, source_target_pairs={{0,2},{1,3},{2,4},{3,5},{4,6},{5,7},{6,0},{7,1},{8,10},{9,11},{10,... | collective-permute-start | bytes 147464 | tf_op jit(solution)/shard_map/ppermute | solution.py:323
  233.7 26.5 %copy-start.3 = (bf16[512,1024]{1,0:T(8,128)(2,1)S(1)}, bf16[512,1024]{1,0:T(8,128)(2,1)}, u32[]{:S(2)}) copy-start(bf16[512,1024]{1,0:T(8,128)(2,1)} %prompts.1) | copy-start | bytes 3145732
  246.9 13.3 %all-to-all-start.11 = ((bf16[32,16,128]{2,1,0:T(8,128)(2,1)}), bf16[32,16,128]{2,1,0:T(8,128)(2,1)S(1)}, u32[]{:S(2)}, u32[]{:S(2)}) async-start(bf16[32,16,128]{2,1,0:T(8,128)(2,1)} %shard_map.96), calls=%async_computation.11 | async-start | bytes 262144 | tf_op jit(solution)/shard_map/all_to_all | solution.py:355
  276.1 7.1 %collective-permute-start.24 = (f32[64,704]{1,0:T(8,128)S(1)}, f32[64,704]{1,0:T(8,128)S(1)}, u32[]{:S(2)}, u32[]{:S(2)}) collective-permute-start(f32[64,704]{1,0:T(8,128)S(1)} %shard_map.98.own), channel_id=1, source_target_pairs={{0,1},{1,0},{2,3},{3,2},{4,5},{5,4},{6,7},{7,6},{8,9},{9,8},{10,11... | collective-permute-start | bytes 540680 | tf_op jit(solution)/shard_map/ppermute | solution.py:328
  283.3 5.5 %collective-permute-start.27 = (bf16[64,768]{1,0:T(8,128)(2,1)S(1)}, bf16[64,768]{1,0:T(8,128)(2,1)S(1)}, u32[]{:S(2)}, u32[]{:S(2)}) collective-permute-start(bf16[64,768]{1,0:T(8,128)(2,1)S(1)} %shard_map.99.a), channel_id=1, source_target_pairs={{0,4},{1,5},{2,6},{3,7},{4,0},{5,1},{6,2},{7,3},{8,12},{9,13},{10,... | collective-permute-start | bytes 294920 | tf_op jit(solution)/shard_map/ppermute | solution.py:323
  283.4 5.5 %collective-permute-start.26 = (bf16[64,768]{1,0:T(8,128)(2,1)S(1)}, bf16[64,768]{1,0:T(8,128)(2,1)S(1)}, u32[]{:S(2)}, u32[]{:S(2)}) collective-permute-start(bf16[64,768]{1,0:T(8,128)(2,1)S(1)} %shard_map.99.a), channel_id=1, source_target_pairs={{0,6},{1,7},{2,0},{3,1},{4,2},{5,3},{6,4},{7,5},{8,14},{9,15},{10,... | collective-permute-start | bytes 294920 | tf_op jit(solution)/shard_map/ppermute | solution.py:323
  285.1 5.9 %collective-permute-start.25 = (bf16[64,768]{1,0:T(8,128)(2,1)S(1)}, bf16[64,768]{1,0:T(8,128)(2,1)S(1)}, u32[]{:S(2)}, u32[]{:S(2)}) collective-permute-start(bf16[64,768]{1,0:T(8,128)(2,1)S(1)} %shard_map.99.a), channel_id=1, source_target_pairs={{0,2},{1,3},{2,4},{3,5},{4,6},{5,7},{6,0},{7,1},{8,10},{9,11},{10,... | collective-permute-start | bytes 294920 | tf_op jit(solution)/shard_map/ppermute | solution.py:323

commit v5 on v4

--- a/solution.py
+++ b/solution.py
@@ -206,6 +206,10 @@
     out[...] = jnp.concatenate([dot_nt(numer, stack[...]), dot_nt(numer, numer)], axis=1)
 
 
+def keep_body(value, out):
+    out[...] = value[...]
+
+
 def project_ids_body(tiles, stack, out, ids_out):
     project_body(tiles, stack, out)
     ids = summed(tiles.at[:, 16:])
@@ -331,7 +335,7 @@
 def over_feature(value, gram_size):
     rows, lanes = value.shape
     pair = call(pair_body, shape((rows, lanes + gram_size), BF), value, other_core(value))
-    return [pair] + [around_y(pair, d) for d in (1, 3, 2)]
+    return [pair] + [around_y(pair, d) for d in (2, 3, 1)]
 
 
 def on_device(adapter_down, adapter_up, fisher, init_v, init_u, prompt_rows, request_ids):
@@ -369,7 +373,8 @@
         init_v.T.astype(BF),
         init_u.T.astype(BF),
     )
-    parts, id_tile = lax.optimization_barrier((over_feature(value, 0), id_tile))
+    core = jnp.full((1,), lax.axis_index("feature") % CORES, jnp.int32)
+    parts, id_tile, core = lax.optimization_barrier((over_feature(value, 0), id_tile, core))
     tiles, q, p = call(first_body, [tile_shape, flat, flat], *parts, up, fisher_row)
     for sweep in range(SWEEPS):
         if sweep == 0:
@@ -383,9 +388,9 @@
                 up,
             )
             local_id = every_id[0, : ways * blocks] - position * fisher.shape[0]
-            parts, pick_rows = lax.optimization_barrier(
-                (over_feature(value, size), jnp.repeat(local_id, RANK)[:, None])
-            )
+            pick_rows = jnp.repeat(local_id, RANK)[:, None]
+            pick_rows = call(keep_body, shape(pick_rows.shape, jnp.int32), pick_rows)
+            parts, pick_rows = lax.optimization_barrier((over_feature(value, size), pick_rows))
         else:
             numer = reduced(tiles)
             parts = projected(numer, up)
@@ -403,7 +408,6 @@
                 fisher_row,
                 numer,
             )
-    core = jnp.full((1,), lax.axis_index("feature") % CORES, jnp.int32)
     packed = blocks * RANK * 3 // 4
     picked, hidden, gram = call(
         pick_body,

time: 300 us -> 300 us (level)
  blocking collectives: 161 us -> 174 us
  waiting for transfers between devices: 43.2 us -> 34.3 us
  starting transfers between devices: 60.1 us -> 57 us
    all_to_all x12 -> x13, blocking collectives: 161 us -> 174 us  [swap(): return lax.all_to_all(parts, 'adapter', 0, 0, tiled=True)]
    all_to_all x1 -> x0, waiting for transfers between devices: 9.02 us -> none  [swap(): return lax.all_to_all(parts, 'adapter', 0, 0, tiled=True)]
    all_to_all x1 -> x0, starting transfers between devices: 3.86 us -> none  [swap(): return lax.all_to_all(parts, 'adapter', 0, 0, tiled=True)]
    pallas_call x27 -> x28, Pallas kernels: 21.6 us -> 21 us  [call(): pl.pallas_call(body, out_shape=outs, in_specs=[scalar if arg.shape == (1,...]
  transfers between devices with their start and end apart: 29 -> 28, of which waited for: 22 -> 21; matrix products, arithmetic and copies ran while one was open for 0% -> 0% of each run, Pallas kernels for 0% -> 0%
where the time goes in v5:
time: 300 us; the launch traced here: 295 us
  blocking collectives  174 us (58%)
  starting transfers between devices  57 us (19%)
  waiting for transfers between devices  34.3 us (11%)
  Pallas kernels  25.3 us (8%)
  local copies, waits for them, and re-layouts  3.55 us (1%)
    all_to_all x13, blocking collectives, swap(): return lax.all_to_all(parts, 'adapter', 0, 0, tiled=True)  174 us
    ppermute x7, starting transfers between devices, other_core(): return lax.ppermute(value, 'feature', [(i, i ^ 1) for i in range(size)])  32.6 us
    ppermute x21, waiting for transfers between devices, around_y(): lax.ppermute(value, 'feature', [(i, (i + d * CORES) % size) for i in rang...  28.5 us
    ppermute x21, starting transfers between devices, around_y(): lax.ppermute(value, 'feature', [(i, (i + d * CORES) % size) for i in rang...  24.4 us
    pallas_call x28, Pallas kernels, call(): pl.pallas_call(body, out_shape=outs, in_specs=[scalar if arg.shape == (1,...  21 us
  transfers between devices with their start and end apart: 28, of which 21 were waited for; matrix products, arithmetic and copies ran while one was open for 0% of the time, Pallas kernels for 0%

profile of v5, /device:TPU:1, one launch (start us, length us, event | category | flops | bytes accessed | tf_op | source)
XLA Modules:
  0.0 295.4 jit_solution(9355756709164278121)
XLA Ops:
  0.0 1.1 convert_bitcast_fusion
  2.7 3.3 %collective-permute-start = (f32[64,512]{1,0:T(8,128)S(1)}, f32[64,512]{1,0:T(8,128)S(1)}, u32[]{:S(2)}, u32[]{:S(2)}) collective-permute-start(f32[64,512]{1,0:T(8,128)S(1)} %shard_map.73.own), channel_id=1, source_target_pairs={{0,1},{1,0},{2,3},{3,2},{4,5},{5,4},{6,7},{7,6},{8,9},{9,8},{10,11... | collective-permute-start | bytes 393224 | tf_op jit(solution)/shard_map/ppermute | solution.py:332
  7.5 1.3 collective-permute-start.1
  10.6 2.2 collective-permute-done.1.b
  14.9 20.2 %all_to_all.65.parts = bf16[32,16,128]{2,1,0:T(8,128)(2,1)S(1)} all-to-all(bf16[32,16,128]{2,1,0:T(8,128)(2,1)S(1)} %get-tuple-element.39), channel_id=1, replica_groups=mesh['adapter'=32,'feature'=8] {'adapter'}, dimensions={0} | all-to-all | bytes 262144 | tf_op jit(solution)/shard_map/all_to_all | solution.py:359
  35.1 13.7 %all_to_all.66.tiles = bf16[32,32,128]{2,1,0:T(8,128)(2,1)S(1)} all-to-all(bf16[32,32,128]{2,1,0:T(8,128)(2,1)S(1)} %shard_map.76), channel_id=1, replica_groups=mesh['adapter'=32,'feature'=8] {'adapter'}, dimensions={0} | all-to-all | bytes 524288 | tf_op jit(solution)/shard_map/all_to_all | solution.py:359
  49.1 4.3 %collective-permute-start.4 = (f32[64,320]{1,0:T(8,128)S(1)}, f32[64,320]{1,0:T(8,128)S(1)}, u32[]{:S(2)}, u32[]{:S(2)}) collective-permute-start(f32[64,320]{1,0:T(8,128)S(1)} %get-tuple-element.41.own), channel_id=1, source_target_pairs={{0,1},{1,0},{2,3},{3,2},{4,5},{5,4},{6,7},{7,6},{8,9},{9,8},{10,11... | collective-permute-start | bytes 245768 | tf_op jit(solution)/shard_map/ppermute | solution.py:332
  54.5 1.1 collective-permute-start.5
  57.9 1.1 collective-permute-done.5.b
  59.2 1.6 collective-permute-done.7.d
  60.8 3.1 %shard_map.80 = (bf16[32,16,128]{2,1,0:T(8,128)(2,1)S(1)}, f32[64,256]{1,0:T(8,128)S(1)}) custom-call(bf16[64,384]{1,0:T(8,128)(2,1)S(1)} %shard_map.78.a, bf16[64,384]{1,0:T(8,128)(2,1)S(1)} %collective-permute-done.5.b, bf16[64,384]{1,0:T(8,128)(2,1)S(1)} %collective-permute-done.6.c, bf16[64,384]{1,0:T(8,128)(2,1)S(1)} %collective-permute-done.7.d, ...), custom_call_target="tpu_custom_call" | custom-call | tf_op jit(solution)/shard_map/pallas_call | solution.py:19
  63.9 12.4 %all_to_all.67.parts = bf16[32,16,128]{2,1,0:T(8,128)(2,1)S(1)} all-to-all(bf16[32,16,128]{2,1,0:T(8,128)(2,1)S(1)} %get-tuple-element.48), channel_id=1, replica_groups=mesh['adapter'=32,'feature'=8] {'adapter'}, dimensions={0} | all-to-all | bytes 262144 | tf_op jit(solution)/shard_map/all_to_all | solution.py:359
  76.4 12.6 %all_to_all.68.tiles = bf16[32,16,128]{2,1,0:T(8,128)(2,1)S(1)} all-to-all(bf16[32,16,128]{2,1,0:T(8,128)(2,1)S(1)} %shard_map.81), channel_id=1, replica_groups=mesh['adapter'=32,'feature'=8] {'adapter'}, dimensions={0} | all-to-all | bytes 262144 | tf_op jit(solution)/shard_map/all_to_all | solution.py:359
  89.4 4.7 %collective-permute-start.8 = (f32[64,320]{1,0:T(8,128)S(1)}, f32[64,320]{1,0:T(8,128)S(1)}, u32[]{:S(2)}, u32[]{:S(2)}) collective-permute-start(f32[64,320]{1,0:T(8,128)S(1)} %shard_map.82.own), channel_id=1, source_target_pairs={{0,1},{1,0},{2,3},{3,2},{4,5},{5,4},{6,7},{7,6},{8,9},{9,8},{10,11... | collective-permute-start | bytes 245768 | tf_op jit(solution)/shard_map/ppermute | solution.py:332
  95.3 1.5 collective-permute-start.11
  97.0 1.1 collective-permute-done.10.c
  98.1 1.6 collective-permute-done.11.d
  99.7 1.6 collective-permute-done.9.b
  101.4 3.1 %shard_map.84 = (bf16[32,16,128]{2,1,0:T(8,128)(2,1)S(1)}, f32[64,256]{1,0:T(8,128)S(1)}) custom-call(bf16[64,384]{1,0:T(8,128)(2,1)S(1)} %shard_map.83.a, bf16[64,384]{1,0:T(8,128)(2,1)S(1)} %collective-permute-done.9.b, bf16[64,384]{1,0:T(8,128)(2,1)S(1)} %collective-permute-done.10.c, bf16[64,384]{1,0:T(8,128)(2,1)S(1)} %collective-permute-done.11.d, ...), custom_call_target="tpu_custom_call" | custom-call | tf_op jit(solution)/shard_map/pallas_call | solution.py:19
  104.5 12.4 %all_to_all.69.parts = bf16[32,16,128]{2,1,0:T(8,128)(2,1)S(1)} all-to-all(bf16[32,16,128]{2,1,0:T(8,128)(2,1)S(1)} %get-tuple-element.50), channel_id=1, replica_groups=mesh['adapter'=32,'feature'=8] {'adapter'}, dimensions={0} | all-to-all | bytes 262144 | tf_op jit(solution)/shard_map/all_to_all | solution.py:359
  116.9 12.6 %all_to_all.70.tiles = bf16[32,16,128]{2,1,0:T(8,128)(2,1)S(1)} all-to-all(bf16[32,16,128]{2,1,0:T(8,128)(2,1)S(1)} %shard_map.85), channel_id=1, replica_groups=mesh['adapter'=32,'feature'=8] {'adapter'}, dimensions={0} | all-to-all | bytes 262144 | tf_op jit(solution)/shard_map/all_to_all | solution.py:359
  129.9 4.7 %collective-permute-start.12 = (f32[64,320]{1,0:T(8,128)S(1)}, f32[64,320]{1,0:T(8,128)S(1)}, u32[]{:S(2)}, u32[]{:S(2)}) collective-permute-start(f32[64,320]{1,0:T(8,128)S(1)} %shard_map.86.own), channel_id=1, source_target_pairs={{0,1},{1,0},{2,3},{3,2},{4,5},{5,4},{6,7},{7,6},{8,9},{9,8},{10,11... | collective-permute-start | bytes 245768 | tf_op jit(solution)/shard_map/ppermute | solution.py:332
  135.8 2.0 collective-permute-start.14
  137.8 2.3 collective-permute-done.13.b
  140.1 1.8 collective-permute-done.15.d
  142.0 3.1 %shard_map.88 = (bf16[32,16,128]{2,1,0:T(8,128)(2,1)S(1)}, f32[64,256]{1,0:T(8,128)S(1)}) custom-call(bf16[64,384]{1,0:T(8,128)(2,1)S(1)} %shard_map.87.a, bf16[64,384]{1,0:T(8,128)(2,1)S(1)} %collective-permute-done.13.b, bf16[64,384]{1,0:T(8,128)(2,1)S(1)} %collective-permute-done.14.c, bf16[64,384]{1,0:T(8,128)(2,1)S(1)} %collective-permute-done.15.d, ...), custom_call_target="tpu_custom_call" | custom-call | tf_op jit(solution)/shard_map/pallas_call | solution.py:19
  145.1 12.4 %all_to_all.71.parts = bf16[32,16,128]{2,1,0:T(8,128)(2,1)S(1)} all-to-all(bf16[32,16,128]{2,1,0:T(8,128)(2,1)S(1)} %get-tuple-element.52), channel_id=1, replica_groups=mesh['adapter'=32,'feature'=8] {'adapter'}, dimensions={0} | all-to-all | bytes 262144 | tf_op jit(solution)/shard_map/all_to_all | solution.py:359
  157.6 12.6 %all_to_all.72.tiles = bf16[32,16,128]{2,1,0:T(8,128)(2,1)S(1)} all-to-all(bf16[32,16,128]{2,1,0:T(8,128)(2,1)S(1)} %shard_map.89), channel_id=1, replica_groups=mesh['adapter'=32,'feature'=8] {'adapter'}, dimensions={0} | all-to-all | bytes 262144 | tf_op jit(solution)/shard_map/all_to_all | solution.py:359
  170.6 4.7 %collective-permute-start.16 = (f32[64,320]{1,0:T(8,128)S(1)}, f32[64,320]{1,0:T(8,128)S(1)}, u32[]{:S(2)}, u32[]{:S(2)}) collective-permute-start(f32[64,320]{1,0:T(8,128)S(1)} %shard_map.90.own), channel_id=1, source_target_pairs={{0,1},{1,0},{2,3},{3,2},{4,5},{5,4},{6,7},{7,6},{8,9},{9,8},{10,11... | collective-permute-start | bytes 245768 | tf_op jit(solution)/shard_map/ppermute | solution.py:332
  177.3 10.3 %collective-permute-start.19 = (bf16[64,384]{1,0:T(8,128)(2,1)S(1)}, bf16[64,384]{1,0:T(8,128)(2,1)S(1)}, u32[]{:S(2)}, u32[]{:S(2)}) collective-permute-start(bf16[64,384]{1,0:T(8,128)(2,1)S(1)} %shard_map.91.a), channel_id=1, source_target_pairs={{0,2},{1,3},{2,4},{3,5},{4,6},{5,7},{6,0},{7,1},{8,10},{9,11},{10,... | collective-permute-start | bytes 147464 | tf_op jit(solution)/shard_map/ppermute | solution.py:327
  187.6 3.4 %collective-permute-done.19.d = bf16[64,384]{1,0:T(8,128)(2,1)S(1)} collective-permute-done((bf16[64,384]{1,0:T(8,128)(2,1)S(1)}, bf16[64,384]{1,0:T(8,128)(2,1)S(1)}, u32[]{:S(2)}, u32[]{:S(2)}) %collective-permute-start.19) | collective-permute-done | bytes 49184 | tf_op jit(solution)/shard_map/ppermute | solution.py:327
  191.0 3.1 %shard_map.92 = (bf16[32,16,128]{2,1,0:T(8,128)(2,1)S(1)}, f32[64,256]{1,0:T(8,128)S(1)}) custom-call(bf16[64,384]{1,0:T(8,128)(2,1)S(1)} %shard_map.91.a, bf16[64,384]{1,0:T(8,128)(2,1)S(1)} %collective-permute-done.17.b, bf16[64,384]{1,0:T(8,128)(2,1)S(1)} %collective-permute-done.18.c, bf16[64,384]{1,0:T(8,128)(2,1)S(1)} %collective-permute-done.19.d, ...), custom_call_target="tpu_custom_call" | custom-call | tf_op jit(solution)/shard_map/pallas_call | solution.py:19
  194.1 12.3 %all_to_all.73.parts = bf16[32,16,128]{2,1,0:T(8,128)(2,1)S(1)} all-to-all(bf16[32,16,128]{2,1,0:T(8,128)(2,1)S(1)} %get-tuple-element.54), channel_id=1, replica_groups=mesh['adapter'=32,'feature'=8] {'adapter'}, dimensions={0} | all-to-all | bytes 262144 | tf_op jit(solution)/shard_map/all_to_all | solution.py:359
  206.5 12.6 %all_to_all.74.tiles.numer_tiles = bf16[32,16,128]{2,1,0:T(8,128)(2,1)S(1)} all-to-all(bf16[32,16,128]{2,1,0:T(8,128)(2,1)S(1)} %shard_map.93), channel_id=1, replica_groups=mesh['adapter'=32,'feature'=8] {'adapter'}, dimensions={0} | all-to-all | bytes 262144 | tf_op jit(solution)/shard_map/all_to_all | solution.py:359
  219.5 4.7 %collective-permute-start.20 = (f32[64,320]{1,0:T(8,128)S(1)}, f32[64,320]{1,0:T(8,128)S(1)}, u32[]{:S(2)}, u32[]{:S(2)}) collective-permute-start(f32[64,320]{1,0:T(8,128)S(1)} %shard_map.94.own), channel_id=1, source_target_pairs={{0,1},{1,0},{2,3},{3,2},{4,5},{5,4},{6,7},{7,6},{8,9},{9,8},{10,11... | collective-permute-start | bytes 245768 | tf_op jit(solution)/shard_map/ppermute | solution.py:332
  225.8 1.5 collective-permute-start.22
  227.3 2.4 collective-permute-done.21.b
  229.7 1.7 collective-permute-done.23.d
  231.5 3.2 %shard_map.96 = (bf16[32,16,128]{2,1,0:T(8,128)(2,1)S(1)}, f32[64,256]{1,0:T(8,128)S(1)}, bf16[64,1024]{1,0:T(8,128)(2,1)S(1)}) custom-call(bf16[64,384]{1,0:T(8,128)(2,1)S(1)} %shard_map.95.a, bf16[64,384]{1,0:T(8,128)(2,1)S(1)} %collective-permute-done.21.b, bf16[64,384]{1,0:T(8,128)(2,1)S(1)} %collective-permute-done.22.c, ...), custom_call_target="tpu_custom_call" | custom-call | tf_op jit(solution)/shard_map/pallas_call | solution.py:19
  234.7 12.4 %all_to_all.75.parts = bf16[32,16,128]{2,1,0:T(8,128)(2,1)S(1)} all-to-all(bf16[32,16,128]{2,1,0:T(8,128)(2,1)S(1)} %get-tuple-element.56), channel_id=1, replica_groups=mesh['adapter'=32,'feature'=8] {'adapter'}, dimensions={0} | all-to-all | bytes 262144 | tf_op jit(solution)/shard_map/all_to_all | solution.py:359
  247.1 12.6 %all_to_all.76.tiles = bf16[32,16,128]{2,1,0:T(8,128)(2,1)S(1)} all-to-all(bf16[32,16,128]{2,1,0:T(8,128)(2,1)S(1)} %shard_map.97), channel_id=1, replica_groups=mesh['adapter'=32,'feature'=8] {'adapter'}, dimensions={0} | all-to-all | bytes 262144 | tf_op jit(solution)/shard_map/all_to_all | solution.py:359
  259.7 1.1 shard_map.98
  260.9 14.7 %all_to_all.77.parts = bf16[32,48,128]{2,1,0:T(8,128)(2,1)S(1)} all-to-all(bf16[32,48,128]{2,1,0:T(8,128)(2,1)S(1)} %get-tuple-element.59), channel_id=1, replica_groups=mesh['adapter'=32,'feature'=8] {'adapter'}, dimensions={0} | all-to-all | bytes 786432 | tf_op jit(solution)/shard_map/all_to_all | solution.py:359
  275.7 6.1 %collective-permute-start.24 = (f32[64,704]{1,0:T(8,128)S(1)}, f32[64,704]{1,0:T(8,128)S(1)}, u32[]{:S(2)}, u32[]{:S(2)}) collective-permute-start(f32[64,704]{1,0:T(8,128)S(1)} %shard_map.99.own), channel_id=1, source_target_pairs={{0,1},{1,0},{2,3},{3,2},{4,5},{5,4},{6,7},{7,6},{8,9},{9,8},{10,11... | collective-permute-start | bytes 540680 | tf_op jit(solution)/shard_map/ppermute | solution.py:332
  281.8 1.1 collective-permute-done.24.got
  284.7 3.8 %collective-permute-done.25.b = bf16[64,768]{1,0:T(8,128)(2,1)S(1)} collective-permute-done((bf16[64,768]{1,0:T(8,128)(2,1)S(1)}, bf16[64,768]{1,0:T(8,128)(2,1)S(1)}, u32[]{:S(2)}, u32[]{:S(2)}) %collective-permute-start.25) | collective-permute-done | bytes 98336 | tf_op jit(solution)/shard_map/ppermute | solution.py:327
  288.5 2.4 collective-permute-done.27.d
  290.9 4.3 %shard_map.101 = bf16[512,1024]{1,0:T(8,128)(2,1)} custom-call(bf16[64,768]{1,0:T(8,128)(2,1)S(1)} %shard_map.100.a, bf16[64,768]{1,0:T(8,128)(2,1)S(1)} %collective-permute-done.25.b, bf16[64,768]{1,0:T(8,128)(2,1)S(1)} %collective-permute-done.26.c, bf16[64,768]{1,0:T(8,128)(2,1)S(1)} %collective-permute-done.27.d, ...), custom_call_target="tpu_custom_call" | custom-call | tf_op jit(solution)/shard_map/pallas_call | solution.py:427
  (72 shorter events, 20.4 us)
Async XLA Ops:
  0.0 1.2 copy-start
  1.2 1.0 copy-start.1
  2.7 4.8 %collective-permute-start = (f32[64,512]{1,0:T(8,128)S(1)}, f32[64,512]{1,0:T(8,128)S(1)}, u32[]{:S(2)}, u32[]{:S(2)}) collective-permute-start(f32[64,512]{1,0:T(8,128)S(1)} %shard_map.73.own), channel_id=1, source_target_pairs={{0,1},{1,0},{2,3},{3,2},{4,5},{5,4},{6,7},{7,6},{8,9},{9,8},{10,11... | collective-permute-start | bytes 393224 | tf_op jit(solution)/shard_map/ppermute | solution.py:332
  6.0 0.7 copy-start.4
  6.8 0.7 copy-start.5
  7.5 5.3 %collective-permute-start.1 = (bf16[64,512]{1,0:T(8,128)(2,1)S(1)}, bf16[64,512]{1,0:T(8,128)(2,1)S(1)}, u32[]{:S(2)}, u32[]{:S(2)}) collective-permute-start(bf16[64,512]{1,0:T(8,128)(2,1)S(1)} %shard_map.74.a), channel_id=1, source_target_pairs={{0,4},{1,5},{2,6},{3,7},{4,0},{5,1},{6,2},{7,3},{8,12},{9,13},{10,... | collective-permute-start | bytes 196616 | tf_op jit(solution)/shard_map/ppermute | solution.py:327
  8.8 4.0 %collective-permute-start.2 = (bf16[64,512]{1,0:T(8,128)(2,1)S(1)}, bf16[64,512]{1,0:T(8,128)(2,1)S(1)}, u32[]{:S(2)}, u32[]{:S(2)}) collective-permute-start(bf16[64,512]{1,0:T(8,128)(2,1)S(1)} %shard_map.74.a), channel_id=1, source_target_pairs={{0,6},{1,7},{2,0},{3,1},{4,2},{5,3},{6,4},{7,5},{8,14},{9,15},{10,... | collective-permute-start | bytes 196616 | tf_op jit(solution)/shard_map/ppermute | solution.py:327
  9.6 4.3 %collective-permute-start.3 = (bf16[64,512]{1,0:T(8,128)(2,1)S(1)}, bf16[64,512]{1,0:T(8,128)(2,1)S(1)}, u32[]{:S(2)}, u32[]{:S(2)}) collective-permute-start(bf16[64,512]{1,0:T(8,128)(2,1)S(1)} %shard_map.74.a), channel_id=1, source_target_pairs={{0,2},{1,3},{2,4},{3,5},{4,6},{5,7},{6,0},{7,1},{8,10},{9,11},{10,... | collective-permute-start | bytes 196616 | tf_op jit(solution)/shard_map/ppermute | solution.py:327
  49.1 5.3 %collective-permute-start.4 = (f32[64,320]{1,0:T(8,128)S(1)}, f32[64,320]{1,0:T(8,128)S(1)}, u32[]{:S(2)}, u32[]{:S(2)}) collective-permute-start(f32[64,320]{1,0:T(8,128)S(1)} %get-tuple-element.41.own), channel_id=1, source_target_pairs={{0,1},{1,0},{2,3},{3,2},{4,5},{5,4},{6,7},{7,6},{8,9},{9,8},{10,11... | collective-permute-start | bytes 245768 | tf_op jit(solution)/shard_map/ppermute | solution.py:332
  54.5 4.5 %collective-permute-start.5 = (bf16[64,384]{1,0:T(8,128)(2,1)S(1)}, bf16[64,384]{1,0:T(8,128)(2,1)S(1)}, u32[]{:S(2)}, u32[]{:S(2)}) collective-permute-start(bf16[64,384]{1,0:T(8,128)(2,1)S(1)} %shard_map.78.a), channel_id=1, source_target_pairs={{0,4},{1,5},{2,6},{3,7},{4,0},{5,1},{6,2},{7,3},{8,12},{9,13},{10,... | collective-permute-start | bytes 147464 | tf_op jit(solution)/shard_map/ppermute | solution.py:327
  55.6 3.6 %collective-permute-start.6 = (bf16[64,384]{1,0:T(8,128)(2,1)S(1)}, bf16[64,384]{1,0:T(8,128)(2,1)S(1)}, u32[]{:S(2)}, u32[]{:S(2)}) collective-permute-start(bf16[64,384]{1,0:T(8,128)(2,1)S(1)} %shard_map.78.a), channel_id=1, source_target_pairs={{0,6},{1,7},{2,0},{3,1},{4,2},{5,3},{6,4},{7,5},{8,14},{9,15},{10,... | collective-permute-start | bytes 147464 | tf_op jit(solution)/shard_map/ppermute | solution.py:327
  56.6 4.2 %collective-permute-start.7 = (bf16[64,384]{1,0:T(8,128)(2,1)S(1)}, bf16[64,384]{1,0:T(8,128)(2,1)S(1)}, u32[]{:S(2)}, u32[]{:S(2)}) collective-permute-start(bf16[64,384]{1,0:T(8,128)(2,1)S(1)} %shard_map.78.a), channel_id=1, source_target_pairs={{0,2},{1,3},{2,4},{3,5},{4,6},{5,7},{6,0},{7,1},{8,10},{9,11},{10,... | collective-permute-start | bytes 147464 | tf_op jit(solution)/shard_map/ppermute | solution.py:327
  57.8 3.0 %copy-start.2 = (bf16[16,16,1024]{2,1,0:T(8,128)(2,1)S(1)}, bf16[16,16,1024]{2,1,0:T(8,128)(2,1)}, u32[]{:S(2)}) copy-start(bf16[16,16,1024]{2,1,0:T(8,128)(2,1)} %param.7) | copy-start | bytes 1572868
  89.4 5.7 %collective-permute-start.8 = (f32[64,320]{1,0:T(8,128)S(1)}, f32[64,320]{1,0:T(8,128)S(1)}, u32[]{:S(2)}, u32[]{:S(2)}) collective-permute-start(f32[64,320]{1,0:T(8,128)S(1)} %shard_map.82.own), channel_id=1, source_target_pairs={{0,1},{1,0},{2,3},{3,2},{4,5},{5,4},{6,7},{7,6},{8,9},{9,8},{10,11... | collective-permute-start | bytes 245768 | tf_op jit(solution)/shard_map/ppermute | solution.py:332
  95.1 3.0 %collective-permute-start.10 = (bf16[64,384]{1,0:T(8,128)(2,1)S(1)}, bf16[64,384]{1,0:T(8,128)(2,1)S(1)}, u32[]{:S(2)}, u32[]{:S(2)}) collective-permute-start(bf16[64,384]{1,0:T(8,128)(2,1)S(1)} %shard_map.83.a), channel_id=1, source_target_pairs={{0,6},{1,7},{2,0},{3,1},{4,2},{5,3},{6,4},{7,5},{8,14},{9,15},{10,... | collective-permute-start | bytes 147464 | tf_op jit(solution)/shard_map/ppermute | solution.py:327
  95.3 4.4 %collective-permute-start.11 = (bf16[64,384]{1,0:T(8,128)(2,1)S(1)}, bf16[64,384]{1,0:T(8,128)(2,1)S(1)}, u32[]{:S(2)}, u32[]{:S(2)}) collective-permute-start(bf16[64,384]{1,0:T(8,128)(2,1)S(1)} %shard_map.83.a), channel_id=1, source_target_pairs={{0,2},{1,3},{2,4},{3,5},{4,6},{5,7},{6,0},{7,1},{8,10},{9,11},{10,... | collective-permute-start | bytes 147464 | tf_op jit(solution)/shard_map/ppermute | solution.py:327
  96.9 4.5 %collective-permute-start.9 = (bf16[64,384]{1,0:T(8,128)(2,1)S(1)}, bf16[64,384]{1,0:T(8,128)(2,1)S(1)}, u32[]{:S(2)}, u32[]{:S(2)}) collective-permute-start(bf16[64,384]{1,0:T(8,128)(2,1)S(1)} %shard_map.83.a), channel_id=1, source_target_pairs={{0,4},{1,5},{2,6},{3,7},{4,0},{5,1},{6,2},{7,3},{8,12},{9,13},{10,... | collective-permute-start | bytes 147464 | tf_op jit(solution)/shard_map/ppermute | solution.py:327
  129.9 5.7 %collective-permute-start.12 = (f32[64,320]{1,0:T(8,128)S(1)}, f32[64,320]{1,0:T(8,128)S(1)}, u32[]{:S(2)}, u32[]{:S(2)}) collective-permute-start(f32[64,320]{1,0:T(8,128)S(1)} %shard_map.86.own), channel_id=1, source_target_pairs={{0,1},{1,0},{2,3},{3,2},{4,5},{5,4},{6,7},{7,6},{8,9},{9,8},{10,11... | collective-permute-start | bytes 245768 | tf_op jit(solution)/shard_map/ppermute | solution.py:332
  135.7 4.5 %collective-permute-start.13 = (bf16[64,384]{1,0:T(8,128)(2,1)S(1)}, bf16[64,384]{1,0:T(8,128)(2,1)S(1)}, u32[]{:S(2)}, u32[]{:S(2)}) collective-permute-start(bf16[64,384]{1,0:T(8,128)(2,1)S(1)} %shard_map.87.a), channel_id=1, source_target_pairs={{0,4},{1,5},{2,6},{3,7},{4,0},{5,1},{6,2},{7,3},{8,12},{9,13},{10,... | collective-permute-start | bytes 147464 | tf_op jit(solution)/shard_map/ppermute | solution.py:327
  135.8 4.3 %collective-permute-start.14 = (bf16[64,384]{1,0:T(8,128)(2,1)S(1)}, bf16[64,384]{1,0:T(8,128)(2,1)S(1)}, u32[]{:S(2)}, u32[]{:S(2)}) collective-permute-start(bf16[64,384]{1,0:T(8,128)(2,1)S(1)} %shard_map.87.a), channel_id=1, source_target_pairs={{0,6},{1,7},{2,0},{3,1},{4,2},{5,3},{6,4},{7,5},{8,14},{9,15},{10,... | collective-permute-start | bytes 147464 | tf_op jit(solution)/shard_map/ppermute | solution.py:327
  137.8 4.2 %collective-permute-start.15 = (bf16[64,384]{1,0:T(8,128)(2,1)S(1)}, bf16[64,384]{1,0:T(8,128)(2,1)S(1)}, u32[]{:S(2)}, u32[]{:S(2)}) collective-permute-start(bf16[64,384]{1,0:T(8,128)(2,1)S(1)} %shard_map.87.a), channel_id=1, source_target_pairs={{0,2},{1,3},{2,4},{3,5},{4,6},{5,7},{6,0},{7,1},{8,10},{9,11},{10,... | collective-permute-start | bytes 147464 | tf_op jit(solution)/shard_map/ppermute | solution.py:327
  170.6 5.7 %collective-permute-start.16 = (f32[64,320]{1,0:T(8,128)S(1)}, f32[64,320]{1,0:T(8,128)S(1)}, u32[]{:S(2)}, u32[]{:S(2)}) collective-permute-start(f32[64,320]{1,0:T(8,128)S(1)} %shard_map.90.own), channel_id=1, source_target_pairs={{0,1},{1,0},{2,3},{3,2},{4,5},{5,4},{6,7},{7,6},{8,9},{9,8},{10,11... | collective-permute-start | bytes 245768 | tf_op jit(solution)/shard_map/ppermute | solution.py:332
  176.3 11.3 %collective-permute-start.17 = (bf16[64,384]{1,0:T(8,128)(2,1)S(1)}, bf16[64,384]{1,0:T(8,128)(2,1)S(1)}, u32[]{:S(2)}, u32[]{:S(2)}) collective-permute-start(bf16[64,384]{1,0:T(8,128)(2,1)S(1)} %shard_map.91.a), channel_id=1, source_target_pairs={{0,4},{1,5},{2,6},{3,7},{4,0},{5,1},{6,2},{7,3},{8,12},{9,13},{10,... | collective-permute-start | bytes 147464 | tf_op jit(solution)/shard_map/ppermute | solution.py:327
  176.6 11.0 %collective-permute-start.18 = (bf16[64,384]{1,0:T(8,128)(2,1)S(1)}, bf16[64,384]{1,0:T(8,128)(2,1)S(1)}, u32[]{:S(2)}, u32[]{:S(2)}) collective-permute-start(bf16[64,384]{1,0:T(8,128)(2,1)S(1)} %shard_map.91.a), channel_id=1, source_target_pairs={{0,6},{1,7},{2,0},{3,1},{4,2},{5,3},{6,4},{7,5},{8,14},{9,15},{10,... | collective-permute-start | bytes 147464 | tf_op jit(solution)/shard_map/ppermute | solution.py:327
  177.3 13.7 %collective-permute-start.19 = (bf16[64,384]{1,0:T(8,128)(2,1)S(1)}, bf16[64,384]{1,0:T(8,128)(2,1)S(1)}, u32[]{:S(2)}, u32[]{:S(2)}) collective-permute-start(bf16[64,384]{1,0:T(8,128)(2,1)S(1)} %shard_map.91.a), channel_id=1, source_target_pairs={{0,2},{1,3},{2,4},{3,5},{4,6},{5,7},{6,0},{7,1},{8,10},{9,11},{10,... | collective-permute-start | bytes 147464 | tf_op jit(solution)/shard_map/ppermute | solution.py:327
  219.5 40.2 %copy-start.3 = (bf16[512,1024]{1,0:T(8,128)(2,1)S(1)}, bf16[512,1024]{1,0:T(8,128)(2,1)}, u32[]{:S(2)}) copy-start(bf16[512,1024]{1,0:T(8,128)(2,1)} %prompts.1) | copy-start | bytes 3145732
  219.5 5.7 %collective-permute-start.20 = (f32[64,320]{1,0:T(8,128)S(1)}, f32[64,320]{1,0:T(8,128)S(1)}, u32[]{:S(2)}, u32[]{:S(2)}) collective-permute-start(f32[64,320]{1,0:T(8,128)S(1)} %shard_map.94.own), channel_id=1, source_target_pairs={{0,1},{1,0},{2,3},{3,2},{4,5},{5,4},{6,7},{7,6},{8,9},{9,8},{10,11... | collective-permute-start | bytes 245768 | tf_op jit(solution)/shard_map/ppermute | solution.py:332
  225.2 4.5 %collective-permute-start.21 = (bf16[64,384]{1,0:T(8,128)(2,1)S(1)}, bf16[64,384]{1,0:T(8,128)(2,1)S(1)}, u32[]{:S(2)}, u32[]{:S(2)}) collective-permute-start(bf16[64,384]{1,0:T(8,128)(2,1)S(1)} %shard_map.95.a), channel_id=1, source_target_pairs={{0,4},{1,5},{2,6},{3,7},{4,0},{5,1},{6,2},{7,3},{8,12},{9,13},{10,... | collective-permute-start | bytes 147464 | tf_op jit(solution)/shard_map/ppermute | solution.py:327
  225.8 3.9 %collective-permute-start.22 = (bf16[64,384]{1,0:T(8,128)(2,1)S(1)}, bf16[64,384]{1,0:T(8,128)(2,1)S(1)}, u32[]{:S(2)}, u32[]{:S(2)}) collective-permute-start(bf16[64,384]{1,0:T(8,128)(2,1)S(1)} %shard_map.95.a), channel_id=1, source_target_pairs={{0,6},{1,7},{2,0},{3,1},{4,2},{5,3},{6,4},{7,5},{8,14},{9,15},{10,... | collective-permute-start | bytes 147464 | tf_op jit(solution)/shard_map/ppermute | solution.py:327
  227.3 4.2 %collective-permute-start.23 = (bf16[64,384]{1,0:T(8,128)(2,1)S(1)}, bf16[64,384]{1,0:T(8,128)(2,1)S(1)}, u32[]{:S(2)}, u32[]{:S(2)}) collective-permute-start(bf16[64,384]{1,0:T(8,128)(2,1)S(1)} %shard_map.95.a), channel_id=1, source_target_pairs={{0,2},{1,3},{2,4},{3,5},{4,6},{5,7},{6,0},{7,1},{8,10},{9,11},{10,... | collective-permute-start | bytes 147464 | tf_op jit(solution)/shard_map/ppermute | solution.py:327
  275.7 7.1 %collective-permute-start.24 = (f32[64,704]{1,0:T(8,128)S(1)}, f32[64,704]{1,0:T(8,128)S(1)}, u32[]{:S(2)}, u32[]{:S(2)}) collective-permute-start(f32[64,704]{1,0:T(8,128)S(1)} %shard_map.99.own), channel_id=1, source_target_pairs={{0,1},{1,0},{2,3},{3,2},{4,5},{5,4},{6,7},{7,6},{8,9},{9,8},{10,11... | collective-permute-start | bytes 540680 | tf_op jit(solution)/shard_map/ppermute | solution.py:332
  282.9 5.5 %collective-permute-start.25 = (bf16[64,768]{1,0:T(8,128)(2,1)S(1)}, bf16[64,768]{1,0:T(8,128)(2,1)S(1)}, u32[]{:S(2)}, u32[]{:S(2)}) collective-permute-start(bf16[64,768]{1,0:T(8,128)(2,1)S(1)} %shard_map.100.a), channel_id=1, source_target_pairs={{0,4},{1,5},{2,6},{3,7},{4,0},{5,1},{6,2},{7,3},{8,12},{9,13},{10,... | collective-permute-start | bytes 294920 | tf_op jit(solution)/shard_map/ppermute | solution.py:327
  283.2 5.3 %collective-permute-start.26 = (bf16[64,768]{1,0:T(8,128)(2,1)S(1)}, bf16[64,768]{1,0:T(8,128)(2,1)S(1)}, u32[]{:S(2)}, u32[]{:S(2)}) collective-permute-start(bf16[64,768]{1,0:T(8,128)(2,1)S(1)} %shard_map.100.a), channel_id=1, source_target_pairs={{0,6},{1,7},{2,0},{3,1},{4,2},{5,3},{6,4},{7,5},{8,14},{9,15},{10,... | collective-permute-start | bytes 294920 | tf_op jit(solution)/shard_map/ppermute | solution.py:327
  284.1 6.7 %collective-permute-start.27 = (bf16[64,768]{1,0:T(8,128)(2,1)S(1)}, bf16[64,768]{1,0:T(8,128)(2,1)S(1)}, u32[]{:S(2)}, u32[]{:S(2)}) collective-permute-start(bf16[64,768]{1,0:T(8,128)(2,1)S(1)} %shard_map.100.a), channel_id=1, source_target_pairs={{0,2},{1,3},{2,4},{3,5},{4,6},{5,7},{6,0},{7,1},{8,10},{9,11},{10,... | collective-permute-start | bytes 294920 | tf_op jit(solution)/shard_map/ppermute | solution.py:327

commit v6 on v5

--- a/solution.py
+++ b/solution.py
@@ -176,11 +176,10 @@
         out[...] = jnp.concatenate([total[:, :plain].astype(BF), halves(total[:, plain:])], axis=1)
 
 
-def first_body(a, b, c, d, stack, fisher_row, tiles, q_out, p_out):
+def first_body(a, b, c, d, stack, fisher_row, tiles, p_out):
     total = added((a, b, c, d))
     count = total.shape[1] // 2
     q, p = total[:, :count], total[:, count:]
-    q_out[...] = q
     p_out[...] = p
     terms = weighted_terms(p, q, fisher_row[...])
     write_tiles(tiles, dot_nn(terms, stack[...]))
@@ -332,10 +331,10 @@
     return lax.ppermute(value, "feature", [(i, i ^ 1) for i in range(size)])
 
 
-def over_feature(value, gram_size):
+def over_feature(value, gram_size, steps=(2, 3, 1)):
     rows, lanes = value.shape
     pair = call(pair_body, shape((rows, lanes + gram_size), BF), value, other_core(value))
-    return [pair] + [around_y(pair, d) for d in (2, 3, 1)]
+    return [pair] + [around_y(pair, d) for d in steps]
 
 
 def on_device(adapter_down, adapter_up, fisher, init_v, init_u, prompt_rows, request_ids):
@@ -361,9 +360,9 @@
     def reduced(tiles):
         return swap(call(sum_body, tile_shape, swap(tiles)))
 
-    def projected(numer, stack):
+    def projected(numer, stack, steps=(2, 3, 1)):
         value = call(project_body, shape((size, count + size), F32), numer, stack)
-        return over_feature(value, size)
+        return over_feature(value, size, steps)
 
     value = call(
         start_body,
@@ -375,7 +374,7 @@
     )
     core = jnp.full((1,), lax.axis_index("feature") % CORES, jnp.int32)
     parts, id_tile, core = lax.optimization_barrier((over_feature(value, 0), id_tile, core))
-    tiles, q, p = call(first_body, [tile_shape, flat, flat], *parts, up, fisher_row)
+    tiles, p = call(first_body, [tile_shape, flat], *parts, up, fisher_row)
     for sweep in range(SWEEPS):
         if sweep == 0:
             copies = call(
@@ -396,7 +395,7 @@
             parts = projected(numer, up)
         if sweep < SWEEPS - 1:
             tiles, q = call(renew_body, [tile_shape, flat], *parts, p, down, fisher_row)
-            parts = projected(reduced(tiles), down)
+            parts = projected(reduced(tiles), down, (1, 2, 3) if sweep == 0 else (2, 3, 1))
             tiles, p = call(renew_body, [tile_shape, flat], *parts, q, up, fisher_row)
         else:
             tiles, q, basis = call(

time: 300 us -> 298 us (level)
  no operation moved by 1% of the time
where the time goes in v6:
time: 298 us; the launch traced here: 294 us
  blocking collectives  174 us (58%)
  starting transfers between devices  56 us (19%)
  waiting for transfers between devices  33.9 us (11%)
  Pallas kernels  25.1 us (8%)
  local copies, waits for them, and re-layouts  3.55 us (1%)
    all_to_all x13, blocking collectives, swap(): return lax.all_to_all(parts, 'adapter', 0, 0, tiled=True)  174 us
    ppermute x7, starting transfers between devices, other_core(): return lax.ppermute(value, 'feature', [(i, i ^ 1) for i in range(size)])  32.1 us
    ppermute x21, waiting for transfers between devices, around_y(): lax.ppermute(value, 'feature', [(i, (i + d * CORES) % size) for i in rang...  28.1 us
    ppermute x21, starting transfers between devices, around_y(): lax.ppermute(value, 'feature', [(i, (i + d * CORES) % size) for i in rang...  23.9 us
    pallas_call x28, Pallas kernels, call(): pl.pallas_call(body, out_shape=outs, in_specs=[scalar if arg.shape == (1,...  20.8 us
  transfers between devices with their start and end apart: 28, of which 21 were waited for; matrix products, arithmetic and copies ran while one was open for 0% of the time, Pallas kernels for 0%

profile of v6, /device:TPU:1, one launch (start us, length us, event | category | flops | bytes accessed | tf_op | source)
XLA Modules:
  0.0 293.8 jit_solution(15905798118846964313)
XLA Ops:
  0.0 1.1 convert_bitcast_fusion
  2.7 3.3 %collective-permute-start = (f32[64,512]{1,0:T(8,128)S(1)}, f32[64,512]{1,0:T(8,128)S(1)}, u32[]{:S(2)}, u32[]{:S(2)}) collective-permute-start(f32[64,512]{1,0:T(8,128)S(1)} %shard_map.73.own), channel_id=1, source_target_pairs={{0,1},{1,0},{2,3},{3,2},{4,5},{5,4},{6,7},{7,6},{8,9},{9,8},{10,11... | collective-permute-start | bytes 393224 | tf_op jit(solution)/shard_map/ppermute | solution.py:331
  7.5 1.3 collective-permute-start.1
  10.6 2.2 collective-permute-done.1.b
  14.7 20.2 %all_to_all.65.parts = bf16[32,16,128]{2,1,0:T(8,128)(2,1)S(1)} all-to-all(bf16[32,16,128]{2,1,0:T(8,128)(2,1)S(1)} %get-tuple-element.39), channel_id=1, replica_groups=mesh['adapter'=32,'feature'=8] {'adapter'}, dimensions={0} | all-to-all | bytes 262144 | tf_op jit(solution)/shard_map/all_to_all | solution.py:358
  34.9 13.7 %all_to_all.66.tiles = bf16[32,32,128]{2,1,0:T(8,128)(2,1)S(1)} all-to-all(bf16[32,32,128]{2,1,0:T(8,128)(2,1)S(1)} %shard_map.76), channel_id=1, replica_groups=mesh['adapter'=32,'feature'=8] {'adapter'}, dimensions={0} | all-to-all | bytes 524288 | tf_op jit(solution)/shard_map/all_to_all | solution.py:358
  49.0 4.3 %collective-permute-start.4 = (f32[64,320]{1,0:T(8,128)S(1)}, f32[64,320]{1,0:T(8,128)S(1)}, u32[]{:S(2)}, u32[]{:S(2)}) collective-permute-start(f32[64,320]{1,0:T(8,128)S(1)} %get-tuple-element.41.own), channel_id=1, source_target_pairs={{0,1},{1,0},{2,3},{3,2},{4,5},{5,4},{6,7},{7,6},{8,9},{9,8},{10,11... | collective-permute-start | bytes 245768 | tf_op jit(solution)/shard_map/ppermute | solution.py:331
  54.3 1.1 collective-permute-start.5
  57.7 1.1 collective-permute-done.5.b
  59.0 1.6 collective-permute-done.7.d
  60.6 3.1 %shard_map.80 = (bf16[32,16,128]{2,1,0:T(8,128)(2,1)S(1)}, f32[64,256]{1,0:T(8,128)S(1)}) custom-call(bf16[64,384]{1,0:T(8,128)(2,1)S(1)} %shard_map.78.a, bf16[64,384]{1,0:T(8,128)(2,1)S(1)} %collective-permute-done.5.b, bf16[64,384]{1,0:T(8,128)(2,1)S(1)} %collective-permute-done.6.c, bf16[64,384]{1,0:T(8,128)(2,1)S(1)} %collective-permute-done.7.d, ...), custom_call_target="tpu_custom_call" | custom-call | tf_op jit(solution)/shard_map/pallas_call | solution.py:19
  63.8 12.4 %all_to_all.67.parts = bf16[32,16,128]{2,1,0:T(8,128)(2,1)S(1)} all-to-all(bf16[32,16,128]{2,1,0:T(8,128)(2,1)S(1)} %get-tuple-element.48), channel_id=1, replica_groups=mesh['adapter'=32,'feature'=8] {'adapter'}, dimensions={0} | all-to-all | bytes 262144 | tf_op jit(solution)/shard_map/all_to_all | solution.py:358
  76.2 12.6 %all_to_all.68.tiles = bf16[32,16,128]{2,1,0:T(8,128)(2,1)S(1)} all-to-all(bf16[32,16,128]{2,1,0:T(8,128)(2,1)S(1)} %shard_map.81), channel_id=1, replica_groups=mesh['adapter'=32,'feature'=8] {'adapter'}, dimensions={0} | all-to-all | bytes 262144 | tf_op jit(solution)/shard_map/all_to_all | solution.py:358
  89.2 4.7 %collective-permute-start.8 = (f32[64,320]{1,0:T(8,128)S(1)}, f32[64,320]{1,0:T(8,128)S(1)}, u32[]{:S(2)}, u32[]{:S(2)}) collective-permute-start(f32[64,320]{1,0:T(8,128)S(1)} %shard_map.82.own), channel_id=1, source_target_pairs={{0,1},{1,0},{2,3},{3,2},{4,5},{5,4},{6,7},{7,6},{8,9},{9,8},{10,11... | collective-permute-start | bytes 245768 | tf_op jit(solution)/shard_map/ppermute | solution.py:331
  95.1 1.7 collective-permute-start.11
  96.8 2.6 collective-permute-done.10.c
  99.5 1.5 collective-permute-done.9.b
  101.0 3.1 %shard_map.84 = (bf16[32,16,128]{2,1,0:T(8,128)(2,1)S(1)}, f32[64,256]{1,0:T(8,128)S(1)}) custom-call(bf16[64,384]{1,0:T(8,128)(2,1)S(1)} %shard_map.83.a, bf16[64,384]{1,0:T(8,128)(2,1)S(1)} %collective-permute-done.9.b, bf16[64,384]{1,0:T(8,128)(2,1)S(1)} %collective-permute-done.10.c, bf16[64,384]{1,0:T(8,128)(2,1)S(1)} %collective-permute-done.11.d, ...), custom_call_target="tpu_custom_call" | custom-call | tf_op jit(solution)/shard_map/pallas_call | solution.py:19
  104.1 12.4 %all_to_all.69.parts = bf16[32,16,128]{2,1,0:T(8,128)(2,1)S(1)} all-to-all(bf16[32,16,128]{2,1,0:T(8,128)(2,1)S(1)} %get-tuple-element.50), channel_id=1, replica_groups=mesh['adapter'=32,'feature'=8] {'adapter'}, dimensions={0} | all-to-all | bytes 262144 | tf_op jit(solution)/shard_map/all_to_all | solution.py:358
  116.6 12.6 %all_to_all.70.tiles = bf16[32,16,128]{2,1,0:T(8,128)(2,1)S(1)} all-to-all(bf16[32,16,128]{2,1,0:T(8,128)(2,1)S(1)} %shard_map.85), channel_id=1, replica_groups=mesh['adapter'=32,'feature'=8] {'adapter'}, dimensions={0} | all-to-all | bytes 262144 | tf_op jit(solution)/shard_map/all_to_all | solution.py:358
  129.6 4.7 %collective-permute-start.12 = (f32[64,320]{1,0:T(8,128)S(1)}, f32[64,320]{1,0:T(8,128)S(1)}, u32[]{:S(2)}, u32[]{:S(2)}) collective-permute-start(f32[64,320]{1,0:T(8,128)S(1)} %shard_map.86.own), channel_id=1, source_target_pairs={{0,1},{1,0},{2,3},{3,2},{4,5},{5,4},{6,7},{7,6},{8,9},{9,8},{10,11... | collective-permute-start | bytes 245768 | tf_op jit(solution)/shard_map/ppermute | solution.py:331
  135.4 1.1 collective-permute-start.14
  136.9 2.9 collective-permute-done.13.b
  139.8 1.3 collective-permute-done.15.d
  141.1 3.1 %shard_map.88 = (bf16[32,16,128]{2,1,0:T(8,128)(2,1)S(1)}, f32[64,256]{1,0:T(8,128)S(1)}) custom-call(bf16[64,384]{1,0:T(8,128)(2,1)S(1)} %shard_map.87.a, bf16[64,384]{1,0:T(8,128)(2,1)S(1)} %collective-permute-done.13.b, bf16[64,384]{1,0:T(8,128)(2,1)S(1)} %collective-permute-done.14.c, bf16[64,384]{1,0:T(8,128)(2,1)S(1)} %collective-permute-done.15.d, ...), custom_call_target="tpu_custom_call" | custom-call | tf_op jit(solution)/shard_map/pallas_call | solution.py:19
  144.2 12.3 %all_to_all.71.parts = bf16[32,16,128]{2,1,0:T(8,128)(2,1)S(1)} all-to-all(bf16[32,16,128]{2,1,0:T(8,128)(2,1)S(1)} %get-tuple-element.52), channel_id=1, replica_groups=mesh['adapter'=32,'feature'=8] {'adapter'}, dimensions={0} | all-to-all | bytes 262144 | tf_op jit(solution)/shard_map/all_to_all | solution.py:358
  156.6 12.7 %all_to_all.72.tiles = bf16[32,16,128]{2,1,0:T(8,128)(2,1)S(1)} all-to-all(bf16[32,16,128]{2,1,0:T(8,128)(2,1)S(1)} %shard_map.89), channel_id=1, replica_groups=mesh['adapter'=32,'feature'=8] {'adapter'}, dimensions={0} | all-to-all | bytes 262144 | tf_op jit(solution)/shard_map/all_to_all | solution.py:358
  169.6 4.2 %collective-permute-start.16 = (f32[64,320]{1,0:T(8,128)S(1)}, f32[64,320]{1,0:T(8,128)S(1)}, u32[]{:S(2)}, u32[]{:S(2)}) collective-permute-start(f32[64,320]{1,0:T(8,128)S(1)} %shard_map.90.own), channel_id=1, source_target_pairs={{0,1},{1,0},{2,3},{3,2},{4,5},{5,4},{6,7},{7,6},{8,9},{9,8},{10,11... | collective-permute-start | bytes 245768 | tf_op jit(solution)/shard_map/ppermute | solution.py:331
  175.2 1.1 collective-permute-start.18
  176.4 9.9 %collective-permute-start.19 = (bf16[64,384]{1,0:T(8,128)(2,1)S(1)}, bf16[64,384]{1,0:T(8,128)(2,1)S(1)}, u32[]{:S(2)}, u32[]{:S(2)}) collective-permute-start(bf16[64,384]{1,0:T(8,128)(2,1)S(1)} %shard_map.91.a), channel_id=1, source_target_pairs={{0,2},{1,3},{2,4},{3,5},{4,6},{5,7},{6,0},{7,1},{8,10},{9,11},{10,... | collective-permute-start | bytes 147464 | tf_op jit(solution)/shard_map/ppermute | solution.py:326
  186.2 3.8 %collective-permute-done.19.d = bf16[64,384]{1,0:T(8,128)(2,1)S(1)} collective-permute-done((bf16[64,384]{1,0:T(8,128)(2,1)S(1)}, bf16[64,384]{1,0:T(8,128)(2,1)S(1)}, u32[]{:S(2)}, u32[]{:S(2)}) %collective-permute-start.19) | collective-permute-done | bytes 49184 | tf_op jit(solution)/shard_map/ppermute | solution.py:326
  190.1 3.1 %shard_map.92 = (bf16[32,16,128]{2,1,0:T(8,128)(2,1)S(1)}, f32[64,256]{1,0:T(8,128)S(1)}) custom-call(bf16[64,384]{1,0:T(8,128)(2,1)S(1)} %shard_map.91.a, bf16[64,384]{1,0:T(8,128)(2,1)S(1)} %collective-permute-done.17.b, bf16[64,384]{1,0:T(8,128)(2,1)S(1)} %collective-permute-done.18.c, bf16[64,384]{1,0:T(8,128)(2,1)S(1)} %collective-permute-done.19.d, ...), custom_call_target="tpu_custom_call" | custom-call | tf_op jit(solution)/shard_map/pallas_call | solution.py:19
  193.2 12.4 %all_to_all.73.parts = bf16[32,16,128]{2,1,0:T(8,128)(2,1)S(1)} all-to-all(bf16[32,16,128]{2,1,0:T(8,128)(2,1)S(1)} %get-tuple-element.54), channel_id=1, replica_groups=mesh['adapter'=32,'feature'=8] {'adapter'}, dimensions={0} | all-to-all | bytes 262144 | tf_op jit(solution)/shard_map/all_to_all | solution.py:358
  205.6 12.6 %all_to_all.74.tiles.numer_tiles = bf16[32,16,128]{2,1,0:T(8,128)(2,1)S(1)} all-to-all(bf16[32,16,128]{2,1,0:T(8,128)(2,1)S(1)} %shard_map.93), channel_id=1, replica_groups=mesh['adapter'=32,'feature'=8] {'adapter'}, dimensions={0} | all-to-all | bytes 262144 | tf_op jit(solution)/shard_map/all_to_all | solution.py:358
  218.6 4.7 %collective-permute-start.20 = (f32[64,320]{1,0:T(8,128)S(1)}, f32[64,320]{1,0:T(8,128)S(1)}, u32[]{:S(2)}, u32[]{:S(2)}) collective-permute-start(f32[64,320]{1,0:T(8,128)S(1)} %shard_map.94.own), channel_id=1, source_target_pairs={{0,1},{1,0},{2,3},{3,2},{4,5},{5,4},{6,7},{7,6},{8,9},{9,8},{10,11... | collective-permute-start | bytes 245768 | tf_op jit(solution)/shard_map/ppermute | solution.py:331
  226.5 2.3 collective-permute-done.21.b
  228.8 1.3 collective-permute-done.23.d
  230.2 3.2 %shard_map.96 = (bf16[32,16,128]{2,1,0:T(8,128)(2,1)S(1)}, f32[64,256]{1,0:T(8,128)S(1)}, bf16[64,1024]{1,0:T(8,128)(2,1)S(1)}) custom-call(bf16[64,384]{1,0:T(8,128)(2,1)S(1)} %shard_map.95.a, bf16[64,384]{1,0:T(8,128)(2,1)S(1)} %collective-permute-done.21.b, bf16[64,384]{1,0:T(8,128)(2,1)S(1)} %collective-permute-done.22.c, ...), custom_call_target="tpu_custom_call" | custom-call | tf_op jit(solution)/shard_map/pallas_call | solution.py:19
  233.4 12.4 %all_to_all.75.parts = bf16[32,16,128]{2,1,0:T(8,128)(2,1)S(1)} all-to-all(bf16[32,16,128]{2,1,0:T(8,128)(2,1)S(1)} %get-tuple-element.56), channel_id=1, replica_groups=mesh['adapter'=32,'feature'=8] {'adapter'}, dimensions={0} | all-to-all | bytes 262144 | tf_op jit(solution)/shard_map/all_to_all | solution.py:358
  245.8 12.6 %all_to_all.76.tiles = bf16[32,16,128]{2,1,0:T(8,128)(2,1)S(1)} all-to-all(bf16[32,16,128]{2,1,0:T(8,128)(2,1)S(1)} %shard_map.97), channel_id=1, replica_groups=mesh['adapter'=32,'feature'=8] {'adapter'}, dimensions={0} | all-to-all | bytes 262144 | tf_op jit(solution)/shard_map/all_to_all | solution.py:358
  258.4 1.1 shard_map.98
  259.6 14.7 %all_to_all.77.parts = bf16[32,48,128]{2,1,0:T(8,128)(2,1)S(1)} all-to-all(bf16[32,48,128]{2,1,0:T(8,128)(2,1)S(1)} %get-tuple-element.59), channel_id=1, replica_groups=mesh['adapter'=32,'feature'=8] {'adapter'}, dimensions={0} | all-to-all | bytes 786432 | tf_op jit(solution)/shard_map/all_to_all | solution.py:358
  274.4 6.0 %collective-permute-start.24 = (f32[64,704]{1,0:T(8,128)S(1)}, f32[64,704]{1,0:T(8,128)S(1)}, u32[]{:S(2)}, u32[]{:S(2)}) collective-permute-start(f32[64,704]{1,0:T(8,128)S(1)} %shard_map.99.own), channel_id=1, source_target_pairs={{0,1},{1,0},{2,3},{3,2},{4,5},{5,4},{6,7},{7,6},{8,9},{9,8},{10,11... | collective-permute-start | bytes 540680 | tf_op jit(solution)/shard_map/ppermute | solution.py:331
  280.4 1.1 collective-permute-done.24.got
  281.6 1.7 collective-permute-start.26
  283.3 3.8 %collective-permute-done.25.b = bf16[64,768]{1,0:T(8,128)(2,1)S(1)} collective-permute-done((bf16[64,768]{1,0:T(8,128)(2,1)S(1)}, bf16[64,768]{1,0:T(8,128)(2,1)S(1)}, u32[]{:S(2)}, u32[]{:S(2)}) %collective-permute-start.25) | collective-permute-done | bytes 98336 | tf_op jit(solution)/shard_map/ppermute | solution.py:326
  287.3 2.0 collective-permute-done.27.d
  289.3 4.3 %shard_map.101 = bf16[512,1024]{1,0:T(8,128)(2,1)} custom-call(bf16[64,768]{1,0:T(8,128)(2,1)S(1)} %shard_map.100.a, bf16[64,768]{1,0:T(8,128)(2,1)S(1)} %collective-permute-done.25.b, bf16[64,768]{1,0:T(8,128)(2,1)S(1)} %collective-permute-done.26.c, bf16[64,768]{1,0:T(8,128)(2,1)S(1)} %collective-permute-done.27.d, ...), custom_call_target="tpu_custom_call" | custom-call | tf_op jit(solution)/shard_map/pallas_call | solution.py:426
  (72 shorter events, 19.8 us)
Async XLA Ops:
  0.0 1.2 copy-start
  1.2 1.0 copy-start.1
  2.7 4.8 %collective-permute-start = (f32[64,512]{1,0:T(8,128)S(1)}, f32[64,512]{1,0:T(8,128)S(1)}, u32[]{:S(2)}, u32[]{:S(2)}) collective-permute-start(f32[64,512]{1,0:T(8,128)S(1)} %shard_map.73.own), channel_id=1, source_target_pairs={{0,1},{1,0},{2,3},{3,2},{4,5},{5,4},{6,7},{7,6},{8,9},{9,8},{10,11... | collective-permute-start | bytes 393224 | tf_op jit(solution)/shard_map/ppermute | solution.py:331
  6.0 0.7 copy-start.4
  6.8 0.7 copy-start.5
  7.5 5.3 %collective-permute-start.1 = (bf16[64,512]{1,0:T(8,128)(2,1)S(1)}, bf16[64,512]{1,0:T(8,128)(2,1)S(1)}, u32[]{:S(2)}, u32[]{:S(2)}) collective-permute-start(bf16[64,512]{1,0:T(8,128)(2,1)S(1)} %shard_map.74.a), channel_id=1, source_target_pairs={{0,4},{1,5},{2,6},{3,7},{4,0},{5,1},{6,2},{7,3},{8,12},{9,13},{10,... | collective-permute-start | bytes 196616 | tf_op jit(solution)/shard_map/ppermute | solution.py:326
  8.8 4.0 %collective-permute-start.2 = (bf16[64,512]{1,0:T(8,128)(2,1)S(1)}, bf16[64,512]{1,0:T(8,128)(2,1)S(1)}, u32[]{:S(2)}, u32[]{:S(2)}) collective-permute-start(bf16[64,512]{1,0:T(8,128)(2,1)S(1)} %shard_map.74.a), channel_id=1, source_target_pairs={{0,6},{1,7},{2,0},{3,1},{4,2},{5,3},{6,4},{7,5},{8,14},{9,15},{10,... | collective-permute-start | bytes 196616 | tf_op jit(solution)/shard_map/ppermute | solution.py:326
  9.6 4.3 %collective-permute-start.3 = (bf16[64,512]{1,0:T(8,128)(2,1)S(1)}, bf16[64,512]{1,0:T(8,128)(2,1)S(1)}, u32[]{:S(2)}, u32[]{:S(2)}) collective-permute-start(bf16[64,512]{1,0:T(8,128)(2,1)S(1)} %shard_map.74.a), channel_id=1, source_target_pairs={{0,2},{1,3},{2,4},{3,5},{4,6},{5,7},{6,0},{7,1},{8,10},{9,11},{10,... | collective-permute-start | bytes 196616 | tf_op jit(solution)/shard_map/ppermute | solution.py:326
  49.0 5.3 %collective-permute-start.4 = (f32[64,320]{1,0:T(8,128)S(1)}, f32[64,320]{1,0:T(8,128)S(1)}, u32[]{:S(2)}, u32[]{:S(2)}) collective-permute-start(f32[64,320]{1,0:T(8,128)S(1)} %get-tuple-element.41.own), channel_id=1, source_target_pairs={{0,1},{1,0},{2,3},{3,2},{4,5},{5,4},{6,7},{7,6},{8,9},{9,8},{10,11... | collective-permute-start | bytes 245768 | tf_op jit(solution)/shard_map/ppermute | solution.py:331
  54.3 4.5 %collective-permute-start.5 = (bf16[64,384]{1,0:T(8,128)(2,1)S(1)}, bf16[64,384]{1,0:T(8,128)(2,1)S(1)}, u32[]{:S(2)}, u32[]{:S(2)}) collective-permute-start(bf16[64,384]{1,0:T(8,128)(2,1)S(1)} %shard_map.78.a), channel_id=1, source_target_pairs={{0,4},{1,5},{2,6},{3,7},{4,0},{5,1},{6,2},{7,3},{8,12},{9,13},{10,... | collective-permute-start | bytes 147464 | tf_op jit(solution)/shard_map/ppermute | solution.py:326
  55.5 3.6 %collective-permute-start.6 = (bf16[64,384]{1,0:T(8,128)(2,1)S(1)}, bf16[64,384]{1,0:T(8,128)(2,1)S(1)}, u32[]{:S(2)}, u32[]{:S(2)}) collective-permute-start(bf16[64,384]{1,0:T(8,128)(2,1)S(1)} %shard_map.78.a), channel_id=1, source_target_pairs={{0,6},{1,7},{2,0},{3,1},{4,2},{5,3},{6,4},{7,5},{8,14},{9,15},{10,... | collective-permute-start | bytes 147464 | tf_op jit(solution)/shard_map/ppermute | solution.py:326
  56.5 4.2 %collective-permute-start.7 = (bf16[64,384]{1,0:T(8,128)(2,1)S(1)}, bf16[64,384]{1,0:T(8,128)(2,1)S(1)}, u32[]{:S(2)}, u32[]{:S(2)}) collective-permute-start(bf16[64,384]{1,0:T(8,128)(2,1)S(1)} %shard_map.78.a), channel_id=1, source_target_pairs={{0,2},{1,3},{2,4},{3,5},{4,6},{5,7},{6,0},{7,1},{8,10},{9,11},{10,... | collective-permute-start | bytes 147464 | tf_op jit(solution)/shard_map/ppermute | solution.py:326
  57.6 3.0 %copy-start.2 = (bf16[16,16,1024]{2,1,0:T(8,128)(2,1)S(1)}, bf16[16,16,1024]{2,1,0:T(8,128)(2,1)}, u32[]{:S(2)}) copy-start(bf16[16,16,1024]{2,1,0:T(8,128)(2,1)} %param.7) | copy-start | bytes 1572868
  89.2 5.7 %collective-permute-start.8 = (f32[64,320]{1,0:T(8,128)S(1)}, f32[64,320]{1,0:T(8,128)S(1)}, u32[]{:S(2)}, u32[]{:S(2)}) collective-permute-start(f32[64,320]{1,0:T(8,128)S(1)} %shard_map.82.own), channel_id=1, source_target_pairs={{0,1},{1,0},{2,3},{3,2},{4,5},{5,4},{6,7},{7,6},{8,9},{9,8},{10,11... | collective-permute-start | bytes 245768 | tf_op jit(solution)/shard_map/ppermute | solution.py:331
  95.0 4.5 %collective-permute-start.10 = (bf16[64,384]{1,0:T(8,128)(2,1)S(1)}, bf16[64,384]{1,0:T(8,128)(2,1)S(1)}, u32[]{:S(2)}, u32[]{:S(2)}) collective-permute-start(bf16[64,384]{1,0:T(8,128)(2,1)S(1)} %shard_map.83.a), channel_id=1, source_target_pairs={{0,4},{1,5},{2,6},{3,7},{4,0},{5,1},{6,2},{7,3},{8,12},{9,13},{10,... | collective-permute-start | bytes 147464 | tf_op jit(solution)/shard_map/ppermute | solution.py:326
  95.1 4.3 %collective-permute-start.11 = (bf16[64,384]{1,0:T(8,128)(2,1)S(1)}, bf16[64,384]{1,0:T(8,128)(2,1)S(1)}, u32[]{:S(2)}, u32[]{:S(2)}) collective-permute-start(bf16[64,384]{1,0:T(8,128)(2,1)S(1)} %shard_map.83.a), channel_id=1, source_target_pairs={{0,6},{1,7},{2,0},{3,1},{4,2},{5,3},{6,4},{7,5},{8,14},{9,15},{10,... | collective-permute-start | bytes 147464 | tf_op jit(solution)/shard_map/ppermute | solution.py:326
  96.8 4.2 %collective-permute-start.9 = (bf16[64,384]{1,0:T(8,128)(2,1)S(1)}, bf16[64,384]{1,0:T(8,128)(2,1)S(1)}, u32[]{:S(2)}, u32[]{:S(2)}) collective-permute-start(bf16[64,384]{1,0:T(8,128)(2,1)S(1)} %shard_map.83.a), channel_id=1, source_target_pairs={{0,2},{1,3},{2,4},{3,5},{4,6},{5,7},{6,0},{7,1},{8,10},{9,11},{10,... | collective-permute-start | bytes 147464 | tf_op jit(solution)/shard_map/ppermute | solution.py:326
  129.6 5.7 %collective-permute-start.12 = (f32[64,320]{1,0:T(8,128)S(1)}, f32[64,320]{1,0:T(8,128)S(1)}, u32[]{:S(2)}, u32[]{:S(2)}) collective-permute-start(f32[64,320]{1,0:T(8,128)S(1)} %shard_map.86.own), channel_id=1, source_target_pairs={{0,1},{1,0},{2,3},{3,2},{4,5},{5,4},{6,7},{7,6},{8,9},{9,8},{10,11... | collective-permute-start | bytes 245768 | tf_op jit(solution)/shard_map/ppermute | solution.py:331
  135.3 4.5 %collective-permute-start.13 = (bf16[64,384]{1,0:T(8,128)(2,1)S(1)}, bf16[64,384]{1,0:T(8,128)(2,1)S(1)}, u32[]{:S(2)}, u32[]{:S(2)}) collective-permute-start(bf16[64,384]{1,0:T(8,128)(2,1)S(1)} %shard_map.87.a), channel_id=1, source_target_pairs={{0,4},{1,5},{2,6},{3,7},{4,0},{5,1},{6,2},{7,3},{8,12},{9,13},{10,... | collective-permute-start | bytes 147464 | tf_op jit(solution)/shard_map/ppermute | solution.py:326
  135.4 4.4 %collective-permute-start.14 = (bf16[64,384]{1,0:T(8,128)(2,1)S(1)}, bf16[64,384]{1,0:T(8,128)(2,1)S(1)}, u32[]{:S(2)}, u32[]{:S(2)}) collective-permute-start(bf16[64,384]{1,0:T(8,128)(2,1)S(1)} %shard_map.87.a), channel_id=1, source_target_pairs={{0,6},{1,7},{2,0},{3,1},{4,2},{5,3},{6,4},{7,5},{8,14},{9,15},{10,... | collective-permute-start | bytes 147464 | tf_op jit(solution)/shard_map/ppermute | solution.py:326
  136.4 4.7 %collective-permute-start.15 = (bf16[64,384]{1,0:T(8,128)(2,1)S(1)}, bf16[64,384]{1,0:T(8,128)(2,1)S(1)}, u32[]{:S(2)}, u32[]{:S(2)}) collective-permute-start(bf16[64,384]{1,0:T(8,128)(2,1)S(1)} %shard_map.87.a), channel_id=1, source_target_pairs={{0,2},{1,3},{2,4},{3,5},{4,6},{5,7},{6,0},{7,1},{8,10},{9,11},{10,... | collective-permute-start | bytes 147464 | tf_op jit(solution)/shard_map/ppermute | solution.py:326
  169.6 5.2 %collective-permute-start.16 = (f32[64,320]{1,0:T(8,128)S(1)}, f32[64,320]{1,0:T(8,128)S(1)}, u32[]{:S(2)}, u32[]{:S(2)}) collective-permute-start(f32[64,320]{1,0:T(8,128)S(1)} %shard_map.90.own), channel_id=1, source_target_pairs={{0,1},{1,0},{2,3},{3,2},{4,5},{5,4},{6,7},{7,6},{8,9},{9,8},{10,11... | collective-permute-start | bytes 245768 | tf_op jit(solution)/shard_map/ppermute | solution.py:331
  174.9 11.3 %collective-permute-start.17 = (bf16[64,384]{1,0:T(8,128)(2,1)S(1)}, bf16[64,384]{1,0:T(8,128)(2,1)S(1)}, u32[]{:S(2)}, u32[]{:S(2)}) collective-permute-start(bf16[64,384]{1,0:T(8,128)(2,1)S(1)} %shard_map.91.a), channel_id=1, source_target_pairs={{0,4},{1,5},{2,6},{3,7},{4,0},{5,1},{6,2},{7,3},{8,12},{9,13},{10,... | collective-permute-start | bytes 147464 | tf_op jit(solution)/shard_map/ppermute | solution.py:326
  175.2 11.0 %collective-permute-start.18 = (bf16[64,384]{1,0:T(8,128)(2,1)S(1)}, bf16[64,384]{1,0:T(8,128)(2,1)S(1)}, u32[]{:S(2)}, u32[]{:S(2)}) collective-permute-start(bf16[64,384]{1,0:T(8,128)(2,1)S(1)} %shard_map.91.a), channel_id=1, source_target_pairs={{0,6},{1,7},{2,0},{3,1},{4,2},{5,3},{6,4},{7,5},{8,14},{9,15},{10,... | collective-permute-start | bytes 147464 | tf_op jit(solution)/shard_map/ppermute | solution.py:326
  176.4 13.7 %collective-permute-start.19 = (bf16[64,384]{1,0:T(8,128)(2,1)S(1)}, bf16[64,384]{1,0:T(8,128)(2,1)S(1)}, u32[]{:S(2)}, u32[]{:S(2)}) collective-permute-start(bf16[64,384]{1,0:T(8,128)(2,1)S(1)} %shard_map.91.a), channel_id=1, source_target_pairs={{0,2},{1,3},{2,4},{3,5},{4,6},{5,7},{6,0},{7,1},{8,10},{9,11},{10,... | collective-permute-start | bytes 147464 | tf_op jit(solution)/shard_map/ppermute | solution.py:326
  218.6 39.8 %copy-start.3 = (bf16[512,1024]{1,0:T(8,128)(2,1)S(1)}, bf16[512,1024]{1,0:T(8,128)(2,1)}, u32[]{:S(2)}) copy-start(bf16[512,1024]{1,0:T(8,128)(2,1)} %prompts.1) | copy-start | bytes 3145732
  218.6 5.7 %collective-permute-start.20 = (f32[64,320]{1,0:T(8,128)S(1)}, f32[64,320]{1,0:T(8,128)S(1)}, u32[]{:S(2)}, u32[]{:S(2)}) collective-permute-start(f32[64,320]{1,0:T(8,128)S(1)} %shard_map.94.own), channel_id=1, source_target_pairs={{0,1},{1,0},{2,3},{3,2},{4,5},{5,4},{6,7},{7,6},{8,9},{9,8},{10,11... | collective-permute-start | bytes 245768 | tf_op jit(solution)/shard_map/ppermute | solution.py:331
  224.3 4.5 %collective-permute-start.21 = (bf16[64,384]{1,0:T(8,128)(2,1)S(1)}, bf16[64,384]{1,0:T(8,128)(2,1)S(1)}, u32[]{:S(2)}, u32[]{:S(2)}) collective-permute-start(bf16[64,384]{1,0:T(8,128)(2,1)S(1)} %shard_map.95.a), channel_id=1, source_target_pairs={{0,4},{1,5},{2,6},{3,7},{4,0},{5,1},{6,2},{7,3},{8,12},{9,13},{10,... | collective-permute-start | bytes 147464 | tf_op jit(solution)/shard_map/ppermute | solution.py:326
  225.0 3.8 %collective-permute-start.22 = (bf16[64,384]{1,0:T(8,128)(2,1)S(1)}, bf16[64,384]{1,0:T(8,128)(2,1)S(1)}, u32[]{:S(2)}, u32[]{:S(2)}) collective-permute-start(bf16[64,384]{1,0:T(8,128)(2,1)S(1)} %shard_map.95.a), channel_id=1, source_target_pairs={{0,6},{1,7},{2,0},{3,1},{4,2},{5,3},{6,4},{7,5},{8,14},{9,15},{10,... | collective-permute-start | bytes 147464 | tf_op jit(solution)/shard_map/ppermute | solution.py:326
  226.0 4.2 %collective-permute-start.23 = (bf16[64,384]{1,0:T(8,128)(2,1)S(1)}, bf16[64,384]{1,0:T(8,128)(2,1)S(1)}, u32[]{:S(2)}, u32[]{:S(2)}) collective-permute-start(bf16[64,384]{1,0:T(8,128)(2,1)S(1)} %shard_map.95.a), channel_id=1, source_target_pairs={{0,2},{1,3},{2,4},{3,5},{4,6},{5,7},{6,0},{7,1},{8,10},{9,11},{10,... | collective-permute-start | bytes 147464 | tf_op jit(solution)/shard_map/ppermute | solution.py:326
  274.4 7.1 %collective-permute-start.24 = (f32[64,704]{1,0:T(8,128)S(1)}, f32[64,704]{1,0:T(8,128)S(1)}, u32[]{:S(2)}, u32[]{:S(2)}) collective-permute-start(f32[64,704]{1,0:T(8,128)S(1)} %shard_map.99.own), channel_id=1, source_target_pairs={{0,1},{1,0},{2,3},{3,2},{4,5},{5,4},{6,7},{7,6},{8,9},{9,8},{10,11... | collective-permute-start | bytes 540680 | tf_op jit(solution)/shard_map/ppermute | solution.py:331
  281.6 5.5 %collective-permute-start.25 = (bf16[64,768]{1,0:T(8,128)(2,1)S(1)}, bf16[64,768]{1,0:T(8,128)(2,1)S(1)}, u32[]{:S(2)}, u32[]{:S(2)}) collective-permute-start(bf16[64,768]{1,0:T(8,128)(2,1)S(1)} %shard_map.100.a), channel_id=1, source_target_pairs={{0,4},{1,5},{2,6},{3,7},{4,0},{5,1},{6,2},{7,3},{8,12},{9,13},{10,... | collective-permute-start | bytes 294920 | tf_op jit(solution)/shard_map/ppermute | solution.py:326
  281.6 5.7 %collective-permute-start.26 = (bf16[64,768]{1,0:T(8,128)(2,1)S(1)}, bf16[64,768]{1,0:T(8,128)(2,1)S(1)}, u32[]{:S(2)}, u32[]{:S(2)}) collective-permute-start(bf16[64,768]{1,0:T(8,128)(2,1)S(1)} %shard_map.100.a), channel_id=1, source_target_pairs={{0,6},{1,7},{2,0},{3,1},{4,2},{5,3},{6,4},{7,5},{8,14},{9,15},{10,... | collective-permute-start | bytes 294920 | tf_op jit(solution)/shard_map/ppermute | solution.py:326
  283.3 6.0 %collective-permute-start.27 = (bf16[64,768]{1,0:T(8,128)(2,1)S(1)}, bf16[64,768]{1,0:T(8,128)(2,1)S(1)}, u32[]{:S(2)}, u32[]{:S(2)}) collective-permute-start(bf16[64,768]{1,0:T(8,128)(2,1)S(1)} %shard_map.100.a), channel_id=1, source_target_pairs={{0,2},{1,3},{2,4},{3,5},{4,6},{5,7},{6,0},{7,1},{8,10},{9,11},{10,... | collective-permute-start | bytes 294920 | tf_op jit(solution)/shard_map/ppermute | solution.py:326

commit v7 on v6

--- a/solution.py
+++ b/solution.py
@@ -128,11 +128,12 @@
 
 def weighted_terms(fresh, other, fisher_row):
     count = fresh.shape[1]
-    inner = in_three(dot_tn, fresh, fresh)
+    low = fresh.astype(BF)
+    inner = dot_tn(low, low)
     a = lax.broadcasted_iota(jnp.int32, (count, count), 0) // RANK
     b = lax.broadcasted_iota(jnp.int32, (count, count), 1) // RANK
     inner = jnp.where(a == b, inner, 0.0)
-    return (in_three(dot_nn, other, inner) * fisher_row).astype(BF)
+    return (dot_nn(other.astype(BF), inner.astype(BF)) * fisher_row).astype(BF)
 
 
 def added(refs):
@@ -161,9 +162,17 @@
     )
 
 
-def start_body(down, up, vt, ut, out):
-    q = dot_nt(ut[...], up[...])
-    p = dot_nt(vt[...], down[...])
+def start_body(down, up, vt, ut, out, down_here, up_here, vt_here, ut_here, came):
+    pairs = ((up, up_here), (ut, ut_here), (down, down_here), (vt, vt_here))
+    copies = [pltpu.make_async_copy(a, b, came.at[i]) for i, (a, b) in enumerate(pairs)]
+    for copy in copies:
+        copy.start()
+    copies[0].wait()
+    copies[1].wait()
+    q = dot_nt(ut_here[...].astype(BF), up_here[...])
+    copies[2].wait()
+    copies[3].wait()
+    p = dot_nt(vt_here[...].astype(BF), down_here[...])
     out[...] = jnp.concatenate([q, p], axis=1)
 
 
@@ -331,7 +340,7 @@
     return lax.ppermute(value, "feature", [(i, i ^ 1) for i in range(size)])
 
 
-def over_feature(value, gram_size, steps=(2, 3, 1)):
+def over_feature(value, gram_size, steps=(2, 1, 3)):
     rows, lanes = value.shape
     pair = call(pair_body, shape((rows, lanes + gram_size), BF), value, other_core(value))
     return [pair] + [around_y(pair, d) for d in steps]
@@ -360,18 +369,24 @@
     def reduced(tiles):
         return swap(call(sum_body, tile_shape, swap(tiles)))
 
-    def projected(numer, stack, steps=(2, 3, 1)):
+    def projected(numer, stack, steps=(2, 1, 3)):
         value = call(project_body, shape((size, count + size), F32), numer, stack)
         return over_feature(value, size, steps)
 
-    value = call(
+    value = pl.pallas_call(
         start_body,
-        shape((size, 2 * count), F32),
-        down,
-        up,
-        init_v.T.astype(BF),
-        init_u.T.astype(BF),
-    )
+        out_shape=shape((size, 2 * count), F32),
+        in_specs=[pl.BlockSpec(memory_space=pl.ANY)] * 4,
+        out_specs=pl.BlockSpec(memory_space=pltpu.VMEM),
+        scratch_shapes=[
+            pltpu.VMEM((count, width), BF),
+            pltpu.VMEM((count, width), BF),
+            pltpu.VMEM((size, width), F32),
+            pltpu.VMEM((size, width), F32),
+            pltpu.SemaphoreType.DMA((4,)),
+        ],
+        compiler_params=pltpu.CompilerParams(vmem_limit_bytes=56295424),
+    )(down, up, init_v.T, init_u.T)
     core = jnp.full((1,), lax.axis_index("feature") % CORES, jnp.int32)
     parts, id_tile, core = lax.optimization_barrier((over_feature(value, 0), id_tile, core))
     tiles, p = call(first_body, [tile_shape, flat], *parts, up, fisher_row)
@@ -395,7 +410,7 @@
             parts = projected(numer, up)
         if sweep < SWEEPS - 1:
             tiles, q = call(renew_body, [tile_shape, flat], *parts, p, down, fisher_row)
-            parts = projected(reduced(tiles), down, (1, 2, 3) if sweep == 0 else (2, 3, 1))
+            parts = projected(reduced(tiles), down, (3, 2, 1) if sweep == 0 else (2, 1, 3))
             tiles, p = call(renew_body, [tile_shape, flat], *parts, q, up, fisher_row)
         else:
             tiles, q, basis = call(

time: 298 us -> 296 us (level)
  starting transfers between devices: 56 us -> 66.4 us
  waiting for transfers between devices: 33.9 us -> 24.3 us
    ppermute x21, starting transfers between devices: 23.9 us -> 35.1 us  [around_y(): lax.ppermute(value, 'feature', [(i, (i + d * CORES) % size) for i in rang...]
    ppermute x21, waiting for transfers between devices: 28.1 us -> 18.5 us  [around_y(): lax.ppermute(value, 'feature', [(i, (i + d * CORES) % size) for i in rang...]
    pallas_call x28 -> x27, Pallas kernels: 20.8 us -> 18.9 us  [call(): pl.pallas_call(body, out_shape=outs, in_specs=[scalar if arg.shape == (1,...]
where the time goes in v7:
time: 296 us; the launch traced here: 292 us
  blocking collectives  173 us (58%)
  starting transfers between devices  66.4 us (22%)
  Pallas kernels  25.2 us (9%)
  waiting for transfers between devices  24.3 us (8%)
    all_to_all x13, blocking collectives, swap(): return lax.all_to_all(parts, 'adapter', 0, 0, tiled=True)  173 us
    ppermute x21, starting transfers between devices, around_y(): lax.ppermute(value, 'feature', [(i, (i + d * CORES) % size) for i in rang...  35.1 us
    ppermute x7, starting transfers between devices, other_core(): return lax.ppermute(value, 'feature', [(i, i ^ 1) for i in range(size)])  31.3 us
    pallas_call x27, Pallas kernels, call(): pl.pallas_call(body, out_shape=outs, in_specs=[scalar if arg.shape == (1,...  18.9 us
    ppermute x21, waiting for transfers between devices, around_y(): lax.ppermute(value, 'feature', [(i, (i + d * CORES) % size) for i in rang...  18.5 us
  transfers between devices with their start and end apart: 28, of which 21 were waited for; matrix products, arithmetic and copies ran while one was open for 0% of the time, Pallas kernels for 0%

profile of v7, /device:TPU:1, one launch (start us, length us, event | category | flops | bytes accessed | tf_op | source)
XLA Modules:
  0.0 291.6 jit_solution(12258507371282869659)
XLA Ops:
  0.0 2.0 shard_map.73.own
  2.0 3.3 %collective-permute-start = (f32[64,512]{1,0:T(8,128)S(1)}, f32[64,512]{1,0:T(8,128)S(1)}, u32[]{:S(2)}, u32[]{:S(2)}) collective-permute-start(f32[64,512]{1,0:T(8,128)S(1)} %shard_map.73.own), channel_id=1, source_target_pairs={{0,1},{1,0},{2,3},{3,2},{4,5},{5,4},{6,7},{7,6},{8,9},{9,8},{10,11... | collective-permute-start | bytes 393224 | tf_op jit(solution)/shard_map/ppermute | solution.py:340
  6.9 1.3 collective-permute-start.1
  8.5 2.3 collective-permute-start.3
  12.2 1.5 collective-permute-done.2.c
  14.2 19.0 %all_to_all.65.parts = bf16[32,16,128]{2,1,0:T(8,128)(2,1)S(1)} all-to-all(bf16[32,16,128]{2,1,0:T(8,128)(2,1)S(1)} %get-tuple-element.39), channel_id=1, replica_groups=mesh['adapter'=32,'feature'=8] {'adapter'}, dimensions={0} | all-to-all | bytes 262144 | tf_op jit(solution)/shard_map/all_to_all | solution.py:367
  33.2 13.8 %all_to_all.66.tiles = bf16[32,32,128]{2,1,0:T(8,128)(2,1)S(1)} all-to-all(bf16[32,32,128]{2,1,0:T(8,128)(2,1)S(1)} %shard_map.76), channel_id=1, replica_groups=mesh['adapter'=32,'feature'=8] {'adapter'}, dimensions={0} | all-to-all | bytes 524288 | tf_op jit(solution)/shard_map/all_to_all | solution.py:367
  47.4 4.1 %collective-permute-start.4 = (f32[64,320]{1,0:T(8,128)S(1)}, f32[64,320]{1,0:T(8,128)S(1)}, u32[]{:S(2)}, u32[]{:S(2)}) collective-permute-start(f32[64,320]{1,0:T(8,128)S(1)} %get-tuple-element.41.own), channel_id=1, source_target_pairs={{0,1},{1,0},{2,3},{3,2},{4,5},{5,4},{6,7},{7,6},{8,9},{9,8},{10,11... | collective-permute-start | bytes 245768 | tf_op jit(solution)/shard_map/ppermute | solution.py:340
  52.5 1.3 collective-permute-start.5
  53.8 2.2 collective-permute-start.6
  59.2 2.9 shard_map.80
  62.1 12.7 %all_to_all.67.parts = bf16[32,16,128]{2,1,0:T(8,128)(2,1)S(1)} all-to-all(bf16[32,16,128]{2,1,0:T(8,128)(2,1)S(1)} %get-tuple-element.48), channel_id=1, replica_groups=mesh['adapter'=32,'feature'=8] {'adapter'}, dimensions={0} | all-to-all | bytes 262144 | tf_op jit(solution)/shard_map/all_to_all | solution.py:367
  74.8 12.5 %all_to_all.68.tiles = bf16[32,16,128]{2,1,0:T(8,128)(2,1)S(1)} all-to-all(bf16[32,16,128]{2,1,0:T(8,128)(2,1)S(1)} %shard_map.81), channel_id=1, replica_groups=mesh['adapter'=32,'feature'=8] {'adapter'}, dimensions={0} | all-to-all | bytes 262144 | tf_op jit(solution)/shard_map/all_to_all | solution.py:367
  87.7 4.4 %collective-permute-start.8 = (f32[64,320]{1,0:T(8,128)S(1)}, f32[64,320]{1,0:T(8,128)S(1)}, u32[]{:S(2)}, u32[]{:S(2)}) collective-permute-start(f32[64,320]{1,0:T(8,128)S(1)} %shard_map.82.own), channel_id=1, source_target_pairs={{0,1},{1,0},{2,3},{3,2},{4,5},{5,4},{6,7},{7,6},{8,9},{9,8},{10,11... | collective-permute-start | bytes 245768 | tf_op jit(solution)/shard_map/ppermute | solution.py:340
  93.8 1.8 collective-permute-start.11
  95.6 1.1 collective-permute-start.9
  97.6 1.2 collective-permute-done.11.d
  98.8 2.9 shard_map.84
  101.7 12.4 %all_to_all.69.parts = bf16[32,16,128]{2,1,0:T(8,128)(2,1)S(1)} all-to-all(bf16[32,16,128]{2,1,0:T(8,128)(2,1)S(1)} %get-tuple-element.50), channel_id=1, replica_groups=mesh['adapter'=32,'feature'=8] {'adapter'}, dimensions={0} | all-to-all | bytes 262144 | tf_op jit(solution)/shard_map/all_to_all | solution.py:367
  114.1 12.6 %all_to_all.70.tiles = bf16[32,16,128]{2,1,0:T(8,128)(2,1)S(1)} all-to-all(bf16[32,16,128]{2,1,0:T(8,128)(2,1)S(1)} %shard_map.85), channel_id=1, replica_groups=mesh['adapter'=32,'feature'=8] {'adapter'}, dimensions={0} | all-to-all | bytes 262144 | tf_op jit(solution)/shard_map/all_to_all | solution.py:367
  127.1 4.3 %collective-permute-start.12 = (f32[64,320]{1,0:T(8,128)S(1)}, f32[64,320]{1,0:T(8,128)S(1)}, u32[]{:S(2)}, u32[]{:S(2)}) collective-permute-start(f32[64,320]{1,0:T(8,128)S(1)} %shard_map.86.own), channel_id=1, source_target_pairs={{0,1},{1,0},{2,3},{3,2},{4,5},{5,4},{6,7},{7,6},{8,9},{9,8},{10,11... | collective-permute-start | bytes 245768 | tf_op jit(solution)/shard_map/ppermute | solution.py:340
  132.5 1.3 collective-permute-start.13
  133.8 1.7 collective-permute-start.14
  136.9 1.3 collective-permute-done.14.c
  138.4 2.9 shard_map.88
  141.3 12.4 %all_to_all.71.parts = bf16[32,16,128]{2,1,0:T(8,128)(2,1)S(1)} all-to-all(bf16[32,16,128]{2,1,0:T(8,128)(2,1)S(1)} %get-tuple-element.52), channel_id=1, replica_groups=mesh['adapter'=32,'feature'=8] {'adapter'}, dimensions={0} | all-to-all | bytes 262144 | tf_op jit(solution)/shard_map/all_to_all | solution.py:367
  153.7 12.6 %all_to_all.72.tiles = bf16[32,16,128]{2,1,0:T(8,128)(2,1)S(1)} all-to-all(bf16[32,16,128]{2,1,0:T(8,128)(2,1)S(1)} %shard_map.89), channel_id=1, replica_groups=mesh['adapter'=32,'feature'=8] {'adapter'}, dimensions={0} | all-to-all | bytes 262144 | tf_op jit(solution)/shard_map/all_to_all | solution.py:367
  166.7 4.7 %collective-permute-start.16 = (f32[64,320]{1,0:T(8,128)S(1)}, f32[64,320]{1,0:T(8,128)S(1)}, u32[]{:S(2)}, u32[]{:S(2)}) collective-permute-start(f32[64,320]{1,0:T(8,128)S(1)} %shard_map.90.own), channel_id=1, source_target_pairs={{0,1},{1,0},{2,3},{3,2},{4,5},{5,4},{6,7},{7,6},{8,9},{9,8},{10,11... | collective-permute-start | bytes 245768 | tf_op jit(solution)/shard_map/ppermute | solution.py:340
  172.4 1.2 collective-permute-start.17
  173.6 1.7 collective-permute-start.18
  175.3 10.4 %collective-permute-start.19 = (bf16[64,384]{1,0:T(8,128)(2,1)S(1)}, bf16[64,384]{1,0:T(8,128)(2,1)S(1)}, u32[]{:S(2)}, u32[]{:S(2)}) collective-permute-start(bf16[64,384]{1,0:T(8,128)(2,1)S(1)} %shard_map.91.a), channel_id=1, source_target_pairs={{0,6},{1,7},{2,0},{3,1},{4,2},{5,3},{6,4},{7,5},{8,14},{9,15},{10,... | collective-permute-start | bytes 147464 | tf_op jit(solution)/shard_map/ppermute | solution.py:335
  185.6 1.9 collective-permute-done.19.d
  187.6 2.9 shard_map.92
  190.4 12.4 %all_to_all.73.parts = bf16[32,16,128]{2,1,0:T(8,128)(2,1)S(1)} all-to-all(bf16[32,16,128]{2,1,0:T(8,128)(2,1)S(1)} %get-tuple-element.54), channel_id=1, replica_groups=mesh['adapter'=32,'feature'=8] {'adapter'}, dimensions={0} | all-to-all | bytes 262144 | tf_op jit(solution)/shard_map/all_to_all | solution.py:367
  202.8 12.6 %all_to_all.74.tiles.numer_tiles = bf16[32,16,128]{2,1,0:T(8,128)(2,1)S(1)} all-to-all(bf16[32,16,128]{2,1,0:T(8,128)(2,1)S(1)} %shard_map.93), channel_id=1, replica_groups=mesh['adapter'=32,'feature'=8] {'adapter'}, dimensions={0} | all-to-all | bytes 262144 | tf_op jit(solution)/shard_map/all_to_all | solution.py:367
  215.9 4.7 %collective-permute-start.20 = (f32[64,320]{1,0:T(8,128)S(1)}, f32[64,320]{1,0:T(8,128)S(1)}, u32[]{:S(2)}, u32[]{:S(2)}) collective-permute-start(f32[64,320]{1,0:T(8,128)S(1)} %shard_map.94.own), channel_id=1, source_target_pairs={{0,1},{1,0},{2,3},{3,2},{4,5},{5,4},{6,7},{7,6},{8,9},{9,8},{10,11... | collective-permute-start | bytes 245768 | tf_op jit(solution)/shard_map/ppermute | solution.py:340
  222.1 2.4 collective-permute-start.22
  224.8 1.4 collective-permute-done.21.b
  227.7 3.0 %shard_map.96 = (bf16[32,16,128]{2,1,0:T(8,128)(2,1)S(1)}, f32[64,256]{1,0:T(8,128)S(1)}, bf16[64,1024]{1,0:T(8,128)(2,1)S(1)}) custom-call(bf16[64,384]{1,0:T(8,128)(2,1)S(1)} %shard_map.95.a, bf16[64,384]{1,0:T(8,128)(2,1)S(1)} %collective-permute-done.21.b, bf16[64,384]{1,0:T(8,128)(2,1)S(1)} %collective-permute-done.22.c, ...), custom_call_target="tpu_custom_call" | custom-call | tf_op jit(solution)/shard_map/pallas_call | solution.py:19
  230.8 12.4 %all_to_all.75.parts = bf16[32,16,128]{2,1,0:T(8,128)(2,1)S(1)} all-to-all(bf16[32,16,128]{2,1,0:T(8,128)(2,1)S(1)} %get-tuple-element.56), channel_id=1, replica_groups=mesh['adapter'=32,'feature'=8] {'adapter'}, dimensions={0} | all-to-all | bytes 262144 | tf_op jit(solution)/shard_map/all_to_all | solution.py:367
  243.2 12.6 %all_to_all.76.tiles = bf16[32,16,128]{2,1,0:T(8,128)(2,1)S(1)} all-to-all(bf16[32,16,128]{2,1,0:T(8,128)(2,1)S(1)} %shard_map.97), channel_id=1, replica_groups=mesh['adapter'=32,'feature'=8] {'adapter'}, dimensions={0} | all-to-all | bytes 262144 | tf_op jit(solution)/shard_map/all_to_all | solution.py:367
  255.8 1.1 shard_map.98
  257.0 14.7 %all_to_all.77.parts = bf16[32,48,128]{2,1,0:T(8,128)(2,1)S(1)} all-to-all(bf16[32,48,128]{2,1,0:T(8,128)(2,1)S(1)} %get-tuple-element.59), channel_id=1, replica_groups=mesh['adapter'=32,'feature'=8] {'adapter'}, dimensions={0} | all-to-all | bytes 786432 | tf_op jit(solution)/shard_map/all_to_all | solution.py:367
  271.8 5.7 %collective-permute-start.24 = (f32[64,704]{1,0:T(8,128)S(1)}, f32[64,704]{1,0:T(8,128)S(1)}, u32[]{:S(2)}, u32[]{:S(2)}) collective-permute-start(f32[64,704]{1,0:T(8,128)S(1)} %shard_map.99.own), channel_id=1, source_target_pairs={{0,1},{1,0},{2,3},{3,2},{4,5},{5,4},{6,7},{7,6},{8,9},{9,8},{10,11... | collective-permute-start | bytes 540680 | tf_op jit(solution)/shard_map/ppermute | solution.py:340
  279.3 1.6 collective-permute-start.26
  282.0 2.3 collective-permute-done.25.b
  284.3 2.8 collective-permute-done.26.c
  287.1 4.3 %shard_map.101 = bf16[512,1024]{1,0:T(8,128)(2,1)} custom-call(bf16[64,768]{1,0:T(8,128)(2,1)S(1)} %shard_map.100.a, bf16[64,768]{1,0:T(8,128)(2,1)S(1)} %collective-permute-done.25.b, bf16[64,768]{1,0:T(8,128)(2,1)S(1)} %collective-permute-done.26.c, bf16[64,768]{1,0:T(8,128)(2,1)S(1)} %collective-permute-done.27.d, ...), custom_call_target="tpu_custom_call" | custom-call | tf_op jit(solution)/shard_map/pallas_call | solution.py:441
  (69 shorter events, 22.6 us)
Async XLA Ops:
  0.0 13.7 %copy-start = (bf16[16,16,1024]{2,1,0:T(8,128)(2,1)S(1)}, bf16[16,16,1024]{2,1,0:T(8,128)(2,1)}, u32[]{:S(2)}) copy-start(bf16[16,16,1024]{2,1,0:T(8,128)(2,1)} %param.8) | copy-start | bytes 1572868
  2.0 4.8 %collective-permute-start = (f32[64,512]{1,0:T(8,128)S(1)}, f32[64,512]{1,0:T(8,128)S(1)}, u32[]{:S(2)}, u32[]{:S(2)}) collective-permute-start(f32[64,512]{1,0:T(8,128)S(1)} %shard_map.73.own), channel_id=1, source_target_pairs={{0,1},{1,0},{2,3},{3,2},{4,5},{5,4},{6,7},{7,6},{8,9},{9,8},{10,11... | collective-permute-start | bytes 393224 | tf_op jit(solution)/shard_map/ppermute | solution.py:340
  5.3 0.7 copy-start.3
  6.2 0.7 copy-start.4
  6.9 5.3 %collective-permute-start.1 = (bf16[64,512]{1,0:T(8,128)(2,1)S(1)}, bf16[64,512]{1,0:T(8,128)(2,1)S(1)}, u32[]{:S(2)}, u32[]{:S(2)}) collective-permute-start(bf16[64,512]{1,0:T(8,128)(2,1)S(1)} %shard_map.74.a), channel_id=1, source_target_pairs={{0,4},{1,5},{2,6},{3,7},{4,0},{5,1},{6,2},{7,3},{8,12},{9,13},{10,... | collective-permute-start | bytes 196616 | tf_op jit(solution)/shard_map/ppermute | solution.py:335
  8.1 5.5 %collective-permute-start.2 = (bf16[64,512]{1,0:T(8,128)(2,1)S(1)}, bf16[64,512]{1,0:T(8,128)(2,1)S(1)}, u32[]{:S(2)}, u32[]{:S(2)}) collective-permute-start(bf16[64,512]{1,0:T(8,128)(2,1)S(1)} %shard_map.74.a), channel_id=1, source_target_pairs={{0,2},{1,3},{2,4},{3,5},{4,6},{5,7},{6,0},{7,1},{8,10},{9,11},{10,... | collective-permute-start | bytes 196616 | tf_op jit(solution)/shard_map/ppermute | solution.py:335
  8.5 5.1 %collective-permute-start.3 = (bf16[64,512]{1,0:T(8,128)(2,1)S(1)}, bf16[64,512]{1,0:T(8,128)(2,1)S(1)}, u32[]{:S(2)}, u32[]{:S(2)}) collective-permute-start(bf16[64,512]{1,0:T(8,128)(2,1)S(1)} %shard_map.74.a), channel_id=1, source_target_pairs={{0,6},{1,7},{2,0},{3,1},{4,2},{5,3},{6,4},{7,5},{8,14},{9,15},{10,... | collective-permute-start | bytes 196616 | tf_op jit(solution)/shard_map/ppermute | solution.py:335
  47.4 5.1 %collective-permute-start.4 = (f32[64,320]{1,0:T(8,128)S(1)}, f32[64,320]{1,0:T(8,128)S(1)}, u32[]{:S(2)}, u32[]{:S(2)}) collective-permute-start(f32[64,320]{1,0:T(8,128)S(1)} %get-tuple-element.41.own), channel_id=1, source_target_pairs={{0,1},{1,0},{2,3},{3,2},{4,5},{5,4},{6,7},{7,6},{8,9},{9,8},{10,11... | collective-permute-start | bytes 245768 | tf_op jit(solution)/shard_map/ppermute | solution.py:340
  52.5 4.7 %collective-permute-start.5 = (bf16[64,384]{1,0:T(8,128)(2,1)S(1)}, bf16[64,384]{1,0:T(8,128)(2,1)S(1)}, u32[]{:S(2)}, u32[]{:S(2)}) collective-permute-start(bf16[64,384]{1,0:T(8,128)(2,1)S(1)} %shard_map.78.a), channel_id=1, source_target_pairs={{0,4},{1,5},{2,6},{3,7},{4,0},{5,1},{6,2},{7,3},{8,12},{9,13},{10,... | collective-permute-start | bytes 147464 | tf_op jit(solution)/shard_map/ppermute | solution.py:335
  53.8 4.6 %collective-permute-start.6 = (bf16[64,384]{1,0:T(8,128)(2,1)S(1)}, bf16[64,384]{1,0:T(8,128)(2,1)S(1)}, u32[]{:S(2)}, u32[]{:S(2)}) collective-permute-start(bf16[64,384]{1,0:T(8,128)(2,1)S(1)} %shard_map.78.a), channel_id=1, source_target_pairs={{0,2},{1,3},{2,4},{3,5},{4,6},{5,7},{6,0},{7,1},{8,10},{9,11},{10,... | collective-permute-start | bytes 147464 | tf_op jit(solution)/shard_map/ppermute | solution.py:335
  55.9 3.2 %collective-permute-start.7 = (bf16[64,384]{1,0:T(8,128)(2,1)S(1)}, bf16[64,384]{1,0:T(8,128)(2,1)S(1)}, u32[]{:S(2)}, u32[]{:S(2)}) collective-permute-start(bf16[64,384]{1,0:T(8,128)(2,1)S(1)} %shard_map.78.a), channel_id=1, source_target_pairs={{0,6},{1,7},{2,0},{3,1},{4,2},{5,3},{6,4},{7,5},{8,14},{9,15},{10,... | collective-permute-start | bytes 147464 | tf_op jit(solution)/shard_map/ppermute | solution.py:335
  57.1 2.1 copy-start.1
  87.7 5.3 %collective-permute-start.8 = (f32[64,320]{1,0:T(8,128)S(1)}, f32[64,320]{1,0:T(8,128)S(1)}, u32[]{:S(2)}, u32[]{:S(2)}) collective-permute-start(f32[64,320]{1,0:T(8,128)S(1)} %shard_map.82.own), channel_id=1, source_target_pairs={{0,1},{1,0},{2,3},{3,2},{4,5},{5,4},{6,7},{7,6},{8,9},{9,8},{10,11... | collective-permute-start | bytes 245768 | tf_op jit(solution)/shard_map/ppermute | solution.py:340
  93.1 4.5 %collective-permute-start.10 = (bf16[64,384]{1,0:T(8,128)(2,1)S(1)}, bf16[64,384]{1,0:T(8,128)(2,1)S(1)}, u32[]{:S(2)}, u32[]{:S(2)}) collective-permute-start(bf16[64,384]{1,0:T(8,128)(2,1)S(1)} %shard_map.83.a), channel_id=1, source_target_pairs={{0,4},{1,5},{2,6},{3,7},{4,0},{5,1},{6,2},{7,3},{8,12},{9,13},{10,... | collective-permute-start | bytes 147464 | tf_op jit(solution)/shard_map/ppermute | solution.py:335
  93.8 5.0 %collective-permute-start.11 = (bf16[64,384]{1,0:T(8,128)(2,1)S(1)}, bf16[64,384]{1,0:T(8,128)(2,1)S(1)}, u32[]{:S(2)}, u32[]{:S(2)}) collective-permute-start(bf16[64,384]{1,0:T(8,128)(2,1)S(1)} %shard_map.83.a), channel_id=1, source_target_pairs={{0,2},{1,3},{2,4},{3,5},{4,6},{5,7},{6,0},{7,1},{8,10},{9,11},{10,... | collective-permute-start | bytes 147464 | tf_op jit(solution)/shard_map/ppermute | solution.py:335
  95.6 3.2 %collective-permute-start.9 = (bf16[64,384]{1,0:T(8,128)(2,1)S(1)}, bf16[64,384]{1,0:T(8,128)(2,1)S(1)}, u32[]{:S(2)}, u32[]{:S(2)}) collective-permute-start(bf16[64,384]{1,0:T(8,128)(2,1)S(1)} %shard_map.83.a), channel_id=1, source_target_pairs={{0,6},{1,7},{2,0},{3,1},{4,2},{5,3},{6,4},{7,5},{8,14},{9,15},{10,... | collective-permute-start | bytes 147464 | tf_op jit(solution)/shard_map/ppermute | solution.py:335
  127.1 5.3 %collective-permute-start.12 = (f32[64,320]{1,0:T(8,128)S(1)}, f32[64,320]{1,0:T(8,128)S(1)}, u32[]{:S(2)}, u32[]{:S(2)}) collective-permute-start(f32[64,320]{1,0:T(8,128)S(1)} %shard_map.86.own), channel_id=1, source_target_pairs={{0,1},{1,0},{2,3},{3,2},{4,5},{5,4},{6,7},{7,6},{8,9},{9,8},{10,11... | collective-permute-start | bytes 245768 | tf_op jit(solution)/shard_map/ppermute | solution.py:340
  132.5 4.5 %collective-permute-start.13 = (bf16[64,384]{1,0:T(8,128)(2,1)S(1)}, bf16[64,384]{1,0:T(8,128)(2,1)S(1)}, u32[]{:S(2)}, u32[]{:S(2)}) collective-permute-start(bf16[64,384]{1,0:T(8,128)(2,1)S(1)} %shard_map.87.a), channel_id=1, source_target_pairs={{0,4},{1,5},{2,6},{3,7},{4,0},{5,1},{6,2},{7,3},{8,12},{9,13},{10,... | collective-permute-start | bytes 147464 | tf_op jit(solution)/shard_map/ppermute | solution.py:335
  133.8 4.5 %collective-permute-start.14 = (bf16[64,384]{1,0:T(8,128)(2,1)S(1)}, bf16[64,384]{1,0:T(8,128)(2,1)S(1)}, u32[]{:S(2)}, u32[]{:S(2)}) collective-permute-start(bf16[64,384]{1,0:T(8,128)(2,1)S(1)} %shard_map.87.a), channel_id=1, source_target_pairs={{0,2},{1,3},{2,4},{3,5},{4,6},{5,7},{6,0},{7,1},{8,10},{9,11},{10,... | collective-permute-start | bytes 147464 | tf_op jit(solution)/shard_map/ppermute | solution.py:335
  135.5 2.9 %collective-permute-start.15 = (bf16[64,384]{1,0:T(8,128)(2,1)S(1)}, bf16[64,384]{1,0:T(8,128)(2,1)S(1)}, u32[]{:S(2)}, u32[]{:S(2)}) collective-permute-start(bf16[64,384]{1,0:T(8,128)(2,1)S(1)} %shard_map.87.a), channel_id=1, source_target_pairs={{0,6},{1,7},{2,0},{3,1},{4,2},{5,3},{6,4},{7,5},{8,14},{9,15},{10,... | collective-permute-start | bytes 147464 | tf_op jit(solution)/shard_map/ppermute | solution.py:335
  166.7 5.7 %collective-permute-start.16 = (f32[64,320]{1,0:T(8,128)S(1)}, f32[64,320]{1,0:T(8,128)S(1)}, u32[]{:S(2)}, u32[]{:S(2)}) collective-permute-start(f32[64,320]{1,0:T(8,128)S(1)} %shard_map.90.own), channel_id=1, source_target_pairs={{0,1},{1,0},{2,3},{3,2},{4,5},{5,4},{6,7},{7,6},{8,9},{9,8},{10,11... | collective-permute-start | bytes 245768 | tf_op jit(solution)/shard_map/ppermute | solution.py:340
  172.4 13.2 %collective-permute-start.17 = (bf16[64,384]{1,0:T(8,128)(2,1)S(1)}, bf16[64,384]{1,0:T(8,128)(2,1)S(1)}, u32[]{:S(2)}, u32[]{:S(2)}) collective-permute-start(bf16[64,384]{1,0:T(8,128)(2,1)S(1)} %shard_map.91.a), channel_id=1, source_target_pairs={{0,4},{1,5},{2,6},{3,7},{4,0},{5,1},{6,2},{7,3},{8,12},{9,13},{10,... | collective-permute-start | bytes 147464 | tf_op jit(solution)/shard_map/ppermute | solution.py:335
  173.6 12.0 %collective-permute-start.18 = (bf16[64,384]{1,0:T(8,128)(2,1)S(1)}, bf16[64,384]{1,0:T(8,128)(2,1)S(1)}, u32[]{:S(2)}, u32[]{:S(2)}) collective-permute-start(bf16[64,384]{1,0:T(8,128)(2,1)S(1)} %shard_map.91.a), channel_id=1, source_target_pairs={{0,2},{1,3},{2,4},{3,5},{4,6},{5,7},{6,0},{7,1},{8,10},{9,11},{10,... | collective-permute-start | bytes 147464 | tf_op jit(solution)/shard_map/ppermute | solution.py:335
  175.3 12.3 %collective-permute-start.19 = (bf16[64,384]{1,0:T(8,128)(2,1)S(1)}, bf16[64,384]{1,0:T(8,128)(2,1)S(1)}, u32[]{:S(2)}, u32[]{:S(2)}) collective-permute-start(bf16[64,384]{1,0:T(8,128)(2,1)S(1)} %shard_map.91.a), channel_id=1, source_target_pairs={{0,6},{1,7},{2,0},{3,1},{4,2},{5,3},{6,4},{7,5},{8,14},{9,15},{10,... | collective-permute-start | bytes 147464 | tf_op jit(solution)/shard_map/ppermute | solution.py:335
  215.8 40.0 %copy-start.2 = (bf16[512,1024]{1,0:T(8,128)(2,1)S(1)}, bf16[512,1024]{1,0:T(8,128)(2,1)}, u32[]{:S(2)}) copy-start(bf16[512,1024]{1,0:T(8,128)(2,1)} %prompts.1) | copy-start | bytes 3145732
  215.9 5.7 %collective-permute-start.20 = (f32[64,320]{1,0:T(8,128)S(1)}, f32[64,320]{1,0:T(8,128)S(1)}, u32[]{:S(2)}, u32[]{:S(2)}) collective-permute-start(f32[64,320]{1,0:T(8,128)S(1)} %shard_map.94.own), channel_id=1, source_target_pairs={{0,1},{1,0},{2,3},{3,2},{4,5},{5,4},{6,7},{7,6},{8,9},{9,8},{10,11... | collective-permute-start | bytes 245768 | tf_op jit(solution)/shard_map/ppermute | solution.py:340
  221.6 4.5 %collective-permute-start.21 = (bf16[64,384]{1,0:T(8,128)(2,1)S(1)}, bf16[64,384]{1,0:T(8,128)(2,1)S(1)}, u32[]{:S(2)}, u32[]{:S(2)}) collective-permute-start(bf16[64,384]{1,0:T(8,128)(2,1)S(1)} %shard_map.95.a), channel_id=1, source_target_pairs={{0,4},{1,5},{2,6},{3,7},{4,0},{5,1},{6,2},{7,3},{8,12},{9,13},{10,... | collective-permute-start | bytes 147464 | tf_op jit(solution)/shard_map/ppermute | solution.py:335
  222.1 5.0 %collective-permute-start.22 = (bf16[64,384]{1,0:T(8,128)(2,1)S(1)}, bf16[64,384]{1,0:T(8,128)(2,1)S(1)}, u32[]{:S(2)}, u32[]{:S(2)}) collective-permute-start(bf16[64,384]{1,0:T(8,128)(2,1)S(1)} %shard_map.95.a), channel_id=1, source_target_pairs={{0,2},{1,3},{2,4},{3,5},{4,6},{5,7},{6,0},{7,1},{8,10},{9,11},{10,... | collective-permute-start | bytes 147464 | tf_op jit(solution)/shard_map/ppermute | solution.py:335
  224.5 3.2 %collective-permute-start.23 = (bf16[64,384]{1,0:T(8,128)(2,1)S(1)}, bf16[64,384]{1,0:T(8,128)(2,1)S(1)}, u32[]{:S(2)}, u32[]{:S(2)}) collective-permute-start(bf16[64,384]{1,0:T(8,128)(2,1)S(1)} %shard_map.95.a), channel_id=1, source_target_pairs={{0,6},{1,7},{2,0},{3,1},{4,2},{5,3},{6,4},{7,5},{8,14},{9,15},{10,... | collective-permute-start | bytes 147464 | tf_op jit(solution)/shard_map/ppermute | solution.py:335
  271.8 6.8 %collective-permute-start.24 = (f32[64,704]{1,0:T(8,128)S(1)}, f32[64,704]{1,0:T(8,128)S(1)}, u32[]{:S(2)}, u32[]{:S(2)}) collective-permute-start(f32[64,704]{1,0:T(8,128)S(1)} %shard_map.99.own), channel_id=1, source_target_pairs={{0,1},{1,0},{2,3},{3,2},{4,5},{5,4},{6,7},{7,6},{8,9},{9,8},{10,11... | collective-permute-start | bytes 540680 | tf_op jit(solution)/shard_map/ppermute | solution.py:340
  278.7 5.5 %collective-permute-start.25 = (bf16[64,768]{1,0:T(8,128)(2,1)S(1)}, bf16[64,768]{1,0:T(8,128)(2,1)S(1)}, u32[]{:S(2)}, u32[]{:S(2)}) collective-permute-start(bf16[64,768]{1,0:T(8,128)(2,1)S(1)} %shard_map.100.a), channel_id=1, source_target_pairs={{0,4},{1,5},{2,6},{3,7},{4,0},{5,1},{6,2},{7,3},{8,12},{9,13},{10,... | collective-permute-start | bytes 294920 | tf_op jit(solution)/shard_map/ppermute | solution.py:335
  279.3 7.8 %collective-permute-start.26 = (bf16[64,768]{1,0:T(8,128)(2,1)S(1)}, bf16[64,768]{1,0:T(8,128)(2,1)S(1)}, u32[]{:S(2)}, u32[]{:S(2)}) collective-permute-start(bf16[64,768]{1,0:T(8,128)(2,1)S(1)} %shard_map.100.a), channel_id=1, source_target_pairs={{0,2},{1,3},{2,4},{3,5},{4,6},{5,7},{6,0},{7,1},{8,10},{9,11},{10,... | collective-permute-start | bytes 294920 | tf_op jit(solution)/shard_map/ppermute | solution.py:335
  280.9 6.2 %collective-permute-start.27 = (bf16[64,768]{1,0:T(8,128)(2,1)S(1)}, bf16[64,768]{1,0:T(8,128)(2,1)S(1)}, u32[]{:S(2)}, u32[]{:S(2)}) collective-permute-start(bf16[64,768]{1,0:T(8,128)(2,1)S(1)} %shard_map.100.a), channel_id=1, source_target_pairs={{0,6},{1,7},{2,0},{3,1},{4,2},{5,3},{6,4},{7,5},{8,14},{9,15},{10,... | collective-permute-start | bytes 294920 | tf_op jit(solution)/shard_map/ppermute | solution.py:335
